TPU v7x, 32 devices: a whole 2x2x4 slice. The times are simulated.
32 devices in a mesh: row: 4 (over z), col: 8 (over y, x, core).
Axes of the slice: x: 2, y: 2, z: 4, core: 2. Of those that a mesh axis runs over, the one named last changes fastest.
Arguments:
- matrix: float32 [2048, 2048], P('row', 'col'), may hold values from -40 to 40, as said below
Outputs:
- updated: float32 [2048, 2048], P('row', 'col')
- reflectors: float32 [8, 2048], P(None, 'row')
- images: float32 [8, 2048], P(None, 'row')
- subdiag: float32 [8], replicated
Inputs may be any that keep to these rules, and one draw needn't show every extreme that they name: matrix holds a symmetric matrix of order 2048 in the stored order of the first step.
All inputs are finite; a program needn't handle non-finite values.
Results may differ from a plain program's by a relative error of at most 0.0075.
Values sent between devices are 32-bit elements; how exact they have to be, the bound alone decides.
No kernel may reach another device: no remote copies, remote signals or barrier semaphores. Data moves between devices by JAX's collectives and lax.ppermute only.
A program may use at most 64 MiB of HBM per device.

v0:
```python
import jax
import jax.numpy as jnp
from jax import lax
from jax.sharding import PartitionSpec as P

TILE = 128
PANEL = 8


def from_root(value, axis, source):
    kept = jnp.where(lax.axis_index(axis) == source, value, 0).astype(value.dtype)
    return lax.psum(kept, axis)


def pick_tiles(received, tile_phase, col_ratio):
    width = received.shape[-1]
    leading_shape = received.shape[:-1]
    shaped = received.reshape(leading_shape + (width // (TILE * col_ratio), col_ratio, TILE))
    picked = lax.dynamic_index_in_dim(
        shaped, tile_phase, axis=len(leading_shape) + 1, keepdims=False
    )
    return picked.reshape(leading_shape + (width // col_ratio,))


def per_device(matrix):
    highest = lax.Precision.HIGHEST
    local_rows, local_cols = matrix.shape
    row_count = lax.axis_size("row")
    col_count = lax.axis_size("col")
    grid_row = lax.axis_index("row")
    grid_col = lax.axis_index("col")
    col_ratio = col_count // row_count
    owner_row = grid_col % row_count
    tile_phase = grid_col // row_count
    heads = PANEL + 1
    local_index = jnp.arange(local_rows, dtype=jnp.int32)
    global_row = (local_index // TILE * row_count + grid_row) * TILE + local_index % TILE
    head_index = jnp.arange(heads, dtype=jnp.int32)
    panel = from_root(jnp.transpose(matrix[:, :PANEL]), "col", 0)
    refl_rows = jnp.zeros((PANEL, local_rows), jnp.float32)
    image_rows = jnp.zeros((PANEL, local_rows), jnp.float32)
    refl_cols = jnp.zeros((PANEL, local_cols), jnp.float32)
    head_refl = jnp.zeros((PANEL, heads), jnp.float32)
    head_image = jnp.zeros((PANEL, heads), jnp.float32)
    subdiag_list = []
    for panel_col in range(PANEL):
        column = (
            panel[panel_col]
            - jnp.dot(head_image[:, panel_col], refl_rows, precision=highest)
            - jnp.dot(head_refl[:, panel_col], image_rows, precision=highest)
        )
        tail_mask = global_row > panel_col + 1
        first_mask = global_row == panel_col + 1
        tail_vals = jnp.where(tail_mask, column, 0.0)
        squares = jnp.sum(tail_vals * tail_vals)
        leading = jnp.sum(jnp.where(first_mask, column, 0.0))
        head_column = jnp.where(grid_row == 0, column[:heads], 0.0)
        squares, leading, head_column = lax.psum((squares, leading, head_column), "row")
        radius = jnp.sqrt(leading * leading + squares)
        denominator = leading + radius
        scaling = denominator / radius
        reflector = jnp.where(tail_mask, column / denominator, jnp.where(first_mask, 1.0, 0.0))
        head_vector = jnp.where(
            head_index > panel_col + 1,
            head_column / denominator,
            jnp.where(head_index == panel_col + 1, 1.0, 0.0),
        )
        refl_proj, image_proj = lax.psum(
            (
                jnp.dot(refl_rows, reflector, precision=highest),
                jnp.dot(image_rows, reflector, precision=highest),
            ),
            "row",
        )
        gathered = lax.all_gather(reflector, "row", axis=0, tiled=True)
        received = lax.dynamic_slice_in_dim(gathered, owner_row * local_rows, local_rows, 0)
        reflector_cols = pick_tiles(received, tile_phase, col_ratio)
        product = lax.psum(jnp.dot(matrix, reflector_cols, precision=highest), "col")
        correction = jnp.dot(image_proj, refl_rows, precision=highest) + jnp.dot(
            refl_proj, image_rows, precision=highest
        )
        image = scaling * (product - correction)
        head_product = jnp.where(grid_row == 0, product[:heads], 0.0)
        inner_product, head_product = lax.psum((jnp.sum(image * reflector), head_product), "row")
        adjust = -0.5 * scaling * inner_product
        image = image + adjust * reflector
        head_vals = (
            scaling
            * (
                head_product
                - jnp.dot(image_proj, head_refl, precision=highest)
                - jnp.dot(refl_proj, head_image, precision=highest)
            )
            + adjust * head_vector
        )
        refl_rows = refl_rows.at[panel_col].set(reflector)
        image_rows = image_rows.at[panel_col].set(image)
        refl_cols = refl_cols.at[panel_col].set(reflector_cols)
        head_refl = head_refl.at[panel_col].set(head_vector)
        head_image = head_image.at[panel_col].set(head_vals)
        subdiag_list.append(-radius)
    gathered_images = lax.all_gather(image_rows, "row", axis=1, tiled=True)
    received_images = lax.dynamic_slice_in_dim(
        gathered_images, owner_row * local_rows, local_rows, 1
    )
    image_cols = pick_tiles(received_images, tile_phase, col_ratio)
    updated = (
        matrix
        - jnp.dot(jnp.transpose(refl_rows), image_cols, precision=highest)
        - jnp.dot(jnp.transpose(image_rows), refl_cols, precision=highest)
    )
    return (updated, refl_rows, image_rows, jnp.stack(subdiag_list))


def solution(mesh):
    placed = (P("row", "col"),)
    return jax.shard_map(
        per_device,
        mesh=mesh,
        in_specs=placed,
        out_specs=(P("row", "col"), P(None, "row"), P(None, "row"), P()),
        check_vma=False,
    )
```

profile of v0, /device:TPU:0, one launch (start us, length us, event | category | flops | bytes accessed | tf_op | source)
XLA Modules:
  0.0 522.4 jit_solution(2466424269105696383)
XLA Ops:
  0.8 1.0 select_bitcast_fusion
  1.8 28.4 %psum.437 = f32[8,512]{0,1:T(8,128)S(1)} all-reduce(f32[8,512]{0,1:T(8,128)S(1)} %select_bitcast_fusion), channel_id=1, replica_groups=mesh['row'=4,'col'=8] {'col'}, use_global_device_ids=true, to_apply=%region_0.1 | all-reduce | flops 4096 | bytes 32768 | tf_op jit(solution)/shard_map/psum | solution.py:12
  30.2 1.1 slice_reduce_fusion
  31.9 12.6 %all-reduce.26 = (f32[]{:T(128)}, f32[]{:T(128)}) all-reduce(f32[]{:T(128)} %get-tuple-element.483, f32[]{:T(128)} %get-tuple-element.482), channel_id=1, replica_groups=mesh['row'=4,'col'=8] {'row'}, use_global_device_ids=true, to_apply=%region_2.3 | all-reduce | flops 2 | bytes 16 | tf_op jit(solution)/shard_map/psum | solution.py:58
  47.3 8.4 %psum.442 = f32[8]{0:T(128)S(1)} all-reduce(f32[8]{0:T(128)S(1)} %convolution_bitcast_fusion.14), channel_id=1, replica_groups=mesh['row'=4,'col'=8] {'row'}, use_global_device_ids=true, to_apply=%region_7.8 | all-reduce | flops 8 | bytes 64 | tf_op jit(solution)/shard_map/psum | solution.py:68
  55.8 11.9 %all-gather = f32[4,1,512]{2,1,0:T(1,128)S(1)} all-gather(f32[1,1,512]{2,1,0:T(1,128)S(1)} %bitcast.539), channel_id=1, replica_groups=mesh['row'=4,'col'=8] {'row'}, dimensions={0}, use_global_device_ids=true | all-gather | bytes 10240 | tf_op jit(solution)/shard_map/all_gather | solution.py:75
  68.3 11.8 %psum.440 = f32[512]{0:T(512)S(1)} all-reduce(f32[512]{0:T(512)S(1)} %bitcast.556), channel_id=1, replica_groups=mesh['row'=4,'col'=8] {'col'}, use_global_device_ids=true, to_apply=%region_5.6 | all-reduce | flops 512 | bytes 4096 | tf_op jit(solution)/shard_map/psum | solution.py:78
  80.7 10.0 %all-reduce.25 = (f32[]{:T(128)}, f32[9]{0:T(128)S(1)}, f32[9]{0:T(128)S(1)}) all-reduce(f32[]{:T(128)} %multiply_reduce_fusion.14, f32[9]{0:T(128)S(1)} %broadcast_select_fusion.12, f32[9]{0:T(128)S(1)} %broadcast_select_fusion.13), channel_id=1, replica_groups=mesh['row'=4,'col'=8] {'row'}, use_global_device_ids=true, to_apply=%region_9.10 | all-reduce | flops 19 | bytes 152 | tf_op jit(solution)/shard_map/psum | solution.py:84
  92.8 9.9 %all-reduce.24 = (f32[]{:T(128)}, f32[]{:T(128)}) all-reduce(f32[]{:T(128)} %get-tuple-element.481, f32[]{:T(128)} %get-tuple-element.480), channel_id=1, replica_groups=mesh['row'=4,'col'=8] {'row'}, use_global_device_ids=true, to_apply=%region_12.13 | all-reduce | flops 2 | bytes 16 | tf_op jit(solution)/shard_map/psum | solution.py:58
  105.7 9.4 %all-reduce.23 = (f32[8]{0:T(128)S(1)}, f32[8]{0:T(128)S(1)}) all-reduce(f32[8]{0:T(128)S(1)} %convolution_bitcast_fusion.13, f32[8]{0:T(128)S(1)} %convolution_bitcast_fusion.12), channel_id=1, replica_groups=mesh['row'=4,'col'=8] {'row'}, use_global_device_ids=true, to_apply=%region_17.18 | all-reduce | flops 16 | bytes 128 | tf_op jit(solution)/shard_map/psum | solution.py:68
  115.6 11.9 %all-gather.1 = f32[4,1,512]{2,1,0:T(1,128)S(1)} all-gather(f32[1,1,512]{2,1,0:T(1,128)S(1)} %bitcast.546), channel_id=1, replica_groups=mesh['row'=4,'col'=8] {'row'}, dimensions={0}, use_global_device_ids=true | all-gather | bytes 10240 | tf_op jit(solution)/shard_map/all_gather | solution.py:75
  128.1 11.8 %psum.447 = f32[512]{0:T(512)S(1)} all-reduce(f32[512]{0:T(512)S(1)} %bitcast.557), channel_id=1, replica_groups=mesh['row'=4,'col'=8] {'col'}, use_global_device_ids=true, to_apply=%region_15.16 | all-reduce | flops 512 | bytes 4096 | tf_op jit(solution)/shard_map/psum | solution.py:78
  140.5 9.0 %all-reduce.22 = (f32[]{:T(128)}, f32[9]{0:T(128)S(1)}, f32[9]{0:T(128)S(1)}) all-reduce(f32[]{:T(128)} %get-tuple-element.553, f32[9]{0:T(128)S(1)} %broadcast_select_fusion.10, f32[9]{0:T(128)S(1)} %broadcast_select_fusion.11), channel_id=1, replica_groups=mesh['row'=4,'col'=8] {'row'}, use_global_device_ids=true, to_apply=%region_20.21 | all-reduce | flops 19 | bytes 152 | tf_op jit(solution)/shard_map/psum | solution.py:84
  151.8 11.0 %all-reduce.21 = (f32[]{:T(128)}, f32[]{:T(128)}) all-reduce(f32[]{:T(128)} %get-tuple-element.479, f32[]{:T(128)} %get-tuple-element.478), channel_id=1, replica_groups=mesh['row'=4,'col'=8] {'row'}, use_global_device_ids=true, to_apply=%region_23.24 | all-reduce | flops 2 | bytes 16 | tf_op jit(solution)/shard_map/psum | solution.py:58
  165.7 8.4 %all-reduce.20 = (f32[8]{0:T(128)S(1)}, f32[8]{0:T(128)S(1)}) all-reduce(f32[8]{0:T(128)S(1)} %convolution_bitcast_fusion.11, f32[8]{0:T(128)S(1)} %convolution_bitcast_fusion.10), channel_id=1, replica_groups=mesh['row'=4,'col'=8] {'row'}, use_global_device_ids=true, to_apply=%region_28.29 | all-reduce | flops 16 | bytes 128 | tf_op jit(solution)/shard_map/psum | solution.py:68
  174.5 11.9 %all-gather.2 = f32[4,1,512]{2,1,0:T(1,128)S(1)} all-gather(f32[1,1,512]{2,1,0:T(1,128)S(1)} %bitcast.516), channel_id=1, replica_groups=mesh['row'=4,'col'=8] {'row'}, dimensions={0}, use_global_device_ids=true | all-gather | bytes 10240 | tf_op jit(solution)/shard_map/all_gather | solution.py:75
  187.0 11.8 %psum.455 = f32[512]{0:T(512)S(1)} all-reduce(f32[512]{0:T(512)S(1)} %bitcast.558), channel_id=1, replica_groups=mesh['row'=4,'col'=8] {'col'}, use_global_device_ids=true, to_apply=%region_26.27 | all-reduce | flops 512 | bytes 4096 | tf_op jit(solution)/shard_map/psum | solution.py:78
  199.4 10.0 %all-reduce.19 = (f32[]{:T(128)}, f32[9]{0:T(128)S(1)}, f32[9]{0:T(128)S(1)}) all-reduce(f32[]{:T(128)} %get-tuple-element.550, f32[9]{0:T(128)S(1)} %broadcast_select_fusion.8, f32[9]{0:T(128)S(1)} %broadcast_select_fusion.9), channel_id=1, replica_groups=mesh['row'=4,'col'=8] {'row'}, use_global_device_ids=true, to_apply=%region_31.32 | all-reduce | flops 19 | bytes 152 | tf_op jit(solution)/shard_map/psum | solution.py:84
  211.7 9.9 %all-reduce.18 = (f32[]{:T(128)}, f32[]{:T(128)}) all-reduce(f32[]{:T(128)} %get-tuple-element.477, f32[]{:T(128)} %get-tuple-element.476), channel_id=1, replica_groups=mesh['row'=4,'col'=8] {'row'}, use_global_device_ids=true, to_apply=%region_34.35 | all-reduce | flops 2 | bytes 16 | tf_op jit(solution)/shard_map/psum | solution.py:58
  224.6 9.4 %all-reduce.17 = (f32[8]{0:T(128)S(1)}, f32[8]{0:T(128)S(1)}) all-reduce(f32[8]{0:T(128)S(1)} %convolution_bitcast_fusion.9, f32[8]{0:T(128)S(1)} %convolution_bitcast_fusion.8), channel_id=1, replica_groups=mesh['row'=4,'col'=8] {'row'}, use_global_device_ids=true, to_apply=%region_39.40 | all-reduce | flops 16 | bytes 128 | tf_op jit(solution)/shard_map/psum | solution.py:68
  234.5 11.9 %all-gather.3 = f32[4,1,512]{2,1,0:T(1,128)S(1)} all-gather(f32[1,1,512]{2,1,0:T(1,128)S(1)} %bitcast.520), channel_id=1, replica_groups=mesh['row'=4,'col'=8] {'row'}, dimensions={0}, use_global_device_ids=true | all-gather | bytes 10240 | tf_op jit(solution)/shard_map/all_gather | solution.py:75
  247.0 11.8 %psum.463 = f32[512]{0:T(512)S(1)} all-reduce(f32[512]{0:T(512)S(1)} %bitcast.559), channel_id=1, replica_groups=mesh['row'=4,'col'=8] {'col'}, use_global_device_ids=true, to_apply=%region_37.38 | all-reduce | flops 512 | bytes 4096 | tf_op jit(solution)/shard_map/psum | solution.py:78
  259.4 9.0 %all-reduce.16 = (f32[]{:T(128)}, f32[9]{0:T(128)S(1)}, f32[9]{0:T(128)S(1)}) all-reduce(f32[]{:T(128)} %get-tuple-element.547, f32[9]{0:T(128)S(1)} %broadcast_select_fusion.6, f32[9]{0:T(128)S(1)} %broadcast_select_fusion.7), channel_id=1, replica_groups=mesh['row'=4,'col'=8] {'row'}, use_global_device_ids=true, to_apply=%region_42.43 | all-reduce | flops 19 | bytes 152 | tf_op jit(solution)/shard_map/psum | solution.py:84
  269.9 0.6 multiply_reduce_fusion.7
  270.6 11.0 %all-reduce.15 = (f32[]{:T(128)}, f32[]{:T(128)}) all-reduce(f32[]{:T(128)} %get-tuple-element.475, f32[]{:T(128)} %get-tuple-element.474), channel_id=1, replica_groups=mesh['row'=4,'col'=8] {'row'}, use_global_device_ids=true, to_apply=%region_45.46 | all-reduce | flops 2 | bytes 16 | tf_op jit(solution)/shard_map/psum | solution.py:58
  284.5 8.4 %all-reduce.14 = (f32[8]{0:T(128)S(1)}, f32[8]{0:T(128)S(1)}) all-reduce(f32[8]{0:T(128)S(1)} %convolution_bitcast_fusion.7, f32[8]{0:T(128)S(1)} %convolution_bitcast_fusion.6), channel_id=1, replica_groups=mesh['row'=4,'col'=8] {'row'}, use_global_device_ids=true, to_apply=%region_50.51 | all-reduce | flops 16 | bytes 128 | tf_op jit(solution)/shard_map/psum | solution.py:68
  293.4 11.9 %all-gather.4 = f32[4,1,512]{2,1,0:T(1,128)S(1)} all-gather(f32[1,1,512]{2,1,0:T(1,128)S(1)} %bitcast.524), channel_id=1, replica_groups=mesh['row'=4,'col'=8] {'row'}, dimensions={0}, use_global_device_ids=true | all-gather | bytes 10240 | tf_op jit(solution)/shard_map/all_gather | solution.py:75
  305.9 11.8 %psum.471 = f32[512]{0:T(512)S(1)} all-reduce(f32[512]{0:T(512)S(1)} %bitcast.560), channel_id=1, replica_groups=mesh['row'=4,'col'=8] {'col'}, use_global_device_ids=true, to_apply=%region_48.49 | all-reduce | flops 512 | bytes 4096 | tf_op jit(solution)/shard_map/psum | solution.py:78
  318.3 10.0 %all-reduce.13 = (f32[]{:T(128)}, f32[9]{0:T(128)S(1)}, f32[9]{0:T(128)S(1)}) all-reduce(f32[]{:T(128)} %get-tuple-element.544, f32[9]{0:T(128)S(1)} %broadcast_select_fusion.4, f32[9]{0:T(128)S(1)} %broadcast_select_fusion.5), channel_id=1, replica_groups=mesh['row'=4,'col'=8] {'row'}, use_global_device_ids=true, to_apply=%region_53.54 | all-reduce | flops 19 | bytes 152 | tf_op jit(solution)/shard_map/psum | solution.py:84
  330.5 9.9 %all-reduce.12 = (f32[]{:T(128)}, f32[]{:T(128)}) all-reduce(f32[]{:T(128)} %get-tuple-element.473, f32[]{:T(128)} %get-tuple-element.472), channel_id=1, replica_groups=mesh['row'=4,'col'=8] {'row'}, use_global_device_ids=true, to_apply=%region_56.57 | all-reduce | flops 2 | bytes 16 | tf_op jit(solution)/shard_map/psum | solution.py:58
  343.4 9.4 %all-reduce.11 = (f32[8]{0:T(128)S(1)}, f32[8]{0:T(128)S(1)}) all-reduce(f32[8]{0:T(128)S(1)} %convolution_bitcast_fusion.5, f32[8]{0:T(128)S(1)} %convolution_bitcast_fusion.4), channel_id=1, replica_groups=mesh['row'=4,'col'=8] {'row'}, use_global_device_ids=true, to_apply=%region_61.62 | all-reduce | flops 16 | bytes 128 | tf_op jit(solution)/shard_map/psum | solution.py:68
  353.3 11.9 %all-gather.5 = f32[4,1,512]{2,1,0:T(1,128)S(1)} all-gather(f32[1,1,512]{2,1,0:T(1,128)S(1)} %bitcast.528), channel_id=1, replica_groups=mesh['row'=4,'col'=8] {'row'}, dimensions={0}, use_global_device_ids=true | all-gather | bytes 10240 | tf_op jit(solution)/shard_map/all_gather | solution.py:75
  365.8 11.8 %psum.479 = f32[512]{0:T(512)S(1)} all-reduce(f32[512]{0:T(512)S(1)} %bitcast.561), channel_id=1, replica_groups=mesh['row'=4,'col'=8] {'col'}, use_global_device_ids=true, to_apply=%region_59.60 | all-reduce | flops 512 | bytes 4096 | tf_op jit(solution)/shard_map/psum | solution.py:78
  378.2 9.0 %all-reduce.10 = (f32[]{:T(128)}, f32[9]{0:T(128)S(1)}, f32[9]{0:T(128)S(1)}) all-reduce(f32[]{:T(128)} %get-tuple-element.541, f32[9]{0:T(128)S(1)} %broadcast_select_fusion.2, f32[9]{0:T(128)S(1)} %broadcast_select_fusion.3), channel_id=1, replica_groups=mesh['row'=4,'col'=8] {'row'}, use_global_device_ids=true, to_apply=%region_64.65 | all-reduce | flops 19 | bytes 152 | tf_op jit(solution)/shard_map/psum | solution.py:84
  389.4 11.0 %all-reduce.9 = (f32[]{:T(128)}, f32[]{:T(128)}) all-reduce(f32[]{:T(128)} %get-tuple-element.471, f32[]{:T(128)} %get-tuple-element.470), channel_id=1, replica_groups=mesh['row'=4,'col'=8] {'row'}, use_global_device_ids=true, to_apply=%region_67.68 | all-reduce | flops 2 | bytes 16 | tf_op jit(solution)/shard_map/psum | solution.py:58
  403.4 8.4 %all-reduce.8 = (f32[8]{0:T(128)S(1)}, f32[8]{0:T(128)S(1)}) all-reduce(f32[8]{0:T(128)S(1)} %convolution_bitcast_fusion.3, f32[8]{0:T(128)S(1)} %convolution_bitcast_fusion.2), channel_id=1, replica_groups=mesh['row'=4,'col'=8] {'row'}, use_global_device_ids=true, to_apply=%region_72.73 | all-reduce | flops 16 | bytes 128 | tf_op jit(solution)/shard_map/psum | solution.py:68
  412.2 11.9 %all-gather.6 = f32[4,1,512]{2,1,0:T(1,128)S(1)} all-gather(f32[1,1,512]{2,1,0:T(1,128)S(1)} %bitcast.532), channel_id=1, replica_groups=mesh['row'=4,'col'=8] {'row'}, dimensions={0}, use_global_device_ids=true | all-gather | bytes 10240 | tf_op jit(solution)/shard_map/all_gather | solution.py:75
  424.7 11.8 %psum.487 = f32[512]{0:T(512)S(1)} all-reduce(f32[512]{0:T(512)S(1)} %bitcast.562), channel_id=1, replica_groups=mesh['row'=4,'col'=8] {'col'}, use_global_device_ids=true, to_apply=%region_70.71 | all-reduce | flops 512 | bytes 4096 | tf_op jit(solution)/shard_map/psum | solution.py:78
  437.1 10.0 %all-reduce.7 = (f32[]{:T(128)}, f32[9]{0:T(128)S(1)}, f32[9]{0:T(128)S(1)}) all-reduce(f32[]{:T(128)} %get-tuple-element.538, f32[9]{0:T(128)S(1)} %broadcast_select_fusion, f32[9]{0:T(128)S(1)} %broadcast_select_fusion.1), channel_id=1, replica_groups=mesh['row'=4,'col'=8] {'row'}, use_global_device_ids=true, to_apply=%region_75.76 | all-reduce | flops 19 | bytes 152 | tf_op jit(solution)/shard_map/psum | solution.py:84
  448.7 0.6 multiply_reduce_fusion.1
  449.3 9.9 %all-reduce.6 = (f32[]{:T(128)}, f32[]{:T(128)}) all-reduce(f32[]{:T(128)} %get-tuple-element.469, f32[]{:T(128)} %get-tuple-element.468), channel_id=1, replica_groups=mesh['row'=4,'col'=8] {'row'}, use_global_device_ids=true, to_apply=%region_78.79 | all-reduce | flops 2 | bytes 16 | tf_op jit(solution)/shard_map/psum | solution.py:58
  462.8 9.4 %all-reduce.5 = (f32[8]{0:T(128)S(1)}, f32[8]{0:T(128)S(1)}) all-reduce(f32[8]{0:T(128)S(1)} %convolution_bitcast_fusion.1, f32[8]{0:T(128)S(1)} %convolution_bitcast_fusion), channel_id=1, replica_groups=mesh['row'=4,'col'=8] {'row'}, use_global_device_ids=true, to_apply=%region_82.83 | all-reduce | flops 16 | bytes 128 | tf_op jit(solution)/shard_map/psum | solution.py:68
  472.6 11.9 %all-gather.7 = f32[4,1,512]{2,1,0:T(1,128)S(1)} all-gather(f32[1,1,512]{2,1,0:T(1,128)S(1)} %bitcast.536), channel_id=1, replica_groups=mesh['row'=4,'col'=8] {'row'}, dimensions={0}, use_global_device_ids=true | all-gather | bytes 10240 | tf_op jit(solution)/shard_map/all_gather | solution.py:75
  485.1 11.8 %psum.495 = f32[512]{0:T(512)S(1)} all-reduce(f32[512]{0:T(512)S(1)} %bitcast.563), channel_id=1, replica_groups=mesh['row'=4,'col'=8] {'col'}, use_global_device_ids=true, to_apply=%region_81.82 | all-reduce | flops 512 | bytes 4096 | tf_op jit(solution)/shard_map/psum | solution.py:78
  497.5 9.0 %psum.498 = f32[]{:T(128)} all-reduce(f32[]{:T(128)} %get-tuple-element.535), channel_id=1, replica_groups=mesh['row'=4,'col'=8] {'row'}, use_global_device_ids=true, to_apply=%region_85.86 | all-reduce | flops 1 | bytes 8 | tf_op jit(solution)/shard_map/psum | solution.py:84
  507.2 13.1 %all_gather.35 = f32[8,2048]{1,0:T(8,128)S(1)} all-gather(f32[8,512]{1,0:T(8,128)S(1)} %scatter.175), channel_id=1, replica_groups=mesh['row'=4,'col'=8] {'row'}, dimensions={1}, use_global_device_ids=true | all-gather | bytes 81920 | tf_op jit(solution)/shard_map/all_gather | solution.py:102
  520.3 0.6 convolution_subtract_fusion.1
  521.0 1.4 convolution_subtract_fusion
  (193 shorter events, 26.0 us)
Async XLA Ops:
  30.2 37.6 %copy-start = (f32[512,256]{1,0:T(8,128)S(1)}, f32[512,256]{1,0:T(8,128)}, u32[]{:S(2)}) copy-start(f32[512,256]{1,0:T(8,128)} %param.77) | copy-start | bytes 1572868
  472.4 47.9 %copy-start.2 = (f32[8,512]{1,0:T(8,128)}, f32[8,512]{1,0:T(8,128)S(1)}, u32[]{:S(2)}) copy-start(f32[8,512]{1,0:T(8,128)S(1)} %scatter.174) | copy-start | bytes 49156
  507.2 13.8 %copy-start.1 = (f32[8,512]{1,0:T(8,128)}, f32[8,512]{1,0:T(8,128)S(1)}, u32[]{:S(2)}) copy-start(f32[8,512]{1,0:T(8,128)S(1)} %scatter.175) | copy-start | bytes 49156
where the time goes:
time: 524 us; the launch traced here: 522 us
  blocking collectives  463 us (88%)
  between operations  27.7 us (5%)
  matrix products  14 us (3%)
  other arithmetic  11.1 us (2%)
  local copies, waits for them, and re-layouts  6.3 us (1%)
    all_gather x8, blocking collectives, per_device(): gathered = lax.all_gather(reflector, 'row', axis=0, tiled=True)  95 us
    psum x8, blocking collectives, per_device(): lax.psum(jnp.dot(matrix, reflector_cols, precision=highest), 'col')  94.4 us
    psum x8, blocking collectives, per_device(): lax.psum((squares, leading, head_column), 'row')  85.3 us
    psum x8, blocking collectives, per_device(): lax.psum((jnp.sum(image * reflector), head_product), 'row')  76 us
    psum x8, blocking collectives, per_device(): lax.psum((jnp.dot(refl_rows, reflector, precision=highest), jnp.dot(image...  71.1 us
    psum x1, blocking collectives, from_root(): return lax.psum(kept, axis)  28.4 us
    all_gather x1, blocking collectives, per_device(): gathered_images = lax.all_gather(image_rows, 'row', axis=1, tiled=True)  13.1 us

commit v1 on v0

v1 whole, which is shorter than its diff:
```python
import jax
import jax.numpy as jnp
from jax import lax
from jax.sharding import PartitionSpec as P

TILE = 128
PANEL = 8
AXES = ("row", "col")


def everywhere(value):
    row_count, col_count = lax.axis_size("row"), lax.axis_size("col")
    spread = jnp.broadcast_to(value[None], (row_count * col_count,) + value.shape)
    got = lax.all_to_all(spread, AXES, 0, 0, tiled=False)
    return got.reshape((row_count, col_count) + value.shape)


def per_device(matrix):
    highest = lax.Precision.HIGHEST
    local_rows, local_cols = matrix.shape
    row_count, col_count = lax.axis_size("row"), lax.axis_size("col")
    grid_row, grid_col = lax.axis_index("row"), lax.axis_index("col")
    row_tiles, col_tiles = local_rows // TILE, local_cols // TILE
    order = local_rows * row_count
    position = jnp.arange(order, dtype=jnp.int32)

    def my_rows(vectors):
        shaped = vectors.reshape(vectors.shape[:-1] + (row_tiles, row_count, TILE))
        picked = lax.dynamic_index_in_dim(shaped, grid_row, axis=shaped.ndim - 2, keepdims=False)
        return picked.reshape(vectors.shape[:-1] + (local_rows,))

    def my_cols(vectors):
        shaped = vectors.reshape(vectors.shape[:-1] + (col_tiles, col_count, TILE))
        picked = lax.dynamic_index_in_dim(shaped, grid_col, axis=shaped.ndim - 2, keepdims=False)
        return picked.reshape(vectors.shape[:-1] + (local_cols,))

    def global_cols(pieces):
        shaped = pieces.reshape(pieces.shape[:-1] + (col_tiles, TILE))
        return jnp.moveaxis(shaped, 0, -2).reshape(pieces.shape[1:-1] + (order,))

    panel = global_cols(everywhere(matrix[:PANEL])[0])
    refl = jnp.zeros((PANEL, order), jnp.float32)
    images = jnp.zeros((PANEL, order), jnp.float32)
    subdiag_list = []
    for j in range(PANEL):
        column = panel[j]
        for k in range(j):
            column = column - images[k, j] * refl[k] - refl[k, j] * images[k]
        leading = column[j + 1]
        tail = jnp.where(position > j + 1, column, 0.0)
        radius = jnp.sqrt(leading * leading + jnp.sum(tail * tail))
        denominator = leading + radius
        scaling = denominator / radius
        reflector = jnp.where(position == j + 1, 1.0, tail / denominator)
        partial = jnp.sum(matrix * my_rows(reflector)[:, None], axis=0)
        product = global_cols(jnp.sum(everywhere(partial), axis=0))
        refl_proj = jnp.sum(refl * reflector, axis=1)
        image_proj = jnp.sum(images * reflector, axis=1)
        image = product
        for k in range(j):
            image = image - image_proj[k] * refl[k] - refl_proj[k] * images[k]
        image = scaling * image
        image = image - (0.5 * scaling * jnp.sum(image * reflector)) * reflector
        refl = refl.at[j].set(reflector)
        images = images.at[j].set(image)
        subdiag_list.append(-radius)
    refl_rows, image_rows = my_rows(refl), my_rows(images)
    updated = (
        matrix
        - jnp.dot(jnp.transpose(refl_rows), my_cols(images), precision=highest)
        - jnp.dot(jnp.transpose(image_rows), my_cols(refl), precision=highest)
    )
    return (updated, refl_rows, image_rows, jnp.stack(subdiag_list))


def solution(mesh):
    return jax.shard_map(
        per_device,
        mesh=mesh,
        in_specs=(P("row", "col"),),
        out_specs=(P("row", "col"), P(None, "row"), P(None, "row"), P()),
        check_vma=False,
    )
```

time: 524 us -> 295 us (0.56)
  blocking collectives: 463 us -> 0 us
  other arithmetic: 11.1 us -> 139 us
  waiting for transfers between devices: 0 us -> 40.5 us
  local copies, waits for them, and re-layouts: 6.3 us -> 43.2 us
  starting transfers between devices: 0 us -> 33 us
  matrix products: 14 us -> 2.1 us
  between operations: 27.7 us -> 33.7 us
    psum x33 -> x0, blocking collectives: 355 us -> none  [the longest x8 94.4 us: per_device(): lax.psum(jnp.dot(matrix, reflector_cols, precision=highest), 'col')]
    all_gather x9 -> x0, blocking collectives: 108 us -> none  [the longest x8 95 us: per_device(): gathered = lax.all_gather(reflector, 'row', axis=0, tiled=True)]
    mul x0 -> x27, other arithmetic: none -> 55.1 us  [the longest x13 27.2 us: per_device(): image = image - image_proj[k] * refl[k] - refl_proj[k] * images[k]]
    all_to_all x0 -> x9, waiting for transfers between devices: none -> 40.5 us  [everywhere(): got = lax.all_to_all(spread, AXES, 0, 0, tiled=False)]
    all_to_all x0 -> x9, starting transfers between devices: none -> 33 us  [everywhere(): got = lax.all_to_all(spread, AXES, 0, 0, tiled=False)]
    slice x15 -> x57, local copies, waits for them, and re-layouts: 3.69 us -> 34.1 us  [the longest x26 16.3 us: per_device(): column = column - images[k, j] * refl[k] - refl[k, j] * images[k]]
    reduce_sum x16 -> x38, other arithmetic: 9.88 us -> 37 us  [the longest x8 21.5 us: per_device(): image = image - 0.5 * scaling * jnp.sum(image * reflector) * reflector]
    select_n x23 -> x16, other arithmetic: 1.11 us -> 26 us  [the longest x15 23.4 us: per_device(): reflector = jnp.where(position == j + 1, 1.0, tail / denominator)]
  transfers between devices with their start and end apart: 0 -> 9, of which waited for: 0 -> 7; matrix products, arithmetic and copies ran while one was open for 0% -> 10% of each run, Pallas kernels for 0% -> 0%
where the time goes in v1:
time: 295 us; the launch traced here: 292 us
  other arithmetic  139 us (47%)
  local copies, waits for them, and re-layouts  43.2 us (15%)
  waiting for transfers between devices  40.5 us (14%)
  between operations  33.7 us (11%)
  starting transfers between devices  33 us (11%)
    all_to_all x9, waiting for transfers between devices, everywhere(): got = lax.all_to_all(spread, AXES, 0, 0, tiled=False)  40.5 us
    all_to_all x9, starting transfers between devices, everywhere(): got = lax.all_to_all(spread, AXES, 0, 0, tiled=False)  33 us
    mul x13, other arithmetic, per_device(): image = image - image_proj[k] * refl[k] - refl_proj[k] * images[k]  27.2 us
    mul x12, other arithmetic, per_device(): column = column - images[k, j] * refl[k] - refl[k, j] * images[k]  26.6 us
    select_n x15, other arithmetic, per_device(): reflector = jnp.where(position == j + 1, 1.0, tail / denominator)  23.4 us
    reduce_sum x8, other arithmetic, per_device(): image = image - 0.5 * scaling * jnp.sum(image * reflector) * reflector  21.5 us
    slice x26, local copies, waits for them, and re-layouts, per_device(): column = column - images[k, j] * refl[k] - refl[k, j] * images[k]  16.3 us
    reduce_sum x7, other arithmetic, per_device(): radius = jnp.sqrt(leading * leading + jnp.sum(tail * tail))  13.2 us
  transfers between devices with their start and end apart: 9, of which 7 were waited for; matrix products, arithmetic and copies ran while one was open for 10% of the time, Pallas kernels for 0%

profile of v1, /device:TPU:0, one launch (start us, length us, event | category | flops | bytes accessed | tf_op | source)
XLA Modules:
  0.0 291.9 jit_solution(9193076057417803723)
XLA Ops:
  2.1 7.3 %all-to-all-start = ((f32[32,8,256]{2,1,0:T(8,128)}), f32[32,8,256]{2,1,0:T(8,128)S(1)}, u32[]{:S(2)}, u32[]{:S(2)}) async-start(f32[32,8,256]{2,1,0:T(8,128)} %broadcast_in_dim.107), calls=%async_computation | async-start | bytes 524288 | tf_op jit(solution)/shard_map/all_to_all | solution.py:14
  9.4 10.6 %all-to-all-done = f32[32,8,256]{2,1,0:T(8,128)S(1)} async-done(((f32[32,8,256]{2,1,0:T(8,128)}), f32[32,8,256]{2,1,0:T(8,128)S(1)}, u32[]{:S(2)}, u32[]{:S(2)}) %all-to-all-start) | async-done | bytes 262176 | tf_op jit(solution)/shard_map/all_to_all | solution.py:14
  24.6 2.6 all-to-all-start.1
  27.3 7.2 %all-to-all-done.1 = f32[32,1,256]{2,1,0:T(1,128)S(1)} async-done(((f32[32,1,256]{2,1,0:T(1,128)}), f32[32,1,256]{2,1,0:T(1,128)S(1)}, u32[]{:S(2)}, u32[]{:S(2)}) %all-to-all-start.1) | async-done | bytes 32800 | tf_op jit(solution)/shard_map/all_to_all | solution.py:14
  45.5 2.6 all-to-all-start.2
  48.3 7.0 %all-to-all-done.2 = f32[32,1,256]{2,1,0:T(1,128)S(1)} async-done(((f32[32,1,256]{2,1,0:T(1,128)}), f32[32,1,256]{2,1,0:T(1,128)S(1)}, u32[]{:S(2)}, u32[]{:S(2)}) %all-to-all-start.2) | async-done | bytes 32800 | tf_op jit(solution)/shard_map/all_to_all | solution.py:14
  69.7 2.6 compare_select_fusion.11
  76.4 2.6 all-to-all-start.3
  80.3 6.0 %all-to-all-done.3 = f32[32,1,256]{2,1,0:T(1,128)S(1)} async-done(((f32[32,1,256]{2,1,0:T(1,128)}), f32[32,1,256]{2,1,0:T(1,128)S(1)}, u32[]{:S(2)}, u32[]{:S(2)}) %all-to-all-start.3) | async-done | bytes 32800 | tf_op jit(solution)/shard_map/all_to_all | solution.py:14
  86.2 3.1 %multiply_reduce_fusion.26 = (f32[]{:T(128)}, f32[2,8,128]{2,1,0:T(8,128)S(1)}, f32[2,8,128]{2,1,0:T(8,128)S(1)}) fusion(f32[]{:T(128)S(6)} %add.919, f32[2,8,128]{2,1,0:T(8,128)S(1)} %get-tuple-element.246, f32[2,8,128]{2,1,0:T(8,128)S(1)} %get-tuple-element.245, f32[]{:T(128)S(6)} %mul.5954, f32[]{:T(128)} %bitcast.33, f32[]{:T(128)} %bitcast.32, ...), kind=kLoop, calls=%fused_computation.376 | loop fusion | flops 53247 | bytes 81952 | tf_op jit(solution)/shard_map/reduce_sum | solution.py:63
  90.0 2.5 multiply_subtract_fusion.14
  97.3 2.4 fusion.207
  107.9 2.4 divide_select_fusion.3
  111.2 2.6 all-to-all-start.4
  117.2 3.8 %all-to-all-done.4 = f32[32,1,256]{2,1,0:T(1,128)S(1)} async-done(((f32[32,1,256]{2,1,0:T(1,128)}), f32[32,1,256]{2,1,0:T(1,128)S(1)}, u32[]{:S(2)}, u32[]{:S(2)}) %all-to-all-start.4) | async-done | bytes 32800 | tf_op jit(solution)/shard_map/all_to_all | solution.py:14
  121.0 3.1 %multiply_reduce_fusion.25 = (f32[]{:T(128)}, f32[2,8,128]{2,1,0:T(8,128)S(1)}, f32[2,8,128]{2,1,0:T(8,128)S(1)}) fusion(f32[]{:T(128)S(6)} %add.921, f32[2,8,128]{2,1,0:T(8,128)S(1)} %get-tuple-element.241, f32[2,8,128]{2,1,0:T(8,128)S(1)} %get-tuple-element.240, f32[]{:T(128)S(6)} %mul.6034, f32[]{:T(128)} %bitcast.68, f32[]{:T(128)} %bitcast.67, ...), kind=kLoop, calls=%fused_computation.369 | loop fusion | flops 61439 | bytes 114720 | tf_op jit(solution)/shard_map/reduce_sum | solution.py:63
  127.6 1.9 slice_multiply_fusion.71
  131.3 2.7 fusion.185
  141.9 2.7 divide_select_fusion.2
  145.3 1.9 slice_multiply_fusion.70
  148.1 2.6 all-to-all-start.5
  150.7 2.0 slice_multiply_fusion.68
  153.3 4.6 %all-to-all-done.5 = f32[32,1,256]{2,1,0:T(1,128)S(1)} async-done(((f32[32,1,256]{2,1,0:T(1,128)}), f32[32,1,256]{2,1,0:T(1,128)S(1)}, u32[]{:S(2)}, u32[]{:S(2)}) %all-to-all-start.5) | async-done | bytes 32800 | tf_op jit(solution)/shard_map/all_to_all | solution.py:14
  157.9 3.1 %multiply_reduce_fusion.24 = (f32[]{:T(128)}, f32[2,8,128]{2,1,0:T(8,128)S(1)}, f32[2,8,128]{2,1,0:T(8,128)S(1)}) fusion(f32[]{:T(128)S(6)} %add.923, f32[2,8,128]{2,1,0:T(8,128)S(1)} %get-tuple-element.234, f32[2,8,128]{2,1,0:T(8,128)S(1)} %get-tuple-element.233, f32[]{:T(128)S(6)} %mul.6136, f32[]{:T(128)} %bitcast.121, f32[]{:T(128)} %bitcast.120, ...), kind=kLoop, calls=%fused_computation.362 | loop fusion | flops 69631 | bytes 147488 | tf_op jit(solution)/shard_map/reduce_sum | solution.py:63
  164.4 2.6 slice_multiply_fusion.59
  167.1 2.5 slice_multiply_fusion.57
  169.6 2.5 fusion.157
  179.3 2.5 divide_select_fusion.1
  183.9 2.6 all-to-all-start.6
  186.5 2.5 slice_multiply_fusion.58
  189.2 2.5 slice_multiply_fusion.56
  193.7 3.1 %multiply_reduce_fusion.23 = (f32[]{:T(128)}, f32[2,8,128]{2,1,0:T(8,128)S(1)}, f32[2,8,128]{2,1,0:T(8,128)S(1)}) fusion(f32[]{:T(128)S(6)} %add.925, f32[2,8,128]{2,1,0:T(8,128)S(1)} %get-tuple-element.227, f32[2,8,128]{2,1,0:T(8,128)S(1)} %get-tuple-element.226, f32[]{:T(128)S(6)} %mul.6260, f32[]{:T(128)} %bitcast.192, f32[]{:T(128)} %bitcast.191, ...), kind=kLoop, calls=%fused_computation.355 | loop fusion | flops 77823 | bytes 180256 | tf_op jit(solution)/shard_map/reduce_sum | solution.py:63
  200.3 3.0 %slice_multiply_fusion.41 = (f32[1,2048]{1,0:T(1,128)S(1)}, f32[1,2048]{1,0:T(1,128)S(1)}, f32[1,2048]{1,0:T(1,128)S(1)}, f32[1,2048]{1,0:T(1,128)S(1)}, f32[1,2048]{1,0:T(1,128)S(1)}) fusion(f32[8,2048]{1,0:T(8,128)S(1)} %scatter.71, f32[]{:T(128)} %bitcast.271, f32[]{:T(128)} %bitcast.279, f32[]{:T(128)} %bitcast.277, f32[]{:T(128)} %bitcast.275, f32[]{:T(128)} %bitcast.273), kind=kLoop, calls=%fused_computation.466 | loop fusion | flops 10240 | bytes 81940 | tf_op jit(solution)/shard_map/mul | solution.py:48
  203.4 3.2 %slice_multiply_fusion.43 = (f32[1,2048]{1,0:T(1,128)S(1)}, f32[1,2048]{1,0:T(1,128)S(1)}, f32[1,2048]{1,0:T(1,128)S(1)}, f32[1,2048]{1,0:T(1,128)S(1)}, f32[1,2048]{1,0:T(1,128)S(1)}) fusion(f32[8,2048]{1,0:T(8,128)S(1)} %scatter.70, f32[]{:T(128)} %bitcast.270, f32[]{:T(128)} %bitcast.278, f32[]{:T(128)} %bitcast.276, f32[]{:T(128)} %bitcast.274, f32[]{:T(128)} %bitcast.272), kind=kLoop, calls=%fused_computation.468 | loop fusion | flops 10240 | bytes 81940 | tf_op jit(solution)/shard_map/mul | solution.py:48
  206.6 2.6 fusion.267
  211.1 1.9 fusion.113
  217.8 2.6 divide_select_fusion
  223.8 4.4 %all-to-all-start.7 = ((f32[32,1,256]{2,1,0:T(1,128)}), f32[32,1,256]{2,1,0:T(1,128)S(1)}, u32[]{:S(2)}, u32[]{:S(2)}) async-start(f32[32,1,256]{2,1,0:T(1,128)} %broadcast_in_dim.123), calls=%async_computation.7 | async-start | bytes 65536 | tf_op jit(solution)/shard_map/all_to_all | solution.py:14
  230.1 3.1 %slice_multiply_fusion.42 = (f32[1,2048]{1,0:T(1,128)S(1)}, f32[1,2048]{1,0:T(1,128)S(1)}, f32[1,2048]{1,0:T(1,128)S(1)}, f32[1,2048]{1,0:T(1,128)S(1)}, f32[1,2048]{1,0:T(1,128)S(1)}) fusion(f32[8,2048]{1,0:T(8,128)S(1)} %scatter.70, f32[]{:T(128)} %bitcast.341, f32[]{:T(128)} %bitcast.343, f32[]{:T(128)} %bitcast.345, f32[]{:T(128)} %bitcast.347, f32[]{:T(128)} %bitcast.349), kind=kLoop, calls=%fused_computation.467 | loop fusion | flops 10240 | bytes 81940 | tf_op jit(solution)/shard_map/mul | solution.py:61
  233.5 3.2 %slice_multiply_fusion.40 = (f32[1,2048]{1,0:T(1,128)S(1)}, f32[1,2048]{1,0:T(1,128)S(1)}, f32[1,2048]{1,0:T(1,128)S(1)}, f32[1,2048]{1,0:T(1,128)S(1)}, f32[1,2048]{1,0:T(1,128)S(1)}) fusion(f32[8,2048]{1,0:T(8,128)S(1)} %scatter.71, f32[]{:T(128)} %bitcast.342, f32[]{:T(128)} %bitcast.344, f32[]{:T(128)} %bitcast.346, f32[]{:T(128)} %bitcast.348, f32[]{:T(128)} %bitcast.350), kind=kLoop, calls=%fused_computation.465 | loop fusion | flops 10240 | bytes 81940 | tf_op jit(solution)/shard_map/mul | solution.py:61
  237.3 3.2 %multiply_reduce_fusion.22 = (f32[]{:T(128)}, f32[2,8,128]{2,1,0:T(8,128)S(1)}, f32[2,8,128]{2,1,0:T(8,128)S(1)}) fusion(f32[]{:T(128)} %add.927, f32[2,8,128]{2,1,0:T(8,128)S(1)} %get-tuple-element.220, f32[2,8,128]{2,1,0:T(8,128)S(1)} %get-tuple-element.219, f32[]{:T(128)S(6)} %mul.6406, f32[]{:T(128)} %bitcast.281, f32[]{:T(128)} %bitcast.280, ...), kind=kLoop, calls=%fused_computation.348 | loop fusion | flops 86015 | bytes 213024 | tf_op jit(solution)/shard_map/reduce_sum | solution.py:63
  245.3 3.7 %slice_multiply_fusion.21 = (f32[1,2048]{1,0:T(1,128)S(1)}, f32[1,2048]{1,0:T(1,128)S(1)}, f32[1,2048]{1,0:T(1,128)S(1)}, f32[1,2048]{1,0:T(1,128)S(1)}, f32[1,2048]{1,0:T(1,128)S(1)}, /*index=5*/f32[1,2048]{1,0:T(1,128)S(1)}) fusion(f32[8,2048]{1,0:T(8,128)S(1)} %scatter.75, f32[]{:T(128)} %bitcast.376, f32[]{:T(128)} %bitcast.386, f32[]{:T(128)} %bitcast.384, ...), kind=kLoop, calls=%fused_computation.446 | loop fusion | flops 12288 | bytes 98328 | tf_op jit(solution)/shard_map/mul | solution.py:48
  250.2 3.9 %slice_multiply_fusion.23 = (f32[1,2048]{1,0:T(1,128)S(1)}, f32[1,2048]{1,0:T(1,128)S(1)}, f32[1,2048]{1,0:T(1,128)S(1)}, f32[1,2048]{1,0:T(1,128)S(1)}, f32[1,2048]{1,0:T(1,128)S(1)}, /*index=5*/f32[1,2048]{1,0:T(1,128)S(1)}) fusion(f32[8,2048]{1,0:T(8,128)S(1)} %scatter.74, f32[]{:T(128)} %bitcast.375, f32[]{:T(128)} %bitcast.385, f32[]{:T(128)} %bitcast.383, ...), kind=kLoop, calls=%fused_computation.448 | loop fusion | flops 12288 | bytes 98328 | tf_op jit(solution)/shard_map/mul | solution.py:48
  260.9 2.0 fusion.78
  270.1 5.8 %all-to-all-start.8 = ((f32[32,1,256]{2,1,0:T(1,128)}), f32[32,1,256]{2,1,0:T(1,128)S(1)}, u32[]{:S(2)}, u32[]{:S(2)}) async-start(f32[32,1,256]{2,1,0:T(1,128)} %broadcast_in_dim.124), calls=%async_computation.8 | async-start | bytes 65536 | tf_op jit(solution)/shard_map/all_to_all | solution.py:14
  275.9 3.8 %slice_multiply_fusion.20 = (f32[1,2048]{1,0:T(1,128)S(1)}, f32[1,2048]{1,0:T(1,128)S(1)}, f32[1,2048]{1,0:T(1,128)S(1)}, f32[1,2048]{1,0:T(1,128)S(1)}, f32[1,2048]{1,0:T(1,128)S(1)}, /*index=5*/f32[1,2048]{1,0:T(1,128)S(1)}) fusion(f32[8,2048]{1,0:T(8,128)S(1)} %scatter.75, f32[]{:T(128)} %bitcast.460, f32[]{:T(128)} %bitcast.462, f32[]{:T(128)} %bitcast.464, ...), kind=kLoop, calls=%fused_computation.445 | loop fusion | flops 12288 | bytes 98328 | tf_op jit(solution)/shard_map/mul | solution.py:61
  279.7 3.7 %slice_multiply_fusion.22 = (f32[1,2048]{1,0:T(1,128)S(1)}, f32[1,2048]{1,0:T(1,128)S(1)}, f32[1,2048]{1,0:T(1,128)S(1)}, f32[1,2048]{1,0:T(1,128)S(1)}, f32[1,2048]{1,0:T(1,128)S(1)}, /*index=5*/f32[1,2048]{1,0:T(1,128)S(1)}) fusion(f32[8,2048]{1,0:T(8,128)S(1)} %scatter.74, f32[]{:T(128)} %bitcast.459, f32[]{:T(128)} %bitcast.461, f32[]{:T(128)} %bitcast.463, ...), kind=kLoop, calls=%fused_computation.447 | loop fusion | flops 12288 | bytes 98328 | tf_op jit(solution)/shard_map/mul | solution.py:61
  284.3 3.3 %fusion.268 = f32[]{:T(128)} fusion(f32[2,8,128]{2,1,0:T(8,128)S(1)} %bitcast.1500, f32[2,8,128]{2,1,0:T(8,128)S(1)} %bitcast.1410, f32[2,8,128]{2,1,0:T(8,128)S(1)} %bitcast.1406, f32[2,8,128]{2,1,0:T(8,128)S(1)} %bitcast.1414, f32[2,8,128]{2,1,0:T(8,128)S(1)} %bitcast.1275, f32[2,8,128]{2,1,0:T(8,128)S(1)} %bitcast.1291, f32[2,8,128]{2,1,0:T(8,128)S(1)} %bitcast.1279, ...), kind=kLoop, calls=%fused_computation.424 | loop fusion | flops 94207 | bytes 229408 | tf_op jit(solution)/shard_map/reduce_sum | solution.py:63
  (168 shorter events, 94.3 us)
Async XLA Ops:
  0.6 0.7 slice-start
  1.3 22.5 %copy-start = (f32[512,256]{1,0:T(8,128)S(1)}, f32[512,256]{1,0:T(8,128)}, u32[]{:S(2)}) copy-start(f32[512,256]{1,0:T(8,128)} %param.33) | copy-start | bytes 1572868
  2.1 17.9 %all-to-all-start = ((f32[32,8,256]{2,1,0:T(8,128)}), f32[32,8,256]{2,1,0:T(8,128)S(1)}, u32[]{:S(2)}, u32[]{:S(2)}) async-start(f32[32,8,256]{2,1,0:T(8,128)} %broadcast_in_dim.107), calls=%async_computation | async-start | bytes 524288 | tf_op jit(solution)/shard_map/all_to_all | solution.py:14
  24.6 9.8 %all-to-all-start.1 = ((f32[32,1,256]{2,1,0:T(1,128)}), f32[32,1,256]{2,1,0:T(1,128)S(1)}, u32[]{:S(2)}, u32[]{:S(2)}) async-start(f32[32,1,256]{2,1,0:T(1,128)} %broadcast_in_dim.112), calls=%async_computation.1 | async-start | bytes 65536 | tf_op jit(solution)/shard_map/all_to_all | solution.py:14
  45.5 9.8 %all-to-all-start.2 = ((f32[32,1,256]{2,1,0:T(1,128)}), f32[32,1,256]{2,1,0:T(1,128)S(1)}, u32[]{:S(2)}, u32[]{:S(2)}) async-start(f32[32,1,256]{2,1,0:T(1,128)} %broadcast_in_dim.118), calls=%async_computation.2 | async-start | bytes 65536 | tf_op jit(solution)/shard_map/all_to_all | solution.py:14
  76.4 9.8 %all-to-all-start.3 = ((f32[32,1,256]{2,1,0:T(1,128)}), f32[32,1,256]{2,1,0:T(1,128)S(1)}, u32[]{:S(2)}, u32[]{:S(2)}) async-start(f32[32,1,256]{2,1,0:T(1,128)} %broadcast_in_dim.119), calls=%async_computation.3 | async-start | bytes 65536 | tf_op jit(solution)/shard_map/all_to_all | solution.py:14
  111.2 9.8 %all-to-all-start.4 = ((f32[32,1,256]{2,1,0:T(1,128)}), f32[32,1,256]{2,1,0:T(1,128)S(1)}, u32[]{:S(2)}, u32[]{:S(2)}) async-start(f32[32,1,256]{2,1,0:T(1,128)} %broadcast_in_dim.120), calls=%async_computation.4 | async-start | bytes 65536 | tf_op jit(solution)/shard_map/all_to_all | solution.py:14
  148.1 9.8 %all-to-all-start.5 = ((f32[32,1,256]{2,1,0:T(1,128)}), f32[32,1,256]{2,1,0:T(1,128)S(1)}, u32[]{:S(2)}, u32[]{:S(2)}) async-start(f32[32,1,256]{2,1,0:T(1,128)} %broadcast_in_dim.121), calls=%async_computation.5 | async-start | bytes 65536 | tf_op jit(solution)/shard_map/all_to_all | solution.py:14
  183.9 9.8 %all-to-all-start.6 = ((f32[32,1,256]{2,1,0:T(1,128)}), f32[32,1,256]{2,1,0:T(1,128)S(1)}, u32[]{:S(2)}, u32[]{:S(2)}) async-start(f32[32,1,256]{2,1,0:T(1,128)} %broadcast_in_dim.122), calls=%async_computation.6 | async-start | bytes 65536 | tf_op jit(solution)/shard_map/all_to_all | solution.py:14
  223.8 13.5 %all-to-all-start.7 = ((f32[32,1,256]{2,1,0:T(1,128)}), f32[32,1,256]{2,1,0:T(1,128)S(1)}, u32[]{:S(2)}, u32[]{:S(2)}) async-start(f32[32,1,256]{2,1,0:T(1,128)} %broadcast_in_dim.123), calls=%async_computation.7 | async-start | bytes 65536 | tf_op jit(solution)/shard_map/all_to_all | solution.py:14
  270.1 14.2 %all-to-all-start.8 = ((f32[32,1,256]{2,1,0:T(1,128)}), f32[32,1,256]{2,1,0:T(1,128)S(1)}, u32[]{:S(2)}, u32[]{:S(2)}) async-start(f32[32,1,256]{2,1,0:T(1,128)} %broadcast_in_dim.124), calls=%async_computation.8 | async-start | bytes 65536 | tf_op jit(solution)/shard_map/all_to_all | solution.py:14
  289.8 0.7 copy-start.2
  289.8 0.7 copy-start.1

commit v2 on v1

--- a/solution.py
+++ b/solution.py
@@ -1,11 +1,17 @@
 import jax
 import jax.numpy as jnp
 from jax import lax
+from jax.experimental import pallas as pl
+from jax.experimental.pallas import tpu as pltpu
 from jax.sharding import PartitionSpec as P
 
 TILE = 128
 PANEL = 8
 AXES = ("row", "col")
+ROWS, COLS = 4, 8
+BLOCKS = 16
+HALF = BLOCKS // 2
+LANES8 = TILE // 8
 
 
 def everywhere(value):
@@ -15,7 +21,7 @@
     return got.reshape((row_count, col_count) + value.shape)
 
 
-def per_device(matrix):
+def distributed(matrix):
     highest = lax.Precision.HIGHEST
     local_rows, local_cols = matrix.shape
     row_count, col_count = lax.axis_size("row"), lax.axis_size("col")
@@ -73,6 +79,280 @@
     return (updated, refl_rows, image_rows, jnp.stack(subdiag_list))
 
 
+def pick_kernel(index, matrix, block, block_extra):
+    r, c = index[0], index[1]
+    d = lax.rem(r - c + COLS, ROWS)
+    first = (c + d) // ROWS
+
+    def tile(k, m):
+        start = pl.multiple_of(lax.rem(k, ROWS) * TILE, TILE)
+        return matrix[pl.ds(start, TILE), m * TILE : (m + 1) * TILE]
+
+    for m in range(2):
+        for s in range(2):
+            value = tile(first + 2 * m + s, m)
+            block[2 * m + s] = value
+            block_extra[2 * m + s] = value
+    block_extra[4] = jnp.where(d == 0, tile(first + 2, 0), 0.0)
+
+
+def pick(index, matrix):
+    vmem = pl.BlockSpec(memory_space=pltpu.VMEM)
+    return pl.pallas_call(
+        pick_kernel,
+        out_shape=(
+            jax.ShapeDtypeStruct((4, TILE, TILE), jnp.float32),
+            jax.ShapeDtypeStruct((5, TILE, TILE), jnp.float32),
+        ),
+        in_specs=[pl.BlockSpec(memory_space=pltpu.SMEM), vmem],
+        out_specs=(vmem, vmem),
+        compiler_params=pltpu.CompilerParams(vmem_limit_bytes=4 * 1024 * 1024),
+    )(index, matrix)
+
+
+def involution(move):
+    return [(r * COLS + c, move(r, c)[0] * COLS + move(r, c)[1]) for r in range(ROWS) for c in range(COLS)]
+
+
+TO_CORE = involution(lambda r, c: (r, c ^ 1))
+SIDE_A = involution(lambda r, c: (r, c ^ 2 if c % 2 == 0 else c ^ 4))
+SIDE_B = involution(lambda r, c: (r, c ^ 4 if c % 2 == 0 else c ^ 2))
+OUTER = involution(lambda r, c: (r ^ 1, c))
+MIDDLE = [(r * COLS + c, (3 - r) * COLS + c) for r in (1, 2) for c in range(COLS)]
+
+
+def send(value, pairs):
+    return lax.ppermute(value, AXES, pairs)
+
+
+GROUPS = ((0, 1, 2, 3), (4, 5, 8, 10), (6, 9, 12), (7, 11, 13, 14, 15))
+
+
+def gather(a, a5):
+    ua, ma, b, c = send(a5, OUTER), send(a5, MIDDLE), send(a, SIDE_A), send(a, SIDE_B)
+    e, ub, na, mc = send(b, SIDE_B), send(b, OUTER), send(ua, MIDDLE), send(ma, SIDE_B)
+    uc, mb = send(c, OUTER), send(b, MIDDLE)
+    na = jnp.concatenate([na[:4], (a5[4:] + ua[4:]) + (ma[4:] + na[4:])])
+    nb, nc = send(na, SIDE_A), send(na, SIDE_B)
+    ue, me, ne = send(e, OUTER), send(mb, SIDE_B), send(nb, SIDE_B)
+    own = (a, b, c, e, ua, ub, uc, ue, ma, mb, mc, me, na, nb, nc, ne)
+    return own, tuple(send(jnp.concatenate([own[i] for i in group]), TO_CORE) for group in GROUPS)
+
+
+def tile_place(big_r, delta):
+    big_c = (big_r - delta) % BLOCKS
+    return big_c % COLS, delta % 4, 2 * (big_c // COLS) + delta // 4
+
+
+def panel_kernel(index, *refs):
+    own = refs[:16]
+    others = refs[16 : 16 + len(GROUPS)]
+    out, store, extra_store, v_all, w_all, p_all, rows, acc, sems = refs[16 + len(GROUPS) :]
+    r, c = index[0], index[1]
+
+    def source_of(number, col):
+        z, side = number // 4, number % 4
+        row = (r, r ^ 1, 3 - r, (3 - r) ^ 1)[z]
+        even = lax.rem(col, 2) == 0
+        flip = (0, jnp.where(even, 2, 4), jnp.where(even, 4, 2), 6)[side]
+        return row, col ^ flip
+
+    copies = []
+
+    def load(source, start, number, col):
+        row, from_col = source_of(number, col)
+        d = lax.rem(row - from_col + COLS, ROWS)
+        copies.append(
+            pltpu.make_async_copy(source.at[pl.ds(start, 4)], store.at[from_col, d], sems.at[len(copies)])
+        )
+        if number >= 12:
+            copies.append(
+                pltpu.make_async_copy(source.at[start + 4], extra_store.at[from_col], sems.at[len(copies)])
+            )
+
+    for number in range(16):
+        load(own[number], 0, number, c)
+    for ref, group in zip(others, GROUPS):
+        start = 0
+        for number in group:
+            load(ref, start, number, c ^ 1)
+            start += own[number].shape[0]
+    for copy in copies:
+        copy.start()
+    for copy in copies:
+        copy.wait()
+
+    def tile(big_r, delta):
+        if delta == HALF:
+            return extra_store[big_r - HALF]
+        return store[tile_place(big_r, delta)]
+
+    block_row = lax.broadcasted_iota(jnp.int32, (BLOCKS, TILE), 0)
+    lane = lax.broadcasted_iota(jnp.int32, (BLOCKS, TILE), 1)
+    position = block_row * TILE + lane
+    on_diagonal = lax.broadcasted_iota(jnp.int32, (PANEL, TILE), 0) == lax.broadcasted_iota(
+        jnp.int32, (PANEL, TILE), 1
+    )
+    which = lax.broadcasted_iota(jnp.int32, (BLOCKS, PANEL, TILE), 1)
+    which_sub = lax.broadcasted_iota(jnp.int32, (PANEL, TILE), 0)
+
+    def total(x):
+        return jnp.sum(jnp.sum(x, axis=0, keepdims=True), axis=1, keepdims=True)
+
+    for big_c in range(BLOCKS):
+        delta = -big_c % BLOCKS
+        if delta < HALF:
+            rows[big_c] = tile(0, delta)[:16]
+        else:
+            rows[big_c] = jnp.transpose(tile(big_c, big_c))[:16]
+    v_all[...] = jnp.zeros_like(v_all)
+    w_all[...] = jnp.zeros_like(w_all)
+    p_all[...] = rows[:, :PANEL, :]
+    out[BLOCKS] = jnp.zeros((2 * PANEL, TILE), jnp.float32)
+
+    def multiply(vector):
+        for big_c in range(BLOCKS):
+            acc[big_c] = jnp.zeros((8, TILE), jnp.float32)
+        sums = []
+        for big_r in range(BLOCKS):
+            down = jnp.transpose(jnp.broadcast_to(vector[big_r : big_r + 1], (TILE, TILE)))
+            across = None
+            for delta in range(HALF + 1):
+                if delta == HALF and big_r < HALF:
+                    continue
+                big_c = (big_r - delta) % BLOCKS
+                t = tile(big_r, delta)
+                acc[big_c] += jnp.sum((t * down).reshape(LANES8, 8, TILE), axis=0)
+                if delta > 0:
+                    part = t * vector[big_c : big_c + 1]
+                    across = part if across is None else across + part
+            sums.append(jnp.sum(jnp.transpose(across).reshape(LANES8, 8, TILE), axis=0))
+        for big_r in range(BLOCKS):
+            acc[big_r] += sums[big_r]
+        return jnp.sum(acc[...], axis=1)
+
+    def step(j, column):
+        first = position == j + 1
+        tail = jnp.where(position > j + 1, column, 0.0)
+        tail_product = multiply(tail)
+        leading = total(jnp.where(first, column, 0.0))
+        squares = total(tail * tail)
+        radius = jnp.sqrt(leading * leading + squares)
+        denominator = leading + radius
+        scaling = denominator / radius
+        inverse = 1.0 / denominator
+        v = jnp.where(first, 1.0, tail * inverse)
+        v3 = v[:, None, :]
+        refl, images = v_all[...], w_all[...]
+        refl_proj = jnp.sum(jnp.sum(refl * v3, axis=0), axis=1, keepdims=True)
+        image_proj = jnp.sum(jnp.sum(images * v3, axis=0), axis=1, keepdims=True)
+        correction = jnp.sum(refl * image_proj[None] + images * refl_proj[None], axis=1)
+        v_correction = 2.0 * jnp.sum(refl_proj * image_proj, axis=0, keepdims=True)
+        product = tail_product * inverse + rows[:, pl.ds(j + 1, 1), :].reshape(BLOCKS, TILE)
+        inner = scaling * (total(v * product) - v_correction)
+        w = scaling * (product - correction) - (0.5 * scaling * inner) * v
+        w3 = w[:, None, :]
+        v_heads = jnp.sum(jnp.where(on_diagonal, v[0:1], 0.0), axis=1, keepdims=True)
+        w_heads = jnp.sum(jnp.where(on_diagonal, w[0:1], 0.0), axis=1, keepdims=True)
+        panel = p_all[...] - w_heads[None] * v3 - v_heads[None] * w3
+        p_all[...] = panel
+        v_all[...] = jnp.where(which == j, v3, refl)
+        w_all[...] = jnp.where(which == j, w3, images)
+        out[BLOCKS, :PANEL, :] = jnp.where(which_sub == j, -radius, out[BLOCKS, :PANEL, :])
+        return jnp.sum(jnp.where(which == j + 1, panel, 0.0), axis=1)
+
+    lax.fori_loop(0, PANEL, step, rows[:, 0, :])
+    out[:BLOCKS, :PANEL, :] = v_all[...]
+    out[:BLOCKS, PANEL:, :] = w_all[...]
+
+
+def reduce_panel(index, own, others):
+    held = pl.BlockSpec(memory_space=pltpu.VMEM)
+    vmem = pl.BlockSpec(memory_space=pltpu.VMEM)
+    return pl.pallas_call(
+        panel_kernel,
+        out_shape=jax.ShapeDtypeStruct((BLOCKS + 1, 2 * PANEL, TILE), jnp.float32),
+        in_specs=[pl.BlockSpec(memory_space=pltpu.SMEM)] + [held] * (16 + len(others)),
+        out_specs=vmem,
+        scratch_shapes=[
+            pltpu.VMEM((COLS, ROWS, 4, TILE, TILE), jnp.float32),
+            pltpu.VMEM((HALF, TILE, TILE), jnp.float32),
+            pltpu.VMEM((BLOCKS, PANEL, TILE), jnp.float32),
+            pltpu.VMEM((BLOCKS, PANEL, TILE), jnp.float32),
+            pltpu.VMEM((BLOCKS, PANEL, TILE), jnp.float32),
+            pltpu.VMEM((BLOCKS, 2 * PANEL, TILE), jnp.float32),
+            pltpu.VMEM((BLOCKS, 8, TILE), jnp.float32),
+            pltpu.SemaphoreType.DMA((40,)),
+        ],
+        compiler_params=pltpu.CompilerParams(vmem_limit_bytes=24 * 1024 * 1024),
+    )(index, *own, *others)
+
+
+def update_kernel(index, matrix, mine, theirs, updated, refl_rows, image_rows, subdiag, held):
+    r, c = index[0], index[1]
+
+    @pl.when(jnp.logical_or(r == 1, r == 2))
+    def _():
+        held[...] = mine[...]
+
+    @pl.when(jnp.logical_or(r == 0, r == 3))
+    def _():
+        held[...] = theirs[...]
+
+    right = []
+    for m in range(2):
+        both = held[m * COLS + c]
+        right.append(jnp.concatenate([both[PANEL:], both[:PANEL]], axis=0))
+    right = jnp.concatenate(right, axis=1)
+    for k in range(4):
+        left = held[k * ROWS + r]
+        span = slice(k * TILE, (k + 1) * TILE)
+        updated[span, :] = matrix[span, :] - lax.dot_general(
+            left,
+            right,
+            (((0,), (0,)), ((), ())),
+            precision=lax.Precision.HIGHEST,
+            preferred_element_type=jnp.float32,
+        )
+        refl_rows[:, span] = left[:PANEL]
+        image_rows[:, span] = left[PANEL:]
+    subdiag[...] = held[BLOCKS, :PANEL, :]
+
+
+def finish(index, matrix, mine, theirs):
+    vmem = pl.BlockSpec(memory_space=pltpu.VMEM)
+    rows, _ = matrix.shape
+    return pl.pallas_call(
+        update_kernel,
+        out_shape=(
+            jax.ShapeDtypeStruct(matrix.shape, jnp.float32),
+            jax.ShapeDtypeStruct((PANEL, rows), jnp.float32),
+            jax.ShapeDtypeStruct((PANEL, rows), jnp.float32),
+            jax.ShapeDtypeStruct((PANEL, TILE), jnp.float32),
+        ),
+        in_specs=[pl.BlockSpec(memory_space=pltpu.SMEM), vmem, vmem, vmem],
+        out_specs=(vmem,) * 4,
+        scratch_shapes=[pltpu.VMEM(mine.shape, jnp.float32)],
+        compiler_params=pltpu.CompilerParams(vmem_limit_bytes=6 * 1024 * 1024),
+    )(index, matrix, mine, theirs)
+
+
+def gathered(matrix):
+    index = jnp.stack([lax.axis_index("row"), lax.axis_index("col")]).astype(jnp.int32)
+    own, others = gather(*pick(index, matrix))
+    mine = reduce_panel(index, own, others)
+    theirs = send(mine, OUTER)
+    updated, refl_rows, image_rows, subdiag = finish(index, matrix, mine, theirs)
+    return updated, refl_rows, image_rows, subdiag[:, 0]
+
+
+def per_device(matrix):
+    grid = (lax.axis_size("row"), lax.axis_size("col"))
+    if grid == (ROWS, COLS) and matrix.shape == (BLOCKS // ROWS * TILE, BLOCKS // COLS * TILE):
+        return gathered(matrix)
+    return distributed(matrix)
+
+
 def solution(mesh):
     return jax.shard_map(
         per_device,

time: 295 us -> 83.4 us (0.28)
  other arithmetic: 139 us -> 0.35 us
  local copies, waits for them, and re-layouts: 43.2 us -> 1.8 us
  between operations: 33.7 us -> 0.8 us
  Pallas kernels: 0 us -> 16.2 us
  waiting for transfers between devices: 40.5 us -> 32.7 us
    mul x27 -> x0, other arithmetic: 55.1 us -> none  [the longest x13 27.2 us: per_device(): image = image - image_proj[k] * refl[k] - refl_proj[k] * images[k]]
    all_to_all x9 -> x0, waiting for transfers between devices: 40.5 us -> none  [everywhere(): got = lax.all_to_all(spread, AXES, 0, 0, tiled=False)]
    reduce_sum x38 -> x0, other arithmetic: 37 us -> none  [the longest x8 21.5 us: per_device(): image = image - 0.5 * scaling * jnp.sum(image * reflector) * reflector]
    slice x57 -> x2, local copies, waits for them, and re-layouts: 34.1 us -> 0.64 us  [the longest x1 0.63 us: gathered(): return (updated, refl_rows, image_rows, subdiag[:, 0])]
    all_to_all x9 -> x0, starting transfers between devices: 33 us -> none  [everywhere(): got = lax.all_to_all(spread, AXES, 0, 0, tiled=False)]
    ppermute x0 -> x20, waiting for transfers between devices: none -> 32.7 us  [send(): return lax.ppermute(value, AXES, pairs)]
    ppermute x0 -> x20, starting transfers between devices: none -> 31.3 us  [send(): return lax.ppermute(value, AXES, pairs)]
    select_n x16 -> x0, other arithmetic: 26 us -> none  [the longest x15 23.4 us: per_device(): reflector = jnp.where(position == j + 1, 1.0, tail / denominator)]
  transfers between devices with their start and end apart: 9 -> 20, of which waited for: 7 -> 7; matrix products, arithmetic and copies ran while one was open for 10% -> 0% of each run, Pallas kernels for 0% -> 0%
where the time goes in v2:
time: 83.4 us; the launch traced here: 83.2 us
  waiting for transfers between devices  32.7 us (39%)
  starting transfers between devices  31.3 us (38%)
  Pallas kernels  16.2 us (19%)
  local copies, waits for them, and re-layouts  1.8 us (2%)
    ppermute x20, waiting for transfers between devices, send(): return lax.ppermute(value, AXES, pairs)  32.7 us
    ppermute x20, starting transfers between devices, send(): return lax.ppermute(value, AXES, pairs)  31.3 us
    pallas_call x1, Pallas kernels, reduce_panel(): pl.pallas_call(panel_kernel, out_shape=jax.ShapeDtypeStruct((BLOCKS + 1,...  13.7 us
    pallas_call x1, Pallas kernels, finish(): pl.pallas_call(update_kernel, out_shape=(jax.ShapeDtypeStruct(matrix.shap...  1.98 us
  transfers between devices with their start and end apart: 20, of which 7 were waited for; matrix products, arithmetic and copies ran while one was open for 0% of the time, Pallas kernels for 0%

profile of v2, /device:TPU:0, one launch (start us, length us, event | category | flops | bytes accessed | tf_op | source)
XLA Modules:
  0.0 83.2 jit_solution(15041651138015896116)
XLA Ops:
  0.6 0.1 pad_add_fusion.index
  0.7 1.0 %copy-done = f32[512,256]{1,0:T(8,128)S(1)} copy-done((f32[512,256]{1,0:T(8,128)S(1)}, f32[512,256]{1,0:T(8,128)}, u32[]{:S(2)}) %copy-start) | copy-done | bytes 524312
  1.8 0.6 shard_map.46
  2.4 3.1 %collective-permute-start.3 = (f32[5,128,128]{2,1,0:T(8,128)S(1)}, f32[5,128,128]{2,1,0:T(8,128)S(1)}, u32[]{:S(2)}, u32[]{:S(2)}) collective-permute-start(f32[5,128,128]{2,1,0:T(8,128)S(1)} %get-tuple-element.11), channel_id=1, source_target_pairs={{0,8},{1,9},{2,10},{3,11},{4,12},{5,13},{6,14},{7,15},{8,0},{9,1},... | collective-permute-start | bytes 983048 | tf_op jit(solution)/shard_map/ppermute | solution.py:125
  5.4 1.5 %collective-permute-start = (f32[4,128,128]{2,1,0:T(8,128)S(1)}, f32[4,128,128]{2,1,0:T(8,128)S(1)}, u32[]{:S(2)}, u32[]{:S(2)}) collective-permute-start(f32[4,128,128]{2,1,0:T(8,128)S(1)} %get-tuple-element.10.refs_0_), channel_id=1, source_target_pairs={{0,2},{1,5},{2,0},{3,7},{4,6},{5,1},{6,4},{7,3},{8,10},{9,13},{10,... | collective-permute-start | bytes 786440 | tf_op jit(solution)/shard_map/ppermute | solution.py:125
  6.9 0.7 collective-permute-start.7
  7.6 5.5 %collective-permute-done.3.refs_4_ = f32[5,128,128]{2,1,0:T(8,128)S(1)} collective-permute-done((f32[5,128,128]{2,1,0:T(8,128)S(1)}, f32[5,128,128]{2,1,0:T(8,128)S(1)}, u32[]{:S(2)}, u32[]{:S(2)}) %collective-permute-start.3) | collective-permute-done | bytes 327712 | tf_op jit(solution)/shard_map/ppermute | solution.py:125
  13.2 0.7 collective-permute-start.11
  13.8 0.0 collective-permute-done.refs_1_
  13.8 1.7 %collective-permute-start.2 = (f32[4,128,128]{2,1,0:T(8,128)S(1)}, f32[4,128,128]{2,1,0:T(8,128)S(1)}, u32[]{:S(2)}, u32[]{:S(2)}) collective-permute-start(f32[4,128,128]{2,1,0:T(8,128)S(1)} %collective-permute-done.refs_1_), channel_id=1, source_target_pairs={{0,4},{1,3},{2,6},{3,1},{4,0},{5,7},{6,2},{7,5},{8,12},{9,11},{10,... | collective-permute-start | bytes 786440 | tf_op jit(solution)/shard_map/ppermute | solution.py:125
  15.6 0.7 collective-permute-start.8
  16.3 4.0 %collective-permute-done.2.refs_3_ = f32[4,128,128]{2,1,0:T(8,128)S(1)} collective-permute-done((f32[4,128,128]{2,1,0:T(8,128)S(1)}, f32[4,128,128]{2,1,0:T(8,128)S(1)}, u32[]{:S(2)}, u32[]{:S(2)}) %collective-permute-start.2) | collective-permute-done | bytes 262176 | tf_op jit(solution)/shard_map/ppermute | solution.py:125
  20.3 4.5 %collective-permute-start.6 = (f32[4,128,128]{2,1,0:T(8,128)S(1)}, f32[4,128,128]{2,1,0:T(8,128)S(1)}, u32[]{:S(2)}, u32[]{:S(2)}) collective-permute-start(f32[4,128,128]{2,1,0:T(8,128)S(1)} %collective-permute-done.2.refs_3_), channel_id=1, source_target_pairs={{0,8},{1,9},{2,10},{3,11},{4,12},{5,13},{6,14},{7,15},{8,0},{9,1},... | collective-permute-start | bytes 786440 | tf_op jit(solution)/shard_map/ppermute | solution.py:125
  24.8 0.0 collective-permute-done.7.refs_8_
  24.8 0.0 collective-permute-done.11
  24.9 1.6 %collective-permute-start.12 = (f32[5,128,128]{2,1,0:T(8,128)S(1)}, f32[5,128,128]{2,1,0:T(8,128)S(1)}, u32[]{:S(2)}, u32[]{:S(2)}) collective-permute-start(f32[5,128,128]{2,1,0:T(8,128)S(1)} %pad_maximum_fusion.3.refs_12_), channel_id=1, source_target_pairs={{0,2},{1,5},{2,0},{3,7},{4,6},{5,1},{6,4},{7,3},{8,10},{9,13},{10,... | collective-permute-start | bytes 983048 | tf_op jit(solution)/shard_map/ppermute | solution.py:125
  26.5 0.0 collective-permute-done.8.refs_9_
  26.5 1.5 %collective-permute-start.10 = (f32[4,128,128]{2,1,0:T(8,128)S(1)}, f32[4,128,128]{2,1,0:T(8,128)S(1)}, u32[]{:S(2)}, u32[]{:S(2)}) collective-permute-start(f32[4,128,128]{2,1,0:T(8,128)S(1)} %collective-permute-done.8.refs_9_), channel_id=1, source_target_pairs={{0,4},{1,3},{2,6},{3,1},{4,0},{5,7},{6,2},{7,5},{8,12},{9,11},{10,... | collective-permute-start | bytes 786440 | tf_op jit(solution)/shard_map/ppermute | solution.py:125
  28.0 0.5 collective-permute-start.1
  28.5 5.3 %collective-permute-start.4 = (f32[4,128,128]{2,1,0:T(8,128)S(1)}, f32[4,128,128]{2,1,0:T(8,128)S(1)}, u32[]{:S(2)}, u32[]{:S(2)}) collective-permute-start(f32[4,128,128]{2,1,0:T(8,128)S(1)} %collective-permute-done.refs_1_), channel_id=1, source_target_pairs={{0,8},{1,9},{2,10},{3,11},{4,12},{5,13},{6,14},{7,15},{8,0},{9,1},... | collective-permute-start | bytes 786440 | tf_op jit(solution)/shard_map/ppermute | solution.py:125
  33.8 0.0 collective-permute-done.6.refs_7_
  33.8 0.7 collective-permute-start.13
  34.5 0.0 collective-permute-done.10.refs_11_
  34.6 1.4 %collective-permute-start.9 = (f32[5,128,128]{2,1,0:T(8,128)S(1)}, f32[5,128,128]{2,1,0:T(8,128)S(1)}, u32[]{:S(2)}, u32[]{:S(2)}) collective-permute-start(f32[5,128,128]{2,1,0:T(8,128)S(1)} %collective-permute-done.7.refs_8_), channel_id=1, source_target_pairs={{0,4},{1,3},{2,6},{3,1},{4,0},{5,7},{6,2},{7,5},{8,12},{9,11},{10,... | collective-permute-start | bytes 983048 | tf_op jit(solution)/shard_map/ppermute | solution.py:125
  36.0 0.0 collective-permute-done.12.refs_13_
  36.0 1.2 %collective-permute-start.14 = (f32[5,128,128]{2,1,0:T(8,128)S(1)}, f32[5,128,128]{2,1,0:T(8,128)S(1)}, u32[]{:S(2)}, u32[]{:S(2)}) collective-permute-start(f32[5,128,128]{2,1,0:T(8,128)S(1)} %collective-permute-done.12.refs_13_), channel_id=1, source_target_pairs={{0,4},{1,3},{2,6},{3,1},{4,0},{5,7},{6,2},{7,5},{8,12},{9,11},{10,... | collective-permute-start | bytes 983048 | tf_op jit(solution)/shard_map/ppermute | solution.py:125
  37.2 3.7 %collective-permute-done.13.refs_14_ = f32[5,128,128]{2,1,0:T(8,128)S(1)} collective-permute-done((f32[5,128,128]{2,1,0:T(8,128)S(1)}, f32[5,128,128]{2,1,0:T(8,128)S(1)}, u32[]{:S(2)}, u32[]{:S(2)}) %collective-permute-start.13) | collective-permute-done | bytes 327712 | tf_op jit(solution)/shard_map/ppermute | solution.py:125
  40.9 7.0 %collective-permute-done.14.refs_15_ = f32[5,128,128]{2,1,0:T(8,128)S(1)} collective-permute-done((f32[5,128,128]{2,1,0:T(8,128)S(1)}, f32[5,128,128]{2,1,0:T(8,128)S(1)}, u32[]{:S(2)}, u32[]{:S(2)}) %collective-permute-start.14) | collective-permute-done | bytes 327712 | tf_op jit(solution)/shard_map/ppermute | solution.py:125
  48.0 0.1 collective-permute-start.18
  48.0 0.0 collective-permute-done.1.refs_2_
  48.0 3.7 %collective-permute-start.5 = (f32[4,128,128]{2,1,0:T(8,128)S(1)}, f32[4,128,128]{2,1,0:T(8,128)S(1)}, u32[]{:S(2)}, u32[]{:S(2)}) collective-permute-start(f32[4,128,128]{2,1,0:T(8,128)S(1)} %collective-permute-done.1.refs_2_), channel_id=1, source_target_pairs={{0,8},{1,9},{2,10},{3,11},{4,12},{5,13},{6,14},{7,15},{8,0},{9,1},... | collective-permute-start | bytes 786440 | tf_op jit(solution)/shard_map/ppermute | solution.py:125
  51.7 0.0 collective-permute-done.4.refs_5_
  51.7 0.0 collective-permute-done.9.refs_10_
  51.7 0.1 pad_maximum_fusion
  51.8 0.2 collective-permute-start.16
  52.0 0.1 pad_maximum_fusion.1
  52.1 0.4 collective-permute-start.15
  52.5 6.1 %collective-permute-done.5.refs_6_ = f32[4,128,128]{2,1,0:T(8,128)S(1)} collective-permute-done((f32[4,128,128]{2,1,0:T(8,128)S(1)}, f32[4,128,128]{2,1,0:T(8,128)S(1)}, u32[]{:S(2)}, u32[]{:S(2)}) %collective-permute-start.5) | collective-permute-done | bytes 262176 | tf_op jit(solution)/shard_map/ppermute | solution.py:125
  58.6 0.1 pad_maximum_fusion.2
  58.7 0.0 copy-start.1
  58.7 0.1 collective-permute-start.17
  58.7 2.4 %collective-permute-done.17.refs_18_ = f32[13,128,128]{2,1,0:T(8,128)S(1)} collective-permute-done((f32[13,128,128]{2,1,0:T(8,128)S(1)}, f32[13,128,128]{2,1,0:T(8,128)S(1)}, u32[]{:S(2)}, u32[]{:S(2)}) %collective-permute-start.17) | collective-permute-done | bytes 852000 | tf_op jit(solution)/shard_map/ppermute | solution.py:125
  61.1 0.0 collective-permute-done.15.refs_16_
  61.1 13.7 %shard_map.47.mine = f32[17,16,128]{2,1,0:T(8,128)S(1)} custom-call(s32[2]{0:T(128)S(1)} %pad_add_fusion.index, f32[4,128,128]{2,1,0:T(8,128)S(1)} %get-tuple-element.10.refs_0_, f32[4,128,128]{2,1,0:T(8,128)S(1)} %collective-permute-done.refs_1_, f32[4,128,128]{2,1,0:T(8,128)S(1)} %collective-permute-done.1.refs_2_, ...), custom_call_target="tpu_custom_call" | custom-call | tf_op jit(solution)/shard_map/pallas_call | solution.py:272
  74.8 1.8 %collective-permute-start.19 = (f32[17,16,128]{2,1,0:T(8,128)S(1)}, f32[17,16,128]{2,1,0:T(8,128)S(1)}, u32[]{:S(2)}, u32[]{:S(2)}) collective-permute-start(f32[17,16,128]{2,1,0:T(8,128)S(1)} %shard_map.47.mine), channel_id=1, source_target_pairs={{0,8},{1,9},{2,10},{3,11},{4,12},{5,13},{6,14},{7,15},{8,0},{9,1},... | collective-permute-start | bytes 417800 | tf_op jit(solution)/shard_map/ppermute | solution.py:125
  76.6 4.0 %collective-permute-done.19.theirs = f32[17,16,128]{2,1,0:T(8,128)S(1)} collective-permute-done((f32[17,16,128]{2,1,0:T(8,128)S(1)}, f32[17,16,128]{2,1,0:T(8,128)S(1)}, u32[]{:S(2)}, u32[]{:S(2)}) %collective-permute-start.19) | collective-permute-done | bytes 139296 | tf_op jit(solution)/shard_map/ppermute | solution.py:125
  80.6 2.0 %shard_map.48 = (f32[512,256]{1,0:T(8,128)}, f32[8,512]{1,0:T(8,128)}, f32[8,512]{1,0:T(8,128)}, f32[8,128]{1,0:T(8,128)S(1)}) custom-call(s32[2]{0:T(128)S(1)} %pad_add_fusion.index, f32[512,256]{1,0:T(8,128)S(1)} %copy-done.1, f32[17,16,128]{2,1,0:T(8,128)S(1)} %shard_map.47.mine, f32[17,16,128]{2,1,0:T(8,128)S(1)} %collective-permute-done.19.theirs), custom_call_target="tpu_custom_call" | custom-call | tf_op jit(solution)/shard_map/pallas_call | solution.py:325
  82.6 0.6 slice_reduce_fusion
  (12 shorter events, 0.2 us)
Async XLA Ops:
  0.7 1.0 %copy-start = (f32[512,256]{1,0:T(8,128)S(1)}, f32[512,256]{1,0:T(8,128)}, u32[]{:S(2)}) copy-start(f32[512,256]{1,0:T(8,128)} %matrix.3) | copy-start | bytes 1572868
  2.4 10.8 %collective-permute-start.3 = (f32[5,128,128]{2,1,0:T(8,128)S(1)}, f32[5,128,128]{2,1,0:T(8,128)S(1)}, u32[]{:S(2)}, u32[]{:S(2)}) collective-permute-start(f32[5,128,128]{2,1,0:T(8,128)S(1)} %get-tuple-element.11), channel_id=1, source_target_pairs={{0,8},{1,9},{2,10},{3,11},{4,12},{5,13},{6,14},{7,15},{8,0},{9,1},... | collective-permute-start | bytes 983048 | tf_op jit(solution)/shard_map/ppermute | solution.py:125
  5.4 8.4 %collective-permute-start = (f32[4,128,128]{2,1,0:T(8,128)S(1)}, f32[4,128,128]{2,1,0:T(8,128)S(1)}, u32[]{:S(2)}, u32[]{:S(2)}) collective-permute-start(f32[4,128,128]{2,1,0:T(8,128)S(1)} %get-tuple-element.10.refs_0_), channel_id=1, source_target_pairs={{0,2},{1,5},{2,0},{3,7},{4,6},{5,1},{6,4},{7,3},{8,10},{9,13},{10,... | collective-permute-start | bytes 786440 | tf_op jit(solution)/shard_map/ppermute | solution.py:125
  6.9 17.9 %collective-permute-start.7 = (f32[5,128,128]{2,1,0:T(8,128)S(1)}, f32[5,128,128]{2,1,0:T(8,128)S(1)}, u32[]{:S(2)}, u32[]{:S(2)}) collective-permute-start(f32[5,128,128]{2,1,0:T(8,128)S(1)} %get-tuple-element.11), channel_id=1, source_target_pairs={{8,16},{9,17},{10,18},{11,19},{12,20},{13,21},{14,22},{15,23},{16,... | collective-permute-start | bytes 983048 | tf_op jit(solution)/shard_map/ppermute | solution.py:125
  13.2 11.7 %collective-permute-start.11 = (f32[5,128,128]{2,1,0:T(8,128)S(1)}, f32[5,128,128]{2,1,0:T(8,128)S(1)}, u32[]{:S(2)}, u32[]{:S(2)}) collective-permute-start(f32[5,128,128]{2,1,0:T(8,128)S(1)} %collective-permute-done.3.refs_4_), channel_id=1, source_target_pairs={{8,16},{9,17},{10,18},{11,19},{12,20},{13,21},{14,22},{15,23},{16,... | collective-permute-start | bytes 983048 | tf_op jit(solution)/shard_map/ppermute | solution.py:125
  13.8 6.4 %collective-permute-start.2 = (f32[4,128,128]{2,1,0:T(8,128)S(1)}, f32[4,128,128]{2,1,0:T(8,128)S(1)}, u32[]{:S(2)}, u32[]{:S(2)}) collective-permute-start(f32[4,128,128]{2,1,0:T(8,128)S(1)} %collective-permute-done.refs_1_), channel_id=1, source_target_pairs={{0,4},{1,3},{2,6},{3,1},{4,0},{5,7},{6,2},{7,5},{8,12},{9,11},{10,... | collective-permute-start | bytes 786440 | tf_op jit(solution)/shard_map/ppermute | solution.py:125
  15.6 10.9 %collective-permute-start.8 = (f32[4,128,128]{2,1,0:T(8,128)S(1)}, f32[4,128,128]{2,1,0:T(8,128)S(1)}, u32[]{:S(2)}, u32[]{:S(2)}) collective-permute-start(f32[4,128,128]{2,1,0:T(8,128)S(1)} %collective-permute-done.refs_1_), channel_id=1, source_target_pairs={{8,16},{9,17},{10,18},{11,19},{12,20},{13,21},{14,22},{15,23},{16,... | collective-permute-start | bytes 786440 | tf_op jit(solution)/shard_map/ppermute | solution.py:125
  20.3 13.5 %collective-permute-start.6 = (f32[4,128,128]{2,1,0:T(8,128)S(1)}, f32[4,128,128]{2,1,0:T(8,128)S(1)}, u32[]{:S(2)}, u32[]{:S(2)}) collective-permute-start(f32[4,128,128]{2,1,0:T(8,128)S(1)} %collective-permute-done.2.refs_3_), channel_id=1, source_target_pairs={{0,8},{1,9},{2,10},{3,11},{4,12},{5,13},{6,14},{7,15},{8,0},{9,1},... | collective-permute-start | bytes 786440 | tf_op jit(solution)/shard_map/ppermute | solution.py:125
  24.9 11.0 %collective-permute-start.12 = (f32[5,128,128]{2,1,0:T(8,128)S(1)}, f32[5,128,128]{2,1,0:T(8,128)S(1)}, u32[]{:S(2)}, u32[]{:S(2)}) collective-permute-start(f32[5,128,128]{2,1,0:T(8,128)S(1)} %pad_maximum_fusion.3.refs_12_), channel_id=1, source_target_pairs={{0,2},{1,5},{2,0},{3,7},{4,6},{5,1},{6,4},{7,3},{8,10},{9,13},{10,... | collective-permute-start | bytes 983048 | tf_op jit(solution)/shard_map/ppermute | solution.py:125
  26.5 8.1 %collective-permute-start.10 = (f32[4,128,128]{2,1,0:T(8,128)S(1)}, f32[4,128,128]{2,1,0:T(8,128)S(1)}, u32[]{:S(2)}, u32[]{:S(2)}) collective-permute-start(f32[4,128,128]{2,1,0:T(8,128)S(1)} %collective-permute-done.8.refs_9_), channel_id=1, source_target_pairs={{0,4},{1,3},{2,6},{3,1},{4,0},{5,7},{6,2},{7,5},{8,12},{9,11},{10,... | collective-permute-start | bytes 786440 | tf_op jit(solution)/shard_map/ppermute | solution.py:125
  28.0 20.0 %collective-permute-start.1 = (f32[4,128,128]{2,1,0:T(8,128)S(1)}, f32[4,128,128]{2,1,0:T(8,128)S(1)}, u32[]{:S(2)}, u32[]{:S(2)}) collective-permute-start(f32[4,128,128]{2,1,0:T(8,128)S(1)} %get-tuple-element.10.refs_0_), channel_id=1, source_target_pairs={{0,4},{1,3},{2,6},{3,1},{4,0},{5,7},{6,2},{7,5},{8,12},{9,11},{10,... | collective-permute-start | bytes 786440 | tf_op jit(solution)/shard_map/ppermute | solution.py:125
  28.5 23.2 %collective-permute-start.4 = (f32[4,128,128]{2,1,0:T(8,128)S(1)}, f32[4,128,128]{2,1,0:T(8,128)S(1)}, u32[]{:S(2)}, u32[]{:S(2)}) collective-permute-start(f32[4,128,128]{2,1,0:T(8,128)S(1)} %collective-permute-done.refs_1_), channel_id=1, source_target_pairs={{0,8},{1,9},{2,10},{3,11},{4,12},{5,13},{6,14},{7,15},{8,0},{9,1},... | collective-permute-start | bytes 786440 | tf_op jit(solution)/shard_map/ppermute | solution.py:125
  33.8 7.1 %collective-permute-start.13 = (f32[5,128,128]{2,1,0:T(8,128)S(1)}, f32[5,128,128]{2,1,0:T(8,128)S(1)}, u32[]{:S(2)}, u32[]{:S(2)}) collective-permute-start(f32[5,128,128]{2,1,0:T(8,128)S(1)} %pad_maximum_fusion.3.refs_12_), channel_id=1, source_target_pairs={{0,4},{1,3},{2,6},{3,1},{4,0},{5,7},{6,2},{7,5},{8,12},{9,11},{10,... | collective-permute-start | bytes 983048 | tf_op jit(solution)/shard_map/ppermute | solution.py:125
  34.6 17.1 %collective-permute-start.9 = (f32[5,128,128]{2,1,0:T(8,128)S(1)}, f32[5,128,128]{2,1,0:T(8,128)S(1)}, u32[]{:S(2)}, u32[]{:S(2)}) collective-permute-start(f32[5,128,128]{2,1,0:T(8,128)S(1)} %collective-permute-done.7.refs_8_), channel_id=1, source_target_pairs={{0,4},{1,3},{2,6},{3,1},{4,0},{5,7},{6,2},{7,5},{8,12},{9,11},{10,... | collective-permute-start | bytes 983048 | tf_op jit(solution)/shard_map/ppermute | solution.py:125
  36.0 12.0 %collective-permute-start.14 = (f32[5,128,128]{2,1,0:T(8,128)S(1)}, f32[5,128,128]{2,1,0:T(8,128)S(1)}, u32[]{:S(2)}, u32[]{:S(2)}) collective-permute-start(f32[5,128,128]{2,1,0:T(8,128)S(1)} %collective-permute-done.12.refs_13_), channel_id=1, source_target_pairs={{0,4},{1,3},{2,6},{3,1},{4,0},{5,7},{6,2},{7,5},{8,12},{9,11},{10,... | collective-permute-start | bytes 983048 | tf_op jit(solution)/shard_map/ppermute | solution.py:125
  48.0 13.2 %collective-permute-start.18 = (f32[23,128,128]{2,1,0:T(8,128)S(1)}, f32[23,128,128]{2,1,0:T(8,128)S(1)}, u32[]{:S(2)}, u32[]{:S(2)}) collective-permute-start(f32[23,128,128]{2,1,0:T(8,128)S(1)} %constant_dynamic-update-slice_fusion), channel_id=1, source_target_pairs={{0,1},{1,0},{2,3},{3,2},{4,5},{5,4},{6,7},{7,6},{8,9},{9,8},{10,11... | collective-permute-start | bytes 4521992 | tf_op jit(solution)/shard_map/ppermute | solution.py:125
  48.0 10.5 %collective-permute-start.5 = (f32[4,128,128]{2,1,0:T(8,128)S(1)}, f32[4,128,128]{2,1,0:T(8,128)S(1)}, u32[]{:S(2)}, u32[]{:S(2)}) collective-permute-start(f32[4,128,128]{2,1,0:T(8,128)S(1)} %collective-permute-done.1.refs_2_), channel_id=1, source_target_pairs={{0,8},{1,9},{2,10},{3,11},{4,12},{5,13},{6,14},{7,15},{8,0},{9,1},... | collective-permute-start | bytes 786440 | tf_op jit(solution)/shard_map/ppermute | solution.py:125
  51.8 9.3 %collective-permute-start.16 = (f32[19,128,128]{2,1,0:T(8,128)S(1)}, f32[19,128,128]{2,1,0:T(8,128)S(1)}, u32[]{:S(2)}, u32[]{:S(2)}) collective-permute-start(f32[19,128,128]{2,1,0:T(8,128)S(1)} %pad_maximum_fusion), channel_id=1, source_target_pairs={{0,1},{1,0},{2,3},{3,2},{4,5},{5,4},{6,7},{7,6},{8,9},{9,8},{10,11... | collective-permute-start | bytes 3735560 | tf_op jit(solution)/shard_map/ppermute | solution.py:125
  52.1 9.0 %collective-permute-start.15 = (f32[16,128,128]{2,1,0:T(8,128)S(1)}, f32[16,128,128]{2,1,0:T(8,128)S(1)}, u32[]{:S(2)}, u32[]{:S(2)}) collective-permute-start(f32[16,128,128]{2,1,0:T(8,128)S(1)} %pad_maximum_fusion.1), channel_id=1, source_target_pairs={{0,1},{1,0},{2,3},{3,2},{4,5},{5,4},{6,7},{7,6},{8,9},{9,8},{10,11... | collective-permute-start | bytes 3145736 | tf_op jit(solution)/shard_map/ppermute | solution.py:125
  58.7 21.9 %copy-start.1 = (f32[512,256]{1,0:T(8,128)S(1)}, f32[512,256]{1,0:T(8,128)}, u32[]{:S(2)}) copy-start(f32[512,256]{1,0:T(8,128)} %matrix.3) | copy-start | bytes 1572868
  58.7 2.4 %collective-permute-start.17 = (f32[13,128,128]{2,1,0:T(8,128)S(1)}, f32[13,128,128]{2,1,0:T(8,128)S(1)}, u32[]{:S(2)}, u32[]{:S(2)}) collective-permute-start(f32[13,128,128]{2,1,0:T(8,128)S(1)} %pad_maximum_fusion.2), channel_id=1, source_target_pairs={{0,1},{1,0},{2,3},{3,2},{4,5},{5,4},{6,7},{7,6},{8,9},{9,8},{10,11... | collective-permute-start | bytes 2555912 | tf_op jit(solution)/shard_map/ppermute | solution.py:125
  74.8 5.8 %collective-permute-start.19 = (f32[17,16,128]{2,1,0:T(8,128)S(1)}, f32[17,16,128]{2,1,0:T(8,128)S(1)}, u32[]{:S(2)}, u32[]{:S(2)}) collective-permute-start(f32[17,16,128]{2,1,0:T(8,128)S(1)} %shard_map.47.mine), channel_id=1, source_target_pairs={{0,8},{1,9},{2,10},{3,11},{4,12},{5,13},{6,14},{7,15},{8,0},{9,1},... | collective-permute-start | bytes 417800 | tf_op jit(solution)/shard_map/ppermute | solution.py:125

commit v3 on v2

--- a/solution.py
+++ b/solution.py
@@ -118,25 +118,45 @@
 SIDE_A = involution(lambda r, c: (r, c ^ 2 if c % 2 == 0 else c ^ 4))
 SIDE_B = involution(lambda r, c: (r, c ^ 4 if c % 2 == 0 else c ^ 2))
 OUTER = involution(lambda r, c: (r ^ 1, c))
-MIDDLE = [(r * COLS + c, (3 - r) * COLS + c) for r in (1, 2) for c in range(COLS)]
+MIDDLE = involution(lambda r, c: (3 - r, c) if r in (1, 2) else (r, c ^ 1))
 
 
 def send(value, pairs):
     return lax.ppermute(value, AXES, pairs)
 
 
-GROUPS = ((0, 1, 2, 3), (4, 5, 8, 10), (6, 9, 12), (7, 11, 13, 14, 15))
+GROUPS = ((0, 1, 2, 4, 8), (3, 6, 10, 5, 9, 12), (14, 7, 11, 13), (15, 16))
 
 
 def gather(a, a5):
-    ua, ma, b, c = send(a5, OUTER), send(a5, MIDDLE), send(a, SIDE_A), send(a, SIDE_B)
-    e, ub, na, mc = send(b, SIDE_B), send(b, OUTER), send(ua, MIDDLE), send(ma, SIDE_B)
-    uc, mb = send(c, OUTER), send(b, MIDDLE)
-    na = jnp.concatenate([na[:4], (a5[4:] + ua[4:]) + (ma[4:] + na[4:])])
-    nb, nc = send(na, SIDE_A), send(na, SIDE_B)
-    ue, me, ne = send(e, OUTER), send(mb, SIDE_B), send(nb, SIDE_B)
-    own = (a, b, c, e, ua, ub, uc, ue, ma, mb, mc, me, na, nb, nc, ne)
-    return own, tuple(send(jnp.concatenate([own[i] for i in group]), TO_CORE) for group in GROUPS)
+    b = send(a, SIDE_A)
+    ua = send(a5, OUTER)
+    ma = send(a5, MIDDLE)
+    c = send(a, SIDE_B)
+    first_b = send(jnp.concatenate([b, ua[:4], ma[:4]]), SIDE_B)
+    na = send(ua, MIDDLE)
+    mb = send(ma[:4], SIDE_A)
+    ub = send(b, OUTER)
+    g0 = send(jnp.concatenate([a, b, c, ua, ma]), TO_CORE)
+    e = first_b[:4]
+    uc = first_b[4:8]
+    mc = first_b[8:]
+    tile = (a5[4:] + ua[4:]) + (ma[4:] + na[4:])
+    nb = send(ub, MIDDLE)
+    tile_a = send(tile, SIDE_A)
+    second_b = send(jnp.concatenate([na[:4], tile, ub, mb]), SIDE_B)
+    g1 = send(jnp.concatenate([e, uc, mc, ub, mb, na]), TO_CORE)
+    nc = second_b[:4]
+    tile_b = second_b[4:5]
+    ue = second_b[5:9]
+    me = second_b[9:]
+    third_b = send(jnp.concatenate([nb, tile_a]), SIDE_B)
+    ne = third_b[:4]
+    tiles = jnp.concatenate([tile, tile_a, tile_b, third_b[4:]])
+    g2 = send(jnp.concatenate([nc, ue, me, nb]), TO_CORE)
+    g3 = send(jnp.concatenate([ne, tiles]), TO_CORE)
+    own = (a, b, c, e, ua, ub, uc, ue, ma, mb, mc, me, na, nb, nc, ne, tiles)
+    return own, (g0, g1, g2, g3)
 
 
 def tile_place(big_r, delta):
@@ -145,9 +165,9 @@
 
 
 def panel_kernel(index, *refs):
-    own = refs[:16]
-    others = refs[16 : 16 + len(GROUPS)]
-    out, store, extra_store, v_all, w_all, p_all, rows, acc, sems = refs[16 + len(GROUPS) :]
+    own = refs[:17]
+    others = refs[17 : 17 + len(GROUPS)]
+    for_me, for_next, store, extra_store, v_all, w_all, p_all, rows, acc, radii, sems = refs[17 + len(GROUPS) :]
     r, c = index[0], index[1]
 
     def source_of(number, col):
@@ -165,17 +185,24 @@
         copies.append(
             pltpu.make_async_copy(source.at[pl.ds(start, 4)], store.at[from_col, d], sems.at[len(copies)])
         )
-        if number >= 12:
+
+    def load_extra(source, start, col):
+        for side in range(4):
+            _, from_col = source_of(side, col)
             copies.append(
-                pltpu.make_async_copy(source.at[start + 4], extra_store.at[from_col], sems.at[len(copies)])
+                pltpu.make_async_copy(source.at[start + side], extra_store.at[from_col], sems.at[len(copies)])
             )
 
     for number in range(16):
         load(own[number], 0, number, c)
+    load_extra(own[16], 0, c)
     for ref, group in zip(others, GROUPS):
         start = 0
         for number in group:
-            load(ref, start, number, c ^ 1)
+            if number == 16:
+                load_extra(ref, start, c ^ 1)
+            else:
+                load(ref, start, number, c ^ 1)
             start += own[number].shape[0]
     for copy in copies:
         copy.start()
@@ -194,7 +221,7 @@
         jnp.int32, (PANEL, TILE), 1
     )
     which = lax.broadcasted_iota(jnp.int32, (BLOCKS, PANEL, TILE), 1)
-    which_sub = lax.broadcasted_iota(jnp.int32, (PANEL, TILE), 0)
+    which_sub = lax.broadcasted_iota(jnp.int32, (1, TILE), 1)
 
     def total(x):
         return jnp.sum(jnp.sum(x, axis=0, keepdims=True), axis=1, keepdims=True)
@@ -208,7 +235,7 @@
     v_all[...] = jnp.zeros_like(v_all)
     w_all[...] = jnp.zeros_like(w_all)
     p_all[...] = rows[:, :PANEL, :]
-    out[BLOCKS] = jnp.zeros((2 * PANEL, TILE), jnp.float32)
+    radii[...] = jnp.zeros_like(radii)
 
     def multiply(vector):
         for big_c in range(BLOCKS):
@@ -258,12 +285,16 @@
         p_all[...] = panel
         v_all[...] = jnp.where(which == j, v3, refl)
         w_all[...] = jnp.where(which == j, w3, images)
-        out[BLOCKS, :PANEL, :] = jnp.where(which_sub == j, -radius, out[BLOCKS, :PANEL, :])
+        radii[...] = jnp.where(which_sub == j, -radius, radii[...])
         return jnp.sum(jnp.where(which == j + 1, panel, 0.0), axis=1)
 
     lax.fori_loop(0, PANEL, step, rows[:, 0, :])
-    out[:BLOCKS, :PANEL, :] = v_all[...]
-    out[:BLOCKS, PANEL:, :] = w_all[...]
+    for out, row in ((for_me, r), (for_next, r ^ 1)):
+        blocks = [k * ROWS + row for k in range(4)] + [m * COLS + c for m in range(2)]
+        for place, number in enumerate(blocks):
+            out[place, :PANEL, :] = v_all[number]
+            out[place, PANEL:, :] = w_all[number]
+        out[6] = jnp.broadcast_to(radii[...], (2 * PANEL, TILE))
 
 
 def reduce_panel(index, own, others):
@@ -271,9 +302,9 @@
     vmem = pl.BlockSpec(memory_space=pltpu.VMEM)
     return pl.pallas_call(
         panel_kernel,
-        out_shape=jax.ShapeDtypeStruct((BLOCKS + 1, 2 * PANEL, TILE), jnp.float32),
-        in_specs=[pl.BlockSpec(memory_space=pltpu.SMEM)] + [held] * (16 + len(others)),
-        out_specs=vmem,
+        out_shape=(jax.ShapeDtypeStruct((7, 2 * PANEL, TILE), jnp.float32),) * 2,
+        in_specs=[pl.BlockSpec(memory_space=pltpu.SMEM)] + [held] * (17 + len(others)),
+        out_specs=(vmem, vmem),
         scratch_shapes=[
             pltpu.VMEM((COLS, ROWS, 4, TILE, TILE), jnp.float32),
             pltpu.VMEM((HALF, TILE, TILE), jnp.float32),
@@ -282,6 +313,7 @@
             pltpu.VMEM((BLOCKS, PANEL, TILE), jnp.float32),
             pltpu.VMEM((BLOCKS, 2 * PANEL, TILE), jnp.float32),
             pltpu.VMEM((BLOCKS, 8, TILE), jnp.float32),
+            pltpu.VMEM((1, TILE), jnp.float32),
             pltpu.SemaphoreType.DMA((40,)),
         ],
         compiler_params=pltpu.CompilerParams(vmem_limit_bytes=24 * 1024 * 1024),
@@ -289,7 +321,7 @@
 
 
 def update_kernel(index, matrix, mine, theirs, updated, refl_rows, image_rows, subdiag, held):
-    r, c = index[0], index[1]
+    r = index[0]
 
     @pl.when(jnp.logical_or(r == 1, r == 2))
     def _():
@@ -301,11 +333,11 @@
 
     right = []
     for m in range(2):
-        both = held[m * COLS + c]
+        both = held[4 + m]
         right.append(jnp.concatenate([both[PANEL:], both[:PANEL]], axis=0))
     right = jnp.concatenate(right, axis=1)
     for k in range(4):
-        left = held[k * ROWS + r]
+        left = held[k]
         span = slice(k * TILE, (k + 1) * TILE)
         updated[span, :] = matrix[span, :] - lax.dot_general(
             left,
@@ -316,7 +348,7 @@
         )
         refl_rows[:, span] = left[:PANEL]
         image_rows[:, span] = left[PANEL:]
-    subdiag[...] = held[BLOCKS, :PANEL, :]
+    subdiag[...] = held[6, 0, :PANEL]
 
 
 def finish(index, matrix, mine, theirs):
@@ -328,7 +360,7 @@
             jax.ShapeDtypeStruct(matrix.shape, jnp.float32),
             jax.ShapeDtypeStruct((PANEL, rows), jnp.float32),
             jax.ShapeDtypeStruct((PANEL, rows), jnp.float32),
-            jax.ShapeDtypeStruct((PANEL, TILE), jnp.float32),
+            jax.ShapeDtypeStruct((PANEL,), jnp.float32),
         ),
         in_specs=[pl.BlockSpec(memory_space=pltpu.SMEM), vmem, vmem, vmem],
         out_specs=(vmem,) * 4,
@@ -340,10 +372,8 @@
 def gathered(matrix):
     index = jnp.stack([lax.axis_index("row"), lax.axis_index("col")]).astype(jnp.int32)
     own, others = gather(*pick(index, matrix))
-    mine = reduce_panel(index, own, others)
-    theirs = send(mine, OUTER)
-    updated, refl_rows, image_rows, subdiag = finish(index, matrix, mine, theirs)
-    return updated, refl_rows, image_rows, subdiag[:, 0]
+    mine, for_next = reduce_panel(index, own, others)
+    return tuple(finish(index, matrix, mine, send(for_next, OUTER)))
 
 
 def per_device(matrix):

time: 83.4 us -> 67.2 us (0.81)
  starting transfers between devices: 31.3 us -> 21.6 us
  waiting for transfers between devices: 32.7 us -> 26.4 us
    ppermute x20 -> x17, starting transfers between devices: 31.3 us -> 21.6 us  [send(): return lax.ppermute(value, AXES, pairs)]
    ppermute x20 -> x17, waiting for transfers between devices: 32.7 us -> 26.4 us  [send(): return lax.ppermute(value, AXES, pairs)]
  transfers between devices with their start and end apart: 20 -> 17, of which waited for: 7 -> 7; matrix products, arithmetic and copies ran while one was open for 0% -> 1% of each run, Pallas kernels for 0% -> 0%
where the time goes in v3:
time: 67.2 us; the launch traced here: 67 us
  waiting for transfers between devices  26.4 us (39%)
  starting transfers between devices  21.6 us (32%)
  Pallas kernels  16.3 us (24%)
  local copies, waits for them, and re-layouts  1.41 us (2%)
  between operations  0.85 us (1%)
    ppermute x17, waiting for transfers between devices, send(): return lax.ppermute(value, AXES, pairs)  26.4 us
    ppermute x17, starting transfers between devices, send(): return lax.ppermute(value, AXES, pairs)  21.6 us
    pallas_call x1, Pallas kernels, reduce_panel(): pl.pallas_call(panel_kernel, out_shape=(jax.ShapeDtypeStruct((7, 2 * PANE...  13.7 us
    pallas_call x1, Pallas kernels, finish(): pl.pallas_call(update_kernel, out_shape=(jax.ShapeDtypeStruct(matrix.shap...  1.97 us
  transfers between devices with their start and end apart: 17, of which 7 were waited for; matrix products, arithmetic and copies ran while one was open for 1% of the time, Pallas kernels for 0%

profile of v3, /device:TPU:0, one launch (start us, length us, event | category | flops | bytes accessed | tf_op | source)
XLA Modules:
  0.0 67.0 jit_solution(3341170691465010657)
XLA Ops:
  0.6 0.1 pad_add_fusion.index
  0.7 0.0 copy-start
  0.7 1.0 %copy-done = f32[512,256]{1,0:T(8,128)S(1)} copy-done((f32[512,256]{1,0:T(8,128)S(1)}, f32[512,256]{1,0:T(8,128)}, u32[]{:S(2)}) %copy-start) | copy-done | bytes 524312
  1.8 0.6 shard_map.46
  2.4 3.1 %collective-permute-start.2 = (f32[5,128,128]{2,1,0:T(8,128)S(1)}, f32[5,128,128]{2,1,0:T(8,128)S(1)}, u32[]{:S(2)}, u32[]{:S(2)}) collective-permute-start(f32[5,128,128]{2,1,0:T(8,128)S(1)} %get-tuple-element.9), channel_id=1, source_target_pairs={{0,8},{1,9},{2,10},{3,11},{4,12},{5,13},{6,14},{7,15},{8,0},{9,1},... | collective-permute-start | bytes 983048 | tf_op jit(solution)/shard_map/ppermute | solution.py:125
  5.4 1.5 %collective-permute-start = (f32[4,128,128]{2,1,0:T(8,128)S(1)}, f32[4,128,128]{2,1,0:T(8,128)S(1)}, u32[]{:S(2)}, u32[]{:S(2)}) collective-permute-start(f32[4,128,128]{2,1,0:T(8,128)S(1)} %get-tuple-element.8.refs_0_), channel_id=1, source_target_pairs={{0,2},{1,5},{2,0},{3,7},{4,6},{5,1},{6,4},{7,3},{8,10},{9,13},{10,... | collective-permute-start | bytes 786440 | tf_op jit(solution)/shard_map/ppermute | solution.py:125
  6.9 0.0 collective-permute-start.3
  6.9 1.5 %collective-permute-start.1 = (f32[4,128,128]{2,1,0:T(8,128)S(1)}, f32[4,128,128]{2,1,0:T(8,128)S(1)}, u32[]{:S(2)}, u32[]{:S(2)}) collective-permute-start(f32[4,128,128]{2,1,0:T(8,128)S(1)} %get-tuple-element.8.refs_0_), channel_id=1, source_target_pairs={{0,4},{1,3},{2,6},{3,1},{4,0},{5,7},{6,2},{7,5},{8,12},{9,11},{10,... | collective-permute-start | bytes 786440 | tf_op jit(solution)/shard_map/ppermute | solution.py:125
  8.5 5.1 %collective-permute-done.refs_1_ = f32[4,128,128]{2,1,0:T(8,128)S(1)} collective-permute-done((f32[4,128,128]{2,1,0:T(8,128)S(1)}, f32[4,128,128]{2,1,0:T(8,128)S(1)}, u32[]{:S(2)}, u32[]{:S(2)}) %collective-permute-start) | collective-permute-done | bytes 262176 | tf_op jit(solution)/shard_map/ppermute | solution.py:125
  13.6 0.0 collective-permute-start.5
  13.6 0.0 collective-permute-done.2.refs_4_
  13.6 0.0 collective-permute-start.6
  13.6 0.0 collective-permute-done.3.refs_8_
  13.7 2.5 %collective-permute-start.7 = (f32[4,128,128]{2,1,0:T(8,128)S(1)}, f32[4,128,128]{2,1,0:T(8,128)S(1)}, u32[]{:S(2)}, u32[]{:S(2)}) collective-permute-start(f32[4,128,128]{2,1,0:T(8,128)S(1)} %slice.71), channel_id=1, source_target_pairs={{0,2},{1,5},{2,0},{3,7},{4,6},{5,1},{6,4},{7,3},{8,10},{9,13},{10,... | collective-permute-start | bytes 786440 | tf_op jit(solution)/shard_map/ppermute | solution.py:125
  16.2 0.1 pad_maximum_fusion.3
  16.3 1.6 %collective-permute-start.4 = (f32[12,128,128]{2,1,0:T(8,128)S(1)}, f32[12,128,128]{2,1,0:T(8,128)S(1)}, u32[]{:S(2)}, u32[]{:S(2)}) collective-permute-start(f32[12,128,128]{2,1,0:T(8,128)S(1)} %pad_maximum_fusion.3), channel_id=1, source_target_pairs={{0,4},{1,3},{2,6},{3,1},{4,0},{5,7},{6,2},{7,5},{8,12},{9,11},{10,... | collective-permute-start | bytes 2359304 | tf_op jit(solution)/shard_map/ppermute | solution.py:125
  17.9 0.0 collective-permute-done.1.refs_2_
  17.9 2.1 %collective-permute-done.5.refs_5_ = f32[4,128,128]{2,1,0:T(8,128)S(1)} collective-permute-done((f32[4,128,128]{2,1,0:T(8,128)S(1)}, f32[4,128,128]{2,1,0:T(8,128)S(1)}, u32[]{:S(2)}, u32[]{:S(2)}) %collective-permute-start.5) | collective-permute-done | bytes 262176 | tf_op jit(solution)/shard_map/ppermute | solution.py:125
  20.0 0.0 collective-permute-start.9
  20.0 0.0 collective-permute-done.6.refs_12_
  20.0 2.5 %collective-permute-start.10 = (f32[1,128,128]{2,1,0:T(8,128)S(1)}, f32[1,128,128]{2,1,0:T(8,128)S(1)}, u32[]{:S(2)}, u32[]{:S(2)}) collective-permute-start(f32[1,128,128]{2,1,0:T(8,128)S(1)} %fusion), channel_id=1, source_target_pairs={{0,2},{1,5},{2,0},{3,7},{4,6},{5,1},{6,4},{7,3},{8,10},{9,13},{10,... | collective-permute-start | bytes 196616 | tf_op jit(solution)/shard_map/ppermute | solution.py:125
  22.5 0.0 collective-permute-done.7.refs_9_
  22.5 0.1 pad_maximum_fusion.2
  22.6 2.2 %collective-permute-start.8 = (f32[13,128,128]{2,1,0:T(8,128)S(1)}, f32[13,128,128]{2,1,0:T(8,128)S(1)}, u32[]{:S(2)}, u32[]{:S(2)}) collective-permute-start(f32[13,128,128]{2,1,0:T(8,128)S(1)} %pad_maximum_fusion.2), channel_id=1, source_target_pairs={{0,4},{1,3},{2,6},{3,1},{4,0},{5,7},{6,2},{7,5},{8,12},{9,11},{10,... | collective-permute-start | bytes 2555912 | tf_op jit(solution)/shard_map/ppermute | solution.py:125
  24.8 0.7 %collective-permute-done.10 = f32[1,128,128]{2,1,0:T(8,128)S(1)} collective-permute-done((f32[1,128,128]{2,1,0:T(8,128)S(1)}, f32[1,128,128]{2,1,0:T(8,128)S(1)}, u32[]{:S(2)}, u32[]{:S(2)}) %collective-permute-start.10) | collective-permute-done | bytes 65568 | tf_op jit(solution)/shard_map/ppermute | solution.py:125
  25.5 0.0 collective-permute-done.9.refs_13_
  25.5 1.6 %collective-permute-start.11 = (f32[5,128,128]{2,1,0:T(8,128)S(1)}, f32[5,128,128]{2,1,0:T(8,128)S(1)}, u32[]{:S(2)}, u32[]{:S(2)}) collective-permute-start(f32[5,128,128]{2,1,0:T(8,128)S(1)} %pad_maximum_fusion.4), channel_id=1, source_target_pairs={{0,4},{1,3},{2,6},{3,1},{4,0},{5,7},{6,2},{7,5},{8,12},{9,11},{10,... | collective-permute-start | bytes 983048 | tf_op jit(solution)/shard_map/ppermute | solution.py:125
  27.2 0.1 collective-permute-start.12
  27.3 1.8 %collective-permute-done.4 = f32[12,128,128]{2,1,0:T(8,128)S(1)} collective-permute-done((f32[12,128,128]{2,1,0:T(8,128)S(1)}, f32[12,128,128]{2,1,0:T(8,128)S(1)}, u32[]{:S(2)}, u32[]{:S(2)}) %collective-permute-start.4) | collective-permute-done | bytes 786464 | tf_op jit(solution)/shard_map/ppermute | solution.py:125
  29.0 0.1 pad_maximum_fusion
  29.1 0.8 %collective-permute-start.13 = (f32[25,128,128]{2,1,0:T(8,128)S(1)}, f32[25,128,128]{2,1,0:T(8,128)S(1)}, u32[]{:S(2)}, u32[]{:S(2)}) collective-permute-start(f32[25,128,128]{2,1,0:T(8,128)S(1)} %pad_maximum_fusion), channel_id=1, source_target_pairs={{0,1},{1,0},{2,3},{3,2},{4,5},{5,4},{6,7},{7,6},{8,9},{9,8},{10,11... | collective-permute-start | bytes 4915208 | tf_op jit(solution)/shard_map/ppermute | solution.py:125
  30.0 11.7 %collective-permute-done.11 = f32[5,128,128]{2,1,0:T(8,128)S(1)} collective-permute-done((f32[5,128,128]{2,1,0:T(8,128)S(1)}, f32[5,128,128]{2,1,0:T(8,128)S(1)}, u32[]{:S(2)}, u32[]{:S(2)}) %collective-permute-start.11) | collective-permute-done | bytes 327712 | tf_op jit(solution)/shard_map/ppermute | solution.py:125
  41.7 0.0 collective-permute-done.8
  41.8 0.1 fusion.1
  41.8 0.1 pad_maximum_fusion.1
  41.9 0.5 collective-permute-start.14
  42.5 0.1 collective-permute-start.15
  42.6 0.1 fusion.2
  42.7 0.0 collective-permute-done.12.refs_17_
  42.7 2.8 %collective-permute-done.15.refs_20_ = f32[8,128,128]{2,1,0:T(8,128)S(1)} collective-permute-done((f32[8,128,128]{2,1,0:T(8,128)S(1)}, f32[8,128,128]{2,1,0:T(8,128)S(1)}, u32[]{:S(2)}, u32[]{:S(2)}) %collective-permute-start.15) | collective-permute-done | bytes 524320 | tf_op jit(solution)/shard_map/ppermute | solution.py:125
  45.5 0.0 collective-permute-done.14.refs_19_
  45.5 0.0 collective-permute-done.13.refs_18_
  45.5 0.0 copy-start.1
  45.5 13.7 %shard_map.47 = (f32[7,16,128]{2,1,0:T(8,128)S(1)}, f32[7,16,128]{2,1,0:T(8,128)S(1)}) custom-call(s32[2]{0:T(128)S(1)} %pad_add_fusion.index, f32[4,128,128]{2,1,0:T(8,128)S(1)} %get-tuple-element.8.refs_0_, f32[4,128,128]{2,1,0:T(8,128)S(1)} %collective-permute-done.refs_1_, f32[4,128,128]{2,1,0:T(8,128)S(1)} %collective-permute-done.1.refs_2_, ...), custom_call_target="tpu_custom_call" | custom-call | tf_op jit(solution)/shard_map/pallas_call | solution.py:303
  59.2 3.6 %collective-permute-start.16 = (f32[7,16,128]{2,1,0:T(8,128)S(1)}, f32[7,16,128]{2,1,0:T(8,128)S(1)}, u32[]{:S(2)}, u32[]{:S(2)}) collective-permute-start(f32[7,16,128]{2,1,0:T(8,128)S(1)} %get-tuple-element.11), channel_id=1, source_target_pairs={{0,8},{1,9},{2,10},{3,11},{4,12},{5,13},{6,14},{7,15},{8,0},{9,1},... | collective-permute-start | bytes 172040 | tf_op jit(solution)/shard_map/ppermute | solution.py:125
  62.8 2.2 %collective-permute-done.16.theirs = f32[7,16,128]{2,1,0:T(8,128)S(1)} collective-permute-done((f32[7,16,128]{2,1,0:T(8,128)S(1)}, f32[7,16,128]{2,1,0:T(8,128)S(1)}, u32[]{:S(2)}, u32[]{:S(2)}) %collective-permute-start.16) | collective-permute-done | bytes 57376 | tf_op jit(solution)/shard_map/ppermute | solution.py:125
  65.0 0.0 copy-done.1
  65.0 2.0 %shard_map.48 = (f32[512,256]{1,0:T(8,128)}, f32[8,512]{1,0:T(8,128)}, f32[8,512]{1,0:T(8,128)}, f32[8]{0:T(128)}) custom-call(s32[2]{0:T(128)S(1)} %pad_add_fusion.index, f32[512,256]{1,0:T(8,128)S(1)} %copy-done.1, f32[7,16,128]{2,1,0:T(8,128)S(1)} %get-tuple-element.10.mine, f32[7,16,128]{2,1,0:T(8,128)S(1)} %collective-permute-done.16.theirs), custom_call_target="tpu_custom_call" | custom-call | tf_op jit(solution)/shard_map/pallas_call | solution.py:357
  (17 shorter events, 0.3 us)
Async XLA Ops:
  0.7 1.0 %copy-start = (f32[512,256]{1,0:T(8,128)S(1)}, f32[512,256]{1,0:T(8,128)}, u32[]{:S(2)}) copy-start(f32[512,256]{1,0:T(8,128)} %matrix.3) | copy-start | bytes 1572868
  2.4 11.2 %collective-permute-start.2 = (f32[5,128,128]{2,1,0:T(8,128)S(1)}, f32[5,128,128]{2,1,0:T(8,128)S(1)}, u32[]{:S(2)}, u32[]{:S(2)}) collective-permute-start(f32[5,128,128]{2,1,0:T(8,128)S(1)} %get-tuple-element.9), channel_id=1, source_target_pairs={{0,8},{1,9},{2,10},{3,11},{4,12},{5,13},{6,14},{7,15},{8,0},{9,1},... | collective-permute-start | bytes 983048 | tf_op jit(solution)/shard_map/ppermute | solution.py:125
  5.4 8.1 %collective-permute-start = (f32[4,128,128]{2,1,0:T(8,128)S(1)}, f32[4,128,128]{2,1,0:T(8,128)S(1)}, u32[]{:S(2)}, u32[]{:S(2)}) collective-permute-start(f32[4,128,128]{2,1,0:T(8,128)S(1)} %get-tuple-element.8.refs_0_), channel_id=1, source_target_pairs={{0,2},{1,5},{2,0},{3,7},{4,6},{5,1},{6,4},{7,3},{8,10},{9,13},{10,... | collective-permute-start | bytes 786440 | tf_op jit(solution)/shard_map/ppermute | solution.py:125
  6.9 6.7 %collective-permute-start.3 = (f32[5,128,128]{2,1,0:T(8,128)S(1)}, f32[5,128,128]{2,1,0:T(8,128)S(1)}, u32[]{:S(2)}, u32[]{:S(2)}) collective-permute-start(f32[5,128,128]{2,1,0:T(8,128)S(1)} %get-tuple-element.9), channel_id=1, source_target_pairs={{0,1},{1,0},{2,3},{3,2},{4,5},{5,4},{6,7},{7,6},{8,16},{9,17},{10,... | collective-permute-start | bytes 983048 | tf_op jit(solution)/shard_map/ppermute | solution.py:125
  6.9 10.9 %collective-permute-start.1 = (f32[4,128,128]{2,1,0:T(8,128)S(1)}, f32[4,128,128]{2,1,0:T(8,128)S(1)}, u32[]{:S(2)}, u32[]{:S(2)}) collective-permute-start(f32[4,128,128]{2,1,0:T(8,128)S(1)} %get-tuple-element.8.refs_0_), channel_id=1, source_target_pairs={{0,4},{1,3},{2,6},{3,1},{4,0},{5,7},{6,2},{7,5},{8,12},{9,11},{10,... | collective-permute-start | bytes 786440 | tf_op jit(solution)/shard_map/ppermute | solution.py:125
  13.6 6.4 %collective-permute-start.5 = (f32[4,128,128]{2,1,0:T(8,128)S(1)}, f32[4,128,128]{2,1,0:T(8,128)S(1)}, u32[]{:S(2)}, u32[]{:S(2)}) collective-permute-start(f32[4,128,128]{2,1,0:T(8,128)S(1)} %collective-permute-done.refs_1_), channel_id=1, source_target_pairs={{0,8},{1,9},{2,10},{3,11},{4,12},{5,13},{6,14},{7,15},{8,0},{9,1},... | collective-permute-start | bytes 786440 | tf_op jit(solution)/shard_map/ppermute | solution.py:125
  13.6 6.4 %collective-permute-start.6 = (f32[5,128,128]{2,1,0:T(8,128)S(1)}, f32[5,128,128]{2,1,0:T(8,128)S(1)}, u32[]{:S(2)}, u32[]{:S(2)}) collective-permute-start(f32[5,128,128]{2,1,0:T(8,128)S(1)} %collective-permute-done.2.refs_4_), channel_id=1, source_target_pairs={{0,1},{1,0},{2,3},{3,2},{4,5},{5,4},{6,7},{7,6},{8,16},{9,17},{10,... | collective-permute-start | bytes 983048 | tf_op jit(solution)/shard_map/ppermute | solution.py:125
  13.7 8.9 %collective-permute-start.7 = (f32[4,128,128]{2,1,0:T(8,128)S(1)}, f32[4,128,128]{2,1,0:T(8,128)S(1)}, u32[]{:S(2)}, u32[]{:S(2)}) collective-permute-start(f32[4,128,128]{2,1,0:T(8,128)S(1)} %slice.71), channel_id=1, source_target_pairs={{0,2},{1,5},{2,0},{3,7},{4,6},{5,1},{6,4},{7,3},{8,10},{9,13},{10,... | collective-permute-start | bytes 786440 | tf_op jit(solution)/shard_map/ppermute | solution.py:125
  16.3 12.8 %collective-permute-start.4 = (f32[12,128,128]{2,1,0:T(8,128)S(1)}, f32[12,128,128]{2,1,0:T(8,128)S(1)}, u32[]{:S(2)}, u32[]{:S(2)}) collective-permute-start(f32[12,128,128]{2,1,0:T(8,128)S(1)} %pad_maximum_fusion.3), channel_id=1, source_target_pairs={{0,4},{1,3},{2,6},{3,1},{4,0},{5,7},{6,2},{7,5},{8,12},{9,11},{10,... | collective-permute-start | bytes 2359304 | tf_op jit(solution)/shard_map/ppermute | solution.py:125
  20.0 5.6 %collective-permute-start.9 = (f32[4,128,128]{2,1,0:T(8,128)S(1)}, f32[4,128,128]{2,1,0:T(8,128)S(1)}, u32[]{:S(2)}, u32[]{:S(2)}) collective-permute-start(f32[4,128,128]{2,1,0:T(8,128)S(1)} %collective-permute-done.5.refs_5_), channel_id=1, source_target_pairs={{0,1},{1,0},{2,3},{3,2},{4,5},{5,4},{6,7},{7,6},{8,16},{9,17},{10,... | collective-permute-start | bytes 786440 | tf_op jit(solution)/shard_map/ppermute | solution.py:125
  20.0 5.5 %collective-permute-start.10 = (f32[1,128,128]{2,1,0:T(8,128)S(1)}, f32[1,128,128]{2,1,0:T(8,128)S(1)}, u32[]{:S(2)}, u32[]{:S(2)}) collective-permute-start(f32[1,128,128]{2,1,0:T(8,128)S(1)} %fusion), channel_id=1, source_target_pairs={{0,2},{1,5},{2,0},{3,7},{4,6},{5,1},{6,4},{7,3},{8,10},{9,13},{10,... | collective-permute-start | bytes 196616 | tf_op jit(solution)/shard_map/ppermute | solution.py:125
  22.6 19.1 %collective-permute-start.8 = (f32[13,128,128]{2,1,0:T(8,128)S(1)}, f32[13,128,128]{2,1,0:T(8,128)S(1)}, u32[]{:S(2)}, u32[]{:S(2)}) collective-permute-start(f32[13,128,128]{2,1,0:T(8,128)S(1)} %pad_maximum_fusion.2), channel_id=1, source_target_pairs={{0,4},{1,3},{2,6},{3,1},{4,0},{5,7},{6,2},{7,5},{8,12},{9,11},{10,... | collective-permute-start | bytes 2555912 | tf_op jit(solution)/shard_map/ppermute | solution.py:125
  25.5 16.1 %collective-permute-start.11 = (f32[5,128,128]{2,1,0:T(8,128)S(1)}, f32[5,128,128]{2,1,0:T(8,128)S(1)}, u32[]{:S(2)}, u32[]{:S(2)}) collective-permute-start(f32[5,128,128]{2,1,0:T(8,128)S(1)} %pad_maximum_fusion.4), channel_id=1, source_target_pairs={{0,4},{1,3},{2,6},{3,1},{4,0},{5,7},{6,2},{7,5},{8,12},{9,11},{10,... | collective-permute-start | bytes 983048 | tf_op jit(solution)/shard_map/ppermute | solution.py:125
  27.2 15.5 %collective-permute-start.12 = (f32[22,128,128]{2,1,0:T(8,128)S(1)}, f32[22,128,128]{2,1,0:T(8,128)S(1)}, u32[]{:S(2)}, u32[]{:S(2)}) collective-permute-start(f32[22,128,128]{2,1,0:T(8,128)S(1)} %constant_dynamic-update-slice_fusion), channel_id=1, source_target_pairs={{0,1},{1,0},{2,3},{3,2},{4,5},{5,4},{6,7},{7,6},{8,9},{9,8},{10,11... | collective-permute-start | bytes 4325384 | tf_op jit(solution)/shard_map/ppermute | solution.py:125
  29.1 16.3 %collective-permute-start.13 = (f32[25,128,128]{2,1,0:T(8,128)S(1)}, f32[25,128,128]{2,1,0:T(8,128)S(1)}, u32[]{:S(2)}, u32[]{:S(2)}) collective-permute-start(f32[25,128,128]{2,1,0:T(8,128)S(1)} %pad_maximum_fusion), channel_id=1, source_target_pairs={{0,1},{1,0},{2,3},{3,2},{4,5},{5,4},{6,7},{7,6},{8,9},{9,8},{10,11... | collective-permute-start | bytes 4915208 | tf_op jit(solution)/shard_map/ppermute | solution.py:125
  41.9 3.6 %collective-permute-start.14 = (f32[16,128,128]{2,1,0:T(8,128)S(1)}, f32[16,128,128]{2,1,0:T(8,128)S(1)}, u32[]{:S(2)}, u32[]{:S(2)}) collective-permute-start(f32[16,128,128]{2,1,0:T(8,128)S(1)} %pad_maximum_fusion.1), channel_id=1, source_target_pairs={{0,1},{1,0},{2,3},{3,2},{4,5},{5,4},{6,7},{7,6},{8,9},{9,8},{10,11... | collective-permute-start | bytes 3145736 | tf_op jit(solution)/shard_map/ppermute | solution.py:125
  42.5 3.0 %collective-permute-start.15 = (f32[8,128,128]{2,1,0:T(8,128)S(1)}, f32[8,128,128]{2,1,0:T(8,128)S(1)}, u32[]{:S(2)}, u32[]{:S(2)}) collective-permute-start(f32[8,128,128]{2,1,0:T(8,128)S(1)} %get-tuple-element.20), channel_id=1, source_target_pairs={{0,1},{1,0},{2,3},{3,2},{4,5},{5,4},{6,7},{7,6},{8,9},{9,8},{10,11... | collective-permute-start | bytes 1572872 | tf_op jit(solution)/shard_map/ppermute | solution.py:125
  45.5 19.5 %copy-start.1 = (f32[512,256]{1,0:T(8,128)S(1)}, f32[512,256]{1,0:T(8,128)}, u32[]{:S(2)}) copy-start(f32[512,256]{1,0:T(8,128)} %matrix.3) | copy-start | bytes 1572868
  59.2 5.8 %collective-permute-start.16 = (f32[7,16,128]{2,1,0:T(8,128)S(1)}, f32[7,16,128]{2,1,0:T(8,128)S(1)}, u32[]{:S(2)}, u32[]{:S(2)}) collective-permute-start(f32[7,16,128]{2,1,0:T(8,128)S(1)} %get-tuple-element.11), channel_id=1, source_target_pairs={{0,8},{1,9},{2,10},{3,11},{4,12},{5,13},{6,14},{7,15},{8,0},{9,1},... | collective-permute-start | bytes 172040 | tf_op jit(solution)/shard_map/ppermute | solution.py:125

commit v4 on v3

--- a/solution.py
+++ b/solution.py
@@ -135,26 +135,37 @@
     c = send(a, SIDE_B)
     first_b = send(jnp.concatenate([b, ua[:4], ma[:4]]), SIDE_B)
     na = send(ua, MIDDLE)
-    mb = send(ma[:4], SIDE_A)
-    ub = send(b, OUTER)
-    g0 = send(jnp.concatenate([a, b, c, ua, ma]), TO_CORE)
+    held, b = lax.optimization_barrier((ma[:4], b))
+    mb = send(held, SIDE_A)
+    held, ua = lax.optimization_barrier((b, ua))
+    ub = send(held, OUTER)
+    held, ma = lax.optimization_barrier((jnp.concatenate([a, b, c, ua, ma]), ma))
+    g0 = send(held, TO_CORE)
     e = first_b[:4]
     uc = first_b[4:8]
     mc = first_b[8:]
     tile = (a5[4:] + ua[4:]) + (ma[4:] + na[4:])
-    nb = send(ub, MIDDLE)
-    tile_a = send(tile, SIDE_A)
-    second_b = send(jnp.concatenate([na[:4], tile, ub, mb]), SIDE_B)
-    g1 = send(jnp.concatenate([e, uc, mc, ub, mb, na]), TO_CORE)
+    held, c = lax.optimization_barrier((ub, c))
+    nb = send(held, MIDDLE)
+    held, first_b = lax.optimization_barrier((e, first_b))
+    ue = send(held, OUTER)
+    held, na = lax.optimization_barrier((tile, na))
+    tile_a = send(held, SIDE_A)
+    held, mb = lax.optimization_barrier((jnp.concatenate([na[:4], tile, mb]), mb))
+    second_b = send(held, SIDE_B)
+    held, ub = lax.optimization_barrier((jnp.concatenate([e, uc, mc, ub, mb, na]), ub))
+    g1 = send(held, TO_CORE)
     nc = second_b[:4]
     tile_b = second_b[4:5]
-    ue = second_b[5:9]
-    me = second_b[9:]
-    third_b = send(jnp.concatenate([nb, tile_a]), SIDE_B)
+    me = second_b[5:]
+    held, g0 = lax.optimization_barrier((jnp.concatenate([nb, tile_a]), g0))
+    third_b = send(held, SIDE_B)
     ne = third_b[:4]
     tiles = jnp.concatenate([tile, tile_a, tile_b, third_b[4:]])
-    g2 = send(jnp.concatenate([nc, ue, me, nb]), TO_CORE)
-    g3 = send(jnp.concatenate([ne, tiles]), TO_CORE)
+    held, nb = lax.optimization_barrier((jnp.concatenate([nc, ue, me, nb]), nb))
+    g2 = send(held, TO_CORE)
+    held, ue = lax.optimization_barrier((jnp.concatenate([ne, tiles]), ue))
+    g3 = send(held, TO_CORE)
     own = (a, b, c, e, ua, ub, uc, ue, ma, mb, mc, me, na, nb, nc, ne, tiles)
     return own, (g0, g1, g2, g3)
 
@@ -193,8 +204,6 @@
                 pltpu.make_async_copy(source.at[start + side], extra_store.at[from_col], sems.at[len(copies)])
             )
 
-    for number in range(16):
-        load(own[number], 0, number, c)
     load_extra(own[16], 0, c)
     for ref, group in zip(others, GROUPS):
         start = 0
@@ -206,6 +215,9 @@
             start += own[number].shape[0]
     for copy in copies:
         copy.start()
+    for number in range(16):
+        row, from_col = source_of(number, c)
+        store[from_col, lax.rem(row - from_col + COLS, ROWS)] = own[number][:4]
     for copy in copies:
         copy.wait()
 
@@ -288,7 +300,8 @@
         radii[...] = jnp.where(which_sub == j, -radius, radii[...])
         return jnp.sum(jnp.where(which == j + 1, panel, 0.0), axis=1)
 
-    lax.fori_loop(0, PANEL, step, rows[:, 0, :])
+    steps = jnp.where(jnp.logical_or(r == 1, r == 2), PANEL, 0)
+    lax.fori_loop(0, steps, step, rows[:, 0, :])
     for out, row in ((for_me, r), (for_next, r ^ 1)):
         blocks = [k * ROWS + row for k in range(4)] + [m * COLS + c for m in range(2)]
         for place, number in enumerate(blocks):

time: 67.2 us -> 64.6 us (0.961)
  Pallas kernels: 16.3 us -> 5.14 us
  starting transfers between devices: 21.6 us -> 31.3 us
  waiting for transfers between devices: 26.4 us -> 25.4 us
    pallas_call x1, Pallas kernels: 13.7 us -> 2.57 us  [reduce_panel(): pl.pallas_call(panel_kernel, out_shape=(jax.ShapeDtypeStruct((7, 2 * PANE...]
    ppermute x17 -> x18, starting transfers between devices: 21.6 us -> 31.3 us  [send(): return lax.ppermute(value, AXES, pairs)]
    ppermute x17 -> x18, waiting for transfers between devices: 26.4 us -> 25.4 us  [send(): return lax.ppermute(value, AXES, pairs)]
  transfers between devices with their start and end apart: 17 -> 18, of which waited for: 7 -> 11; matrix products, arithmetic and copies ran while one was open for 1% -> 1% of each run, Pallas kernels for 0% -> 0%
where the time goes in v4:
time: 64.6 us; the launch traced here: 64.4 us
  starting transfers between devices  31.3 us (48%)
  waiting for transfers between devices  25.4 us (39%)
  Pallas kernels  5.14 us (8%)
  local copies, waits for them, and re-layouts  1.36 us (2%)
  between operations  0.86 us (1%)
    ppermute x18, starting transfers between devices, send(): return lax.ppermute(value, AXES, pairs)  31.3 us
    ppermute x18, waiting for transfers between devices, send(): return lax.ppermute(value, AXES, pairs)  25.4 us
    pallas_call x1, Pallas kernels, reduce_panel(): pl.pallas_call(panel_kernel, out_shape=(jax.ShapeDtypeStruct((7, 2 * PANE...  2.57 us
    pallas_call x1, Pallas kernels, finish(): pl.pallas_call(update_kernel, out_shape=(jax.ShapeDtypeStruct(matrix.shap...  1.97 us
  transfers between devices with their start and end apart: 18, of which 11 were waited for; matrix products, arithmetic and copies ran while one was open for 1% of the time, Pallas kernels for 0%

profile of v4, /device:TPU:0, one launch (start us, length us, event | category | flops | bytes accessed | tf_op | source)
XLA Modules:
  0.0 64.4 jit_solution(802899656075062976)
XLA Ops:
  0.6 0.1 pad_add_fusion.index
  0.7 0.0 copy-start
  0.7 1.0 %copy-done = f32[512,256]{1,0:T(8,128)S(1)} copy-done((f32[512,256]{1,0:T(8,128)S(1)}, f32[512,256]{1,0:T(8,128)}, u32[]{:S(2)}) %copy-start) | copy-done | bytes 524312
  1.8 0.6 shard_map.46
  2.4 0.5 collective-permute-start
  2.9 4.1 %collective-permute-start.2 = (f32[5,128,128]{2,1,0:T(8,128)S(1)}, f32[5,128,128]{2,1,0:T(8,128)S(1)}, u32[]{:S(2)}, u32[]{:S(2)}) collective-permute-start(f32[5,128,128]{2,1,0:T(8,128)S(1)} %get-tuple-element.30), channel_id=1, source_target_pairs={{0,8},{1,9},{2,10},{3,11},{4,12},{5,13},{6,14},{7,15},{8,0},{9,1},... | collective-permute-start | bytes 983048 | tf_op jit(solution)/shard_map/ppermute | solution.py:125
  7.0 1.5 %collective-permute-start.1 = (f32[4,128,128]{2,1,0:T(8,128)S(1)}, f32[4,128,128]{2,1,0:T(8,128)S(1)}, u32[]{:S(2)}, u32[]{:S(2)}) collective-permute-start(f32[4,128,128]{2,1,0:T(8,128)S(1)} %get-tuple-element.29.refs_0_), channel_id=1, source_target_pairs={{0,2},{1,5},{2,0},{3,7},{4,6},{5,1},{6,4},{7,3},{8,10},{9,13},{10,... | collective-permute-start | bytes 786440 | tf_op jit(solution)/shard_map/ppermute | solution.py:125
  8.5 1.5 %collective-permute-start.4 = (f32[4,128,128]{2,1,0:T(8,128)S(1)}, f32[4,128,128]{2,1,0:T(8,128)S(1)}, u32[]{:S(2)}, u32[]{:S(2)}) collective-permute-start(f32[4,128,128]{2,1,0:T(8,128)S(1)} %get-tuple-element.29.refs_0_), channel_id=1, source_target_pairs={{0,4},{1,3},{2,6},{3,1},{4,0},{5,7},{6,2},{7,5},{8,12},{9,11},{10,... | collective-permute-start | bytes 786440 | tf_op jit(solution)/shard_map/ppermute | solution.py:125
  10.1 0.0 collective-permute-done.refs_8_
  10.1 5.7 %collective-permute-done.1.refs_1_ = f32[4,128,128]{2,1,0:T(8,128)S(1)} collective-permute-done((f32[4,128,128]{2,1,0:T(8,128)S(1)}, f32[4,128,128]{2,1,0:T(8,128)S(1)}, u32[]{:S(2)}, u32[]{:S(2)}) %collective-permute-start.1) | collective-permute-done | bytes 262176 | tf_op jit(solution)/shard_map/ppermute | solution.py:125
  15.7 0.0 collective-permute-done.2.refs_4_
  15.8 0.0 collective-permute-done.4.refs_2_
  15.9 0.1 collective-permute-start.10
  16.0 0.5 collective-permute-start.3
  16.5 0.2 collective-permute-start.6
  16.7 0.1 pad_maximum_fusion.2
  16.8 1.6 %collective-permute-start.5 = (f32[12,128,128]{2,1,0:T(8,128)S(1)}, f32[12,128,128]{2,1,0:T(8,128)S(1)}, u32[]{:S(2)}, u32[]{:S(2)}) collective-permute-start(f32[12,128,128]{2,1,0:T(8,128)S(1)} %pad_maximum_fusion.2), channel_id=1, source_target_pairs={{0,4},{1,3},{2,6},{3,1},{4,0},{5,7},{6,2},{7,5},{8,12},{9,11},{10,... | collective-permute-start | bytes 2359304 | tf_op jit(solution)/shard_map/ppermute | solution.py:125
  18.4 1.5 %collective-permute-start.7 = (f32[4,128,128]{2,1,0:T(8,128)S(1)}, f32[4,128,128]{2,1,0:T(8,128)S(1)}, u32[]{:S(2)}, u32[]{:S(2)}) collective-permute-start(f32[4,128,128]{2,1,0:T(8,128)S(1)} %slice.62), channel_id=1, source_target_pairs={{0,2},{1,5},{2,0},{3,7},{4,6},{5,1},{6,4},{7,3},{8,10},{9,13},{10,... | collective-permute-start | bytes 786440 | tf_op jit(solution)/shard_map/ppermute | solution.py:125
  19.9 4.8 %collective-permute-done.3.refs_5_ = f32[4,128,128]{2,1,0:T(8,128)S(1)} collective-permute-done((f32[4,128,128]{2,1,0:T(8,128)S(1)}, f32[4,128,128]{2,1,0:T(8,128)S(1)}, u32[]{:S(2)}, u32[]{:S(2)}) %collective-permute-start.3) | collective-permute-done | bytes 262176 | tf_op jit(solution)/shard_map/ppermute | solution.py:125
  24.7 0.0 collective-permute-start.8
  24.7 0.0 collective-permute-done.6.refs_12_
  24.7 1.6 %collective-permute-start.9 = (f32[1,128,128]{2,1,0:T(8,128)S(1)}, f32[1,128,128]{2,1,0:T(8,128)S(1)}, u32[]{:S(2)}, u32[]{:S(2)}) collective-permute-start(f32[1,128,128]{2,1,0:T(8,128)S(1)} %fusion), channel_id=1, source_target_pairs={{0,2},{1,5},{2,0},{3,7},{4,6},{5,1},{6,4},{7,3},{8,10},{9,13},{10,... | collective-permute-start | bytes 196616 | tf_op jit(solution)/shard_map/ppermute | solution.py:125
  26.3 1.3 %collective-permute-done.7.refs_9_ = f32[4,128,128]{2,1,0:T(8,128)S(1)} collective-permute-done((f32[4,128,128]{2,1,0:T(8,128)S(1)}, f32[4,128,128]{2,1,0:T(8,128)S(1)}, u32[]{:S(2)}, u32[]{:S(2)}) %collective-permute-start.7) | collective-permute-done | bytes 262176 | tf_op jit(solution)/shard_map/ppermute | solution.py:125
  27.7 0.5 collective-permute-start.12
  28.2 1.6 %collective-permute-done.9 = f32[1,128,128]{2,1,0:T(8,128)S(1)} collective-permute-done((f32[1,128,128]{2,1,0:T(8,128)S(1)}, f32[1,128,128]{2,1,0:T(8,128)S(1)}, u32[]{:S(2)}, u32[]{:S(2)}) %collective-permute-start.9) | collective-permute-done | bytes 65568 | tf_op jit(solution)/shard_map/ppermute | solution.py:125
  29.8 0.0 collective-permute-done.8.refs_13_
  29.8 2.5 %collective-permute-done.5 = f32[12,128,128]{2,1,0:T(8,128)S(1)} collective-permute-done((f32[12,128,128]{2,1,0:T(8,128)S(1)}, f32[12,128,128]{2,1,0:T(8,128)S(1)}, u32[]{:S(2)}, u32[]{:S(2)}) %collective-permute-start.5) | collective-permute-done | bytes 786464 | tf_op jit(solution)/shard_map/ppermute | solution.py:125
  32.3 0.1 fusion.1
  32.4 2.4 %collective-permute-start.13 = (f32[4,128,128]{2,1,0:T(8,128)S(1)}, f32[4,128,128]{2,1,0:T(8,128)S(1)}, u32[]{:S(2)}, u32[]{:S(2)}) collective-permute-start(f32[4,128,128]{2,1,0:T(8,128)S(1)} %get-tuple-element.45.refs_3_), channel_id=1, source_target_pairs={{0,8},{1,9},{2,10},{3,11},{4,12},{5,13},{6,14},{7,15},{8,0},{9,1},... | collective-permute-start | bytes 786440 | tf_op jit(solution)/shard_map/ppermute | solution.py:125
  34.8 0.1 pad_maximum_fusion
  35.0 0.1 collective-permute-start.14
  35.0 0.0 collective-permute-done.10.refs_17_
  35.0 1.6 %collective-permute-start.11 = (f32[5,128,128]{2,1,0:T(8,128)S(1)}, f32[5,128,128]{2,1,0:T(8,128)S(1)}, u32[]{:S(2)}, u32[]{:S(2)}) collective-permute-start(f32[5,128,128]{2,1,0:T(8,128)S(1)} %pad_maximum_fusion.4), channel_id=1, source_target_pairs={{0,4},{1,3},{2,6},{3,1},{4,0},{5,7},{6,2},{7,5},{8,12},{9,11},{10,... | collective-permute-start | bytes 983048 | tf_op jit(solution)/shard_map/ppermute | solution.py:125
  36.6 2.0 %collective-permute-done.12 = f32[9,128,128]{2,1,0:T(8,128)S(1)} collective-permute-done((f32[9,128,128]{2,1,0:T(8,128)S(1)}, f32[9,128,128]{2,1,0:T(8,128)S(1)}, u32[]{:S(2)}, u32[]{:S(2)}) %collective-permute-start.12) | collective-permute-done | bytes 589856 | tf_op jit(solution)/shard_map/ppermute | solution.py:125
  38.7 1.6 %collective-permute-done.13.refs_7_ = f32[4,128,128]{2,1,0:T(8,128)S(1)} collective-permute-done((f32[4,128,128]{2,1,0:T(8,128)S(1)}, f32[4,128,128]{2,1,0:T(8,128)S(1)}, u32[]{:S(2)}, u32[]{:S(2)}) %collective-permute-start.13) | collective-permute-done | bytes 262176 | tf_op jit(solution)/shard_map/ppermute | solution.py:125
  40.3 0.1 pad_maximum_fusion.1
  40.4 0.1 collective-permute-start.15
  40.5 1.7 %collective-permute-done.11 = f32[5,128,128]{2,1,0:T(8,128)S(1)} collective-permute-done((f32[5,128,128]{2,1,0:T(8,128)S(1)}, f32[5,128,128]{2,1,0:T(8,128)S(1)}, u32[]{:S(2)}, u32[]{:S(2)}) %collective-permute-start.11) | collective-permute-done | bytes 327712 | tf_op jit(solution)/shard_map/ppermute | solution.py:125
  42.3 0.1 collective-permute-start.16
  42.4 0.8 %collective-permute-done.15.refs_19_ = f32[16,128,128]{2,1,0:T(8,128)S(1)} collective-permute-done((f32[16,128,128]{2,1,0:T(8,128)S(1)}, f32[16,128,128]{2,1,0:T(8,128)S(1)}, u32[]{:S(2)}, u32[]{:S(2)}) %collective-permute-start.15) | collective-permute-done | bytes 1048608 | tf_op jit(solution)/shard_map/ppermute | solution.py:125
  43.2 1.1 %collective-permute-done.16.refs_20_ = f32[8,128,128]{2,1,0:T(8,128)S(1)} collective-permute-done((f32[8,128,128]{2,1,0:T(8,128)S(1)}, f32[8,128,128]{2,1,0:T(8,128)S(1)}, u32[]{:S(2)}, u32[]{:S(2)}) %collective-permute-start.16) | collective-permute-done | bytes 524320 | tf_op jit(solution)/shard_map/ppermute | solution.py:125
  44.3 0.0 collective-permute-done.14.refs_18_
  44.3 0.0 copy-start.1
  44.3 2.6 %shard_map.47 = (f32[7,16,128]{2,1,0:T(8,128)S(1)}, f32[7,16,128]{2,1,0:T(8,128)S(1)}) custom-call(s32[2]{0:T(128)S(1)} %pad_add_fusion.index, f32[4,128,128]{2,1,0:T(8,128)S(1)} %get-tuple-element.29.refs_0_, f32[4,128,128]{2,1,0:T(8,128)S(1)} %collective-permute-done.1.refs_1_, f32[4,128,128]{2,1,0:T(8,128)S(1)} %collective-permute-done.4.refs_2_, ...), custom_call_target="tpu_custom_call" | custom-call | tf_op jit(solution)/shard_map/pallas_call | solution.py:316
  46.9 13.4 %collective-permute-start.17 = (f32[7,16,128]{2,1,0:T(8,128)S(1)}, f32[7,16,128]{2,1,0:T(8,128)S(1)}, u32[]{:S(2)}, u32[]{:S(2)}) collective-permute-start(f32[7,16,128]{2,1,0:T(8,128)S(1)} %get-tuple-element.53), channel_id=1, source_target_pairs={{0,8},{1,9},{2,10},{3,11},{4,12},{5,13},{6,14},{7,15},{8,0},{9,1},... | collective-permute-start | bytes 172040 | tf_op jit(solution)/shard_map/ppermute | solution.py:125
  60.2 2.2 %collective-permute-done.17.theirs = f32[7,16,128]{2,1,0:T(8,128)S(1)} collective-permute-done((f32[7,16,128]{2,1,0:T(8,128)S(1)}, f32[7,16,128]{2,1,0:T(8,128)S(1)}, u32[]{:S(2)}, u32[]{:S(2)}) %collective-permute-start.17) | collective-permute-done | bytes 57376 | tf_op jit(solution)/shard_map/ppermute | solution.py:125
  62.4 0.0 copy-done.1
  62.5 2.0 %shard_map.48 = (f32[512,256]{1,0:T(8,128)}, f32[8,512]{1,0:T(8,128)}, f32[8,512]{1,0:T(8,128)}, f32[8]{0:T(128)}) custom-call(s32[2]{0:T(128)S(1)} %pad_add_fusion.index, f32[512,256]{1,0:T(8,128)S(1)} %copy-done.1, f32[7,16,128]{2,1,0:T(8,128)S(1)} %get-tuple-element.52.mine, f32[7,16,128]{2,1,0:T(8,128)S(1)} %collective-permute-done.17.theirs), custom_call_target="tpu_custom_call" | custom-call | tf_op jit(solution)/shard_map/pallas_call | solution.py:370
  (18 shorter events, 0.4 us)
Async XLA Ops:
  0.7 1.0 %copy-start = (f32[512,256]{1,0:T(8,128)S(1)}, f32[512,256]{1,0:T(8,128)}, u32[]{:S(2)}) copy-start(f32[512,256]{1,0:T(8,128)} %matrix.3) | copy-start | bytes 1572868
  2.4 7.7 %collective-permute-start = (f32[5,128,128]{2,1,0:T(8,128)S(1)}, f32[5,128,128]{2,1,0:T(8,128)S(1)}, u32[]{:S(2)}, u32[]{:S(2)}) collective-permute-start(f32[5,128,128]{2,1,0:T(8,128)S(1)} %get-tuple-element.30), channel_id=1, source_target_pairs={{0,1},{1,0},{2,3},{3,2},{4,5},{5,4},{6,7},{7,6},{8,16},{9,17},{10,... | collective-permute-start | bytes 983048 | tf_op jit(solution)/shard_map/ppermute | solution.py:125
  2.9 12.9 %collective-permute-start.2 = (f32[5,128,128]{2,1,0:T(8,128)S(1)}, f32[5,128,128]{2,1,0:T(8,128)S(1)}, u32[]{:S(2)}, u32[]{:S(2)}) collective-permute-start(f32[5,128,128]{2,1,0:T(8,128)S(1)} %get-tuple-element.30), channel_id=1, source_target_pairs={{0,8},{1,9},{2,10},{3,11},{4,12},{5,13},{6,14},{7,15},{8,0},{9,1},... | collective-permute-start | bytes 983048 | tf_op jit(solution)/shard_map/ppermute | solution.py:125
  7.0 8.7 %collective-permute-start.1 = (f32[4,128,128]{2,1,0:T(8,128)S(1)}, f32[4,128,128]{2,1,0:T(8,128)S(1)}, u32[]{:S(2)}, u32[]{:S(2)}) collective-permute-start(f32[4,128,128]{2,1,0:T(8,128)S(1)} %get-tuple-element.29.refs_0_), channel_id=1, source_target_pairs={{0,2},{1,5},{2,0},{3,7},{4,6},{5,1},{6,4},{7,3},{8,10},{9,13},{10,... | collective-permute-start | bytes 786440 | tf_op jit(solution)/shard_map/ppermute | solution.py:125
  8.5 7.3 %collective-permute-start.4 = (f32[4,128,128]{2,1,0:T(8,128)S(1)}, f32[4,128,128]{2,1,0:T(8,128)S(1)}, u32[]{:S(2)}, u32[]{:S(2)}) collective-permute-start(f32[4,128,128]{2,1,0:T(8,128)S(1)} %get-tuple-element.29.refs_0_), channel_id=1, source_target_pairs={{0,4},{1,3},{2,6},{3,1},{4,0},{5,7},{6,2},{7,5},{8,12},{9,11},{10,... | collective-permute-start | bytes 786440 | tf_op jit(solution)/shard_map/ppermute | solution.py:125
  15.9 19.2 %collective-permute-start.10 = (f32[22,128,128]{2,1,0:T(8,128)S(1)}, f32[22,128,128]{2,1,0:T(8,128)S(1)}, u32[]{:S(2)}, u32[]{:S(2)}) collective-permute-start(f32[22,128,128]{2,1,0:T(8,128)S(1)} %constant_dynamic-update-slice_fusion), channel_id=1, source_target_pairs={{0,1},{1,0},{2,3},{3,2},{4,5},{5,4},{6,7},{7,6},{8,9},{9,8},{10,11... | collective-permute-start | bytes 4325384 | tf_op jit(solution)/shard_map/ppermute | solution.py:125
  16.0 8.7 %collective-permute-start.3 = (f32[4,128,128]{2,1,0:T(8,128)S(1)}, f32[4,128,128]{2,1,0:T(8,128)S(1)}, u32[]{:S(2)}, u32[]{:S(2)}) collective-permute-start(f32[4,128,128]{2,1,0:T(8,128)S(1)} %collective-permute-done.1.refs_1_), channel_id=1, source_target_pairs={{0,8},{1,9},{2,10},{3,11},{4,12},{5,13},{6,14},{7,15},{8,0},{9,1},... | collective-permute-start | bytes 786440 | tf_op jit(solution)/shard_map/ppermute | solution.py:125
  16.5 8.2 %collective-permute-start.6 = (f32[5,128,128]{2,1,0:T(8,128)S(1)}, f32[5,128,128]{2,1,0:T(8,128)S(1)}, u32[]{:S(2)}, u32[]{:S(2)}) collective-permute-start(f32[5,128,128]{2,1,0:T(8,128)S(1)} %collective-permute-done.2.refs_4_), channel_id=1, source_target_pairs={{0,1},{1,0},{2,3},{3,2},{4,5},{5,4},{6,7},{7,6},{8,16},{9,17},{10,... | collective-permute-start | bytes 983048 | tf_op jit(solution)/shard_map/ppermute | solution.py:125
  16.8 15.6 %collective-permute-start.5 = (f32[12,128,128]{2,1,0:T(8,128)S(1)}, f32[12,128,128]{2,1,0:T(8,128)S(1)}, u32[]{:S(2)}, u32[]{:S(2)}) collective-permute-start(f32[12,128,128]{2,1,0:T(8,128)S(1)} %pad_maximum_fusion.2), channel_id=1, source_target_pairs={{0,4},{1,3},{2,6},{3,1},{4,0},{5,7},{6,2},{7,5},{8,12},{9,11},{10,... | collective-permute-start | bytes 2359304 | tf_op jit(solution)/shard_map/ppermute | solution.py:125
  18.4 9.2 %collective-permute-start.7 = (f32[4,128,128]{2,1,0:T(8,128)S(1)}, f32[4,128,128]{2,1,0:T(8,128)S(1)}, u32[]{:S(2)}, u32[]{:S(2)}) collective-permute-start(f32[4,128,128]{2,1,0:T(8,128)S(1)} %slice.62), channel_id=1, source_target_pairs={{0,2},{1,5},{2,0},{3,7},{4,6},{5,1},{6,4},{7,3},{8,10},{9,13},{10,... | collective-permute-start | bytes 786440 | tf_op jit(solution)/shard_map/ppermute | solution.py:125
  24.7 5.1 %collective-permute-start.8 = (f32[4,128,128]{2,1,0:T(8,128)S(1)}, f32[4,128,128]{2,1,0:T(8,128)S(1)}, u32[]{:S(2)}, u32[]{:S(2)}) collective-permute-start(f32[4,128,128]{2,1,0:T(8,128)S(1)} %collective-permute-done.3.refs_5_), channel_id=1, source_target_pairs={{0,1},{1,0},{2,3},{3,2},{4,5},{5,4},{6,7},{7,6},{8,16},{9,17},{10,... | collective-permute-start | bytes 786440 | tf_op jit(solution)/shard_map/ppermute | solution.py:125
  24.7 5.1 %collective-permute-start.9 = (f32[1,128,128]{2,1,0:T(8,128)S(1)}, f32[1,128,128]{2,1,0:T(8,128)S(1)}, u32[]{:S(2)}, u32[]{:S(2)}) collective-permute-start(f32[1,128,128]{2,1,0:T(8,128)S(1)} %fusion), channel_id=1, source_target_pairs={{0,2},{1,5},{2,0},{3,7},{4,6},{5,1},{6,4},{7,3},{8,10},{9,13},{10,... | collective-permute-start | bytes 196616 | tf_op jit(solution)/shard_map/ppermute | solution.py:125
  27.7 11.0 %collective-permute-start.12 = (f32[9,128,128]{2,1,0:T(8,128)S(1)}, f32[9,128,128]{2,1,0:T(8,128)S(1)}, u32[]{:S(2)}, u32[]{:S(2)}) collective-permute-start(f32[9,128,128]{2,1,0:T(8,128)S(1)} %pad_maximum_fusion.3), channel_id=1, source_target_pairs={{0,4},{1,3},{2,6},{3,1},{4,0},{5,7},{6,2},{7,5},{8,12},{9,11},{10,... | collective-permute-start | bytes 1769480 | tf_op jit(solution)/shard_map/ppermute | solution.py:125
  32.4 7.9 %collective-permute-start.13 = (f32[4,128,128]{2,1,0:T(8,128)S(1)}, f32[4,128,128]{2,1,0:T(8,128)S(1)}, u32[]{:S(2)}, u32[]{:S(2)}) collective-permute-start(f32[4,128,128]{2,1,0:T(8,128)S(1)} %get-tuple-element.45.refs_3_), channel_id=1, source_target_pairs={{0,8},{1,9},{2,10},{3,11},{4,12},{5,13},{6,14},{7,15},{8,0},{9,1},... | collective-permute-start | bytes 786440 | tf_op jit(solution)/shard_map/ppermute | solution.py:125
  35.0 9.3 %collective-permute-start.14 = (f32[25,128,128]{2,1,0:T(8,128)S(1)}, f32[25,128,128]{2,1,0:T(8,128)S(1)}, u32[]{:S(2)}, u32[]{:S(2)}) collective-permute-start(f32[25,128,128]{2,1,0:T(8,128)S(1)} %pad_maximum_fusion), channel_id=1, source_target_pairs={{0,1},{1,0},{2,3},{3,2},{4,5},{5,4},{6,7},{7,6},{8,9},{9,8},{10,11... | collective-permute-start | bytes 4915208 | tf_op jit(solution)/shard_map/ppermute | solution.py:125
  35.0 7.1 %collective-permute-start.11 = (f32[5,128,128]{2,1,0:T(8,128)S(1)}, f32[5,128,128]{2,1,0:T(8,128)S(1)}, u32[]{:S(2)}, u32[]{:S(2)}) collective-permute-start(f32[5,128,128]{2,1,0:T(8,128)S(1)} %pad_maximum_fusion.4), channel_id=1, source_target_pairs={{0,4},{1,3},{2,6},{3,1},{4,0},{5,7},{6,2},{7,5},{8,12},{9,11},{10,... | collective-permute-start | bytes 983048 | tf_op jit(solution)/shard_map/ppermute | solution.py:125
  40.4 2.7 %collective-permute-start.15 = (f32[16,128,128]{2,1,0:T(8,128)S(1)}, f32[16,128,128]{2,1,0:T(8,128)S(1)}, u32[]{:S(2)}, u32[]{:S(2)}) collective-permute-start(f32[16,128,128]{2,1,0:T(8,128)S(1)} %pad_maximum_fusion.1), channel_id=1, source_target_pairs={{0,1},{1,0},{2,3},{3,2},{4,5},{5,4},{6,7},{7,6},{8,9},{9,8},{10,11... | collective-permute-start | bytes 3145736 | tf_op jit(solution)/shard_map/ppermute | solution.py:125
  42.3 2.0 %collective-permute-start.16 = (f32[8,128,128]{2,1,0:T(8,128)S(1)}, f32[8,128,128]{2,1,0:T(8,128)S(1)}, u32[]{:S(2)}, u32[]{:S(2)}) collective-permute-start(f32[8,128,128]{2,1,0:T(8,128)S(1)} %get-tuple-element.51), channel_id=1, source_target_pairs={{0,1},{1,0},{2,3},{3,2},{4,5},{5,4},{6,7},{7,6},{8,9},{9,8},{10,11... | collective-permute-start | bytes 1572872 | tf_op jit(solution)/shard_map/ppermute | solution.py:125
  44.3 18.2 %copy-start.1 = (f32[512,256]{1,0:T(8,128)S(1)}, f32[512,256]{1,0:T(8,128)}, u32[]{:S(2)}) copy-start(f32[512,256]{1,0:T(8,128)} %matrix.3) | copy-start | bytes 1572868
  46.9 15.6 %collective-permute-start.17 = (f32[7,16,128]{2,1,0:T(8,128)S(1)}, f32[7,16,128]{2,1,0:T(8,128)S(1)}, u32[]{:S(2)}, u32[]{:S(2)}) collective-permute-start(f32[7,16,128]{2,1,0:T(8,128)S(1)} %get-tuple-element.53), channel_id=1, source_target_pairs={{0,8},{1,9},{2,10},{3,11},{4,12},{5,13},{6,14},{7,15},{8,0},{9,1},... | collective-permute-start | bytes 172040 | tf_op jit(solution)/shard_map/ppermute | solution.py:125

commit v5 on v4

--- a/solution.py
+++ b/solution.py
@@ -79,24 +79,29 @@
     return (updated, refl_rows, image_rows, jnp.stack(subdiag_list))
 
 
-def pick_kernel(index, matrix, block, block_extra):
-    r, c = index[0], index[1]
+def pick_kernel(matrix, block, block_extra, sems):
+    r, c = lax.axis_index("row"), lax.axis_index("col")
     d = lax.rem(r - c + COLS, ROWS)
     first = (c + d) // ROWS
 
     def tile(k, m):
         start = pl.multiple_of(lax.rem(k, ROWS) * TILE, TILE)
-        return matrix[pl.ds(start, TILE), m * TILE : (m + 1) * TILE]
-
+        return matrix.at[pl.ds(start, TILE), m * TILE : (m + 1) * TILE]
+
+    copies = []
     for m in range(2):
         for s in range(2):
-            value = tile(first + 2 * m + s, m)
-            block[2 * m + s] = value
-            block_extra[2 * m + s] = value
-    block_extra[4] = jnp.where(d == 0, tile(first + 2, 0), 0.0)
-
-
-def pick(index, matrix):
+            copies.append(pltpu.make_async_copy(tile(first + 2 * m + s, m), block.at[2 * m + s], sems.at[2 * m + s]))
+    copies.append(pltpu.make_async_copy(tile(first + 2, 0), block_extra.at[4], sems.at[4]))
+    for copy in copies:
+        copy.start()
+    for copy in copies:
+        copy.wait()
+    block_extra[:4] = block[...]
+    block_extra[4] = jnp.where(d == 0, block_extra[4], 0.0)
+
+
+def pick(matrix):
     vmem = pl.BlockSpec(memory_space=pltpu.VMEM)
     return pl.pallas_call(
         pick_kernel,
@@ -104,10 +109,11 @@
             jax.ShapeDtypeStruct((4, TILE, TILE), jnp.float32),
             jax.ShapeDtypeStruct((5, TILE, TILE), jnp.float32),
         ),
-        in_specs=[pl.BlockSpec(memory_space=pltpu.SMEM), vmem],
+        in_specs=[pl.BlockSpec(memory_space=pltpu.HBM)],
         out_specs=(vmem, vmem),
+        scratch_shapes=[pltpu.SemaphoreType.DMA((5,))],
         compiler_params=pltpu.CompilerParams(vmem_limit_bytes=4 * 1024 * 1024),
-    )(index, matrix)
+    )(matrix)
 
 
 def involution(move):
@@ -175,11 +181,11 @@
     return big_c % COLS, delta % 4, 2 * (big_c // COLS) + delta // 4
 
 
-def panel_kernel(index, *refs):
+def panel_kernel(*refs):
     own = refs[:17]
     others = refs[17 : 17 + len(GROUPS)]
     for_me, for_next, store, extra_store, v_all, w_all, p_all, rows, acc, radii, sems = refs[17 + len(GROUPS) :]
-    r, c = index[0], index[1]
+    r, c = lax.axis_index("row"), lax.axis_index("col")
 
     def source_of(number, col):
         z, side = number // 4, number % 4
@@ -310,13 +316,13 @@
         out[6] = jnp.broadcast_to(radii[...], (2 * PANEL, TILE))
 
 
-def reduce_panel(index, own, others):
+def reduce_panel(own, others):
     held = pl.BlockSpec(memory_space=pltpu.VMEM)
     vmem = pl.BlockSpec(memory_space=pltpu.VMEM)
     return pl.pallas_call(
         panel_kernel,
         out_shape=(jax.ShapeDtypeStruct((7, 2 * PANEL, TILE), jnp.float32),) * 2,
-        in_specs=[pl.BlockSpec(memory_space=pltpu.SMEM)] + [held] * (17 + len(others)),
+        in_specs=[held] * (17 + len(others)),
         out_specs=(vmem, vmem),
         scratch_shapes=[
             pltpu.VMEM((COLS, ROWS, 4, TILE, TILE), jnp.float32),
@@ -330,11 +336,11 @@
             pltpu.SemaphoreType.DMA((40,)),
         ],
         compiler_params=pltpu.CompilerParams(vmem_limit_bytes=24 * 1024 * 1024),
-    )(index, *own, *others)
-
-
-def update_kernel(index, matrix, mine, theirs, updated, refl_rows, image_rows, subdiag, held):
-    r = index[0]
+    )(*own, *others)
+
+
+def update_kernel(matrix, mine, theirs, updated, refl_rows, image_rows, subdiag, held):
+    r = lax.axis_index("row")
 
     @pl.when(jnp.logical_or(r == 1, r == 2))
     def _():
@@ -364,7 +370,7 @@
     subdiag[...] = held[6, 0, :PANEL]
 
 
-def finish(index, matrix, mine, theirs):
+def finish(matrix, mine, theirs):
     vmem = pl.BlockSpec(memory_space=pltpu.VMEM)
     rows, _ = matrix.shape
     return pl.pallas_call(
@@ -375,18 +381,17 @@
             jax.ShapeDtypeStruct((PANEL, rows), jnp.float32),
             jax.ShapeDtypeStruct((PANEL,), jnp.float32),
         ),
-        in_specs=[pl.BlockSpec(memory_space=pltpu.SMEM), vmem, vmem, vmem],
+        in_specs=[vmem, vmem, vmem],
         out_specs=(vmem,) * 4,
         scratch_shapes=[pltpu.VMEM(mine.shape, jnp.float32)],
         compiler_params=pltpu.CompilerParams(vmem_limit_bytes=6 * 1024 * 1024),
-    )(index, matrix, mine, theirs)
+    )(matrix, mine, theirs)
 
 
 def gathered(matrix):
-    index = jnp.stack([lax.axis_index("row"), lax.axis_index("col")]).astype(jnp.int32)
-    own, others = gather(*pick(index, matrix))
-    mine, for_next = reduce_panel(index, own, others)
-    return tuple(finish(index, matrix, mine, send(for_next, OUTER)))
+    own, others = gather(*pick(matrix))
+    mine, for_next = reduce_panel(own, others)
+    return tuple(finish(matrix, mine, send(for_next, OUTER)))
 
 
 def per_device(matrix):

time: 64.6 us -> 62.9 us (0.974)
  Pallas kernels: 5.14 us -> 3.49 us
where the time goes in v5:
time: 62.9 us; the launch traced here: 62.7 us
  starting transfers between devices  31.3 us (50%)
  waiting for transfers between devices  25.4 us (40%)
  Pallas kernels  3.49 us (6%)
  local copies, waits for them, and re-layouts  1.36 us (2%)
  between operations  0.86 us (1%)
    ppermute x18, starting transfers between devices, send(): return lax.ppermute(value, AXES, pairs)  31.3 us
    ppermute x18, waiting for transfers between devices, send(): return lax.ppermute(value, AXES, pairs)  25.4 us
    pallas_call x1, Pallas kernels, reduce_panel(): pl.pallas_call(panel_kernel, out_shape=(jax.ShapeDtypeStruct((7, 2 * PANE...  1.97 us
    pallas_call x1, Pallas kernels, finish(): pl.pallas_call(update_kernel, out_shape=(jax.ShapeDtypeStruct(matrix.shap...  1.42 us
  transfers between devices with their start and end apart: 18, of which 11 were waited for; matrix products, arithmetic and copies ran while one was open for 1% of the time, Pallas kernels for 0%

profile of v5, /device:TPU:0, one launch (start us, length us, event | category | flops | bytes accessed | tf_op | source)
XLA Modules:
  0.0 62.7 jit_solution(518620466154984228)
XLA Ops:
  0.6 0.0 copy-start
  0.6 1.0 %copy-done = f32[512,256]{1,0:T(8,128)S(1)} copy-done((f32[512,256]{1,0:T(8,128)S(1)}, f32[512,256]{1,0:T(8,128)}, u32[]{:S(2)}) %copy-start) | copy-done | bytes 524312
  1.7 0.1 shard_map.46
  1.8 0.5 collective-permute-start
  2.3 4.1 %collective-permute-start.2 = (f32[5,128,128]{2,1,0:T(8,128)S(1)}, f32[5,128,128]{2,1,0:T(8,128)S(1)}, u32[]{:S(2)}, u32[]{:S(2)}) collective-permute-start(f32[5,128,128]{2,1,0:T(8,128)S(1)} %get-tuple-element.30), channel_id=1, source_target_pairs={{0,8},{1,9},{2,10},{3,11},{4,12},{5,13},{6,14},{7,15},{8,0},{9,1},... | collective-permute-start | bytes 983048 | tf_op jit(solution)/shard_map/ppermute | solution.py:131
  6.5 1.5 %collective-permute-start.1 = (f32[4,128,128]{2,1,0:T(8,128)S(1)}, f32[4,128,128]{2,1,0:T(8,128)S(1)}, u32[]{:S(2)}, u32[]{:S(2)}) collective-permute-start(f32[4,128,128]{2,1,0:T(8,128)S(1)} %get-tuple-element.29.refs_0_), channel_id=1, source_target_pairs={{0,2},{1,5},{2,0},{3,7},{4,6},{5,1},{6,4},{7,3},{8,10},{9,13},{10,... | collective-permute-start | bytes 786440 | tf_op jit(solution)/shard_map/ppermute | solution.py:131
  7.9 1.5 %collective-permute-start.4 = (f32[4,128,128]{2,1,0:T(8,128)S(1)}, f32[4,128,128]{2,1,0:T(8,128)S(1)}, u32[]{:S(2)}, u32[]{:S(2)}) collective-permute-start(f32[4,128,128]{2,1,0:T(8,128)S(1)} %get-tuple-element.29.refs_0_), channel_id=1, source_target_pairs={{0,4},{1,3},{2,6},{3,1},{4,0},{5,7},{6,2},{7,5},{8,12},{9,11},{10,... | collective-permute-start | bytes 786440 | tf_op jit(solution)/shard_map/ppermute | solution.py:131
  9.5 0.0 collective-permute-done.refs_8_
  9.5 5.7 %collective-permute-done.1.refs_1_ = f32[4,128,128]{2,1,0:T(8,128)S(1)} collective-permute-done((f32[4,128,128]{2,1,0:T(8,128)S(1)}, f32[4,128,128]{2,1,0:T(8,128)S(1)}, u32[]{:S(2)}, u32[]{:S(2)}) %collective-permute-start.1) | collective-permute-done | bytes 262176 | tf_op jit(solution)/shard_map/ppermute | solution.py:131
  15.2 0.0 collective-permute-done.2.refs_4_
  15.2 0.0 collective-permute-done.4.refs_2_
  15.3 0.1 collective-permute-start.10
  15.4 0.5 collective-permute-start.3
  15.9 0.2 collective-permute-start.6
  16.1 0.1 pad_maximum_fusion.2
  16.2 1.6 %collective-permute-start.5 = (f32[12,128,128]{2,1,0:T(8,128)S(1)}, f32[12,128,128]{2,1,0:T(8,128)S(1)}, u32[]{:S(2)}, u32[]{:S(2)}) collective-permute-start(f32[12,128,128]{2,1,0:T(8,128)S(1)} %pad_maximum_fusion.2), channel_id=1, source_target_pairs={{0,4},{1,3},{2,6},{3,1},{4,0},{5,7},{6,2},{7,5},{8,12},{9,11},{10,... | collective-permute-start | bytes 2359304 | tf_op jit(solution)/shard_map/ppermute | solution.py:131
  17.8 1.5 %collective-permute-start.7 = (f32[4,128,128]{2,1,0:T(8,128)S(1)}, f32[4,128,128]{2,1,0:T(8,128)S(1)}, u32[]{:S(2)}, u32[]{:S(2)}) collective-permute-start(f32[4,128,128]{2,1,0:T(8,128)S(1)} %slice.62), channel_id=1, source_target_pairs={{0,2},{1,5},{2,0},{3,7},{4,6},{5,1},{6,4},{7,3},{8,10},{9,13},{10,... | collective-permute-start | bytes 786440 | tf_op jit(solution)/shard_map/ppermute | solution.py:131
  19.3 4.8 %collective-permute-done.3.refs_5_ = f32[4,128,128]{2,1,0:T(8,128)S(1)} collective-permute-done((f32[4,128,128]{2,1,0:T(8,128)S(1)}, f32[4,128,128]{2,1,0:T(8,128)S(1)}, u32[]{:S(2)}, u32[]{:S(2)}) %collective-permute-start.3) | collective-permute-done | bytes 262176 | tf_op jit(solution)/shard_map/ppermute | solution.py:131
  24.1 0.0 collective-permute-start.8
  24.1 0.0 collective-permute-done.6.refs_12_
  24.1 1.6 %collective-permute-start.9 = (f32[1,128,128]{2,1,0:T(8,128)S(1)}, f32[1,128,128]{2,1,0:T(8,128)S(1)}, u32[]{:S(2)}, u32[]{:S(2)}) collective-permute-start(f32[1,128,128]{2,1,0:T(8,128)S(1)} %fusion), channel_id=1, source_target_pairs={{0,2},{1,5},{2,0},{3,7},{4,6},{5,1},{6,4},{7,3},{8,10},{9,13},{10,... | collective-permute-start | bytes 196616 | tf_op jit(solution)/shard_map/ppermute | solution.py:131
  25.7 1.3 %collective-permute-done.7.refs_9_ = f32[4,128,128]{2,1,0:T(8,128)S(1)} collective-permute-done((f32[4,128,128]{2,1,0:T(8,128)S(1)}, f32[4,128,128]{2,1,0:T(8,128)S(1)}, u32[]{:S(2)}, u32[]{:S(2)}) %collective-permute-start.7) | collective-permute-done | bytes 262176 | tf_op jit(solution)/shard_map/ppermute | solution.py:131
  27.1 0.5 collective-permute-start.12
  27.6 1.6 %collective-permute-done.9 = f32[1,128,128]{2,1,0:T(8,128)S(1)} collective-permute-done((f32[1,128,128]{2,1,0:T(8,128)S(1)}, f32[1,128,128]{2,1,0:T(8,128)S(1)}, u32[]{:S(2)}, u32[]{:S(2)}) %collective-permute-start.9) | collective-permute-done | bytes 65568 | tf_op jit(solution)/shard_map/ppermute | solution.py:131
  29.2 0.0 collective-permute-done.8.refs_13_
  29.3 2.5 %collective-permute-done.5 = f32[12,128,128]{2,1,0:T(8,128)S(1)} collective-permute-done((f32[12,128,128]{2,1,0:T(8,128)S(1)}, f32[12,128,128]{2,1,0:T(8,128)S(1)}, u32[]{:S(2)}, u32[]{:S(2)}) %collective-permute-start.5) | collective-permute-done | bytes 786464 | tf_op jit(solution)/shard_map/ppermute | solution.py:131
  31.8 0.1 fusion.1
  31.8 2.4 %collective-permute-start.13 = (f32[4,128,128]{2,1,0:T(8,128)S(1)}, f32[4,128,128]{2,1,0:T(8,128)S(1)}, u32[]{:S(2)}, u32[]{:S(2)}) collective-permute-start(f32[4,128,128]{2,1,0:T(8,128)S(1)} %get-tuple-element.45.refs_3_), channel_id=1, source_target_pairs={{0,8},{1,9},{2,10},{3,11},{4,12},{5,13},{6,14},{7,15},{8,0},{9,1},... | collective-permute-start | bytes 786440 | tf_op jit(solution)/shard_map/ppermute | solution.py:131
  34.3 0.1 pad_maximum_fusion
  34.4 0.1 collective-permute-start.14
  34.5 0.0 collective-permute-done.10.refs_17_
  34.5 1.6 %collective-permute-start.11 = (f32[5,128,128]{2,1,0:T(8,128)S(1)}, f32[5,128,128]{2,1,0:T(8,128)S(1)}, u32[]{:S(2)}, u32[]{:S(2)}) collective-permute-start(f32[5,128,128]{2,1,0:T(8,128)S(1)} %pad_maximum_fusion.4), channel_id=1, source_target_pairs={{0,4},{1,3},{2,6},{3,1},{4,0},{5,7},{6,2},{7,5},{8,12},{9,11},{10,... | collective-permute-start | bytes 983048 | tf_op jit(solution)/shard_map/ppermute | solution.py:131
  36.1 2.0 %collective-permute-done.12 = f32[9,128,128]{2,1,0:T(8,128)S(1)} collective-permute-done((f32[9,128,128]{2,1,0:T(8,128)S(1)}, f32[9,128,128]{2,1,0:T(8,128)S(1)}, u32[]{:S(2)}, u32[]{:S(2)}) %collective-permute-start.12) | collective-permute-done | bytes 589856 | tf_op jit(solution)/shard_map/ppermute | solution.py:131
  38.1 1.6 %collective-permute-done.13.refs_7_ = f32[4,128,128]{2,1,0:T(8,128)S(1)} collective-permute-done((f32[4,128,128]{2,1,0:T(8,128)S(1)}, f32[4,128,128]{2,1,0:T(8,128)S(1)}, u32[]{:S(2)}, u32[]{:S(2)}) %collective-permute-start.13) | collective-permute-done | bytes 262176 | tf_op jit(solution)/shard_map/ppermute | solution.py:131
  39.8 0.1 pad_maximum_fusion.1
  39.9 0.1 collective-permute-start.15
  40.0 1.7 %collective-permute-done.11 = f32[5,128,128]{2,1,0:T(8,128)S(1)} collective-permute-done((f32[5,128,128]{2,1,0:T(8,128)S(1)}, f32[5,128,128]{2,1,0:T(8,128)S(1)}, u32[]{:S(2)}, u32[]{:S(2)}) %collective-permute-start.11) | collective-permute-done | bytes 327712 | tf_op jit(solution)/shard_map/ppermute | solution.py:131
  41.7 0.1 collective-permute-start.16
  41.8 0.8 %collective-permute-done.15.refs_19_ = f32[16,128,128]{2,1,0:T(8,128)S(1)} collective-permute-done((f32[16,128,128]{2,1,0:T(8,128)S(1)}, f32[16,128,128]{2,1,0:T(8,128)S(1)}, u32[]{:S(2)}, u32[]{:S(2)}) %collective-permute-start.15) | collective-permute-done | bytes 1048608 | tf_op jit(solution)/shard_map/ppermute | solution.py:131
  42.6 1.1 %collective-permute-done.16.refs_20_ = f32[8,128,128]{2,1,0:T(8,128)S(1)} collective-permute-done((f32[8,128,128]{2,1,0:T(8,128)S(1)}, f32[8,128,128]{2,1,0:T(8,128)S(1)}, u32[]{:S(2)}, u32[]{:S(2)}) %collective-permute-start.16) | collective-permute-done | bytes 524320 | tf_op jit(solution)/shard_map/ppermute | solution.py:131
  43.7 0.0 collective-permute-done.14.refs_18_
  43.7 0.0 copy-start.1
  43.7 2.0 %shard_map.47 = (f32[7,16,128]{2,1,0:T(8,128)S(1)}, f32[7,16,128]{2,1,0:T(8,128)S(1)}) custom-call(f32[4,128,128]{2,1,0:T(8,128)S(1)} %get-tuple-element.29.refs_0_, f32[4,128,128]{2,1,0:T(8,128)S(1)} %collective-permute-done.1.refs_1_, f32[4,128,128]{2,1,0:T(8,128)S(1)} %collective-permute-done.4.refs_2_, f32[4,128,128]{2,1,0:T(8,128)S(1)} %get-tuple-element.45.refs_3_, ...), custom_call_target="tpu_custom_call" | custom-call | tf_op jit(solution)/shard_map/pallas_call | solution.py:322
  45.7 13.4 %collective-permute-start.17 = (f32[7,16,128]{2,1,0:T(8,128)S(1)}, f32[7,16,128]{2,1,0:T(8,128)S(1)}, u32[]{:S(2)}, u32[]{:S(2)}) collective-permute-start(f32[7,16,128]{2,1,0:T(8,128)S(1)} %get-tuple-element.53), channel_id=1, source_target_pairs={{0,8},{1,9},{2,10},{3,11},{4,12},{5,13},{6,14},{7,15},{8,0},{9,1},... | collective-permute-start | bytes 172040 | tf_op jit(solution)/shard_map/ppermute | solution.py:131
  59.1 2.2 %collective-permute-done.17.theirs = f32[7,16,128]{2,1,0:T(8,128)S(1)} collective-permute-done((f32[7,16,128]{2,1,0:T(8,128)S(1)}, f32[7,16,128]{2,1,0:T(8,128)S(1)}, u32[]{:S(2)}, u32[]{:S(2)}) %collective-permute-start.17) | collective-permute-done | bytes 57376 | tf_op jit(solution)/shard_map/ppermute | solution.py:131
  61.3 0.0 copy-done.1
  61.3 1.4 %shard_map.48 = (f32[512,256]{1,0:T(8,128)}, f32[8,512]{1,0:T(8,128)}, f32[8,512]{1,0:T(8,128)}, f32[8]{0:T(128)}) custom-call(f32[512,256]{1,0:T(8,128)S(1)} %copy-done.1, f32[7,16,128]{2,1,0:T(8,128)S(1)} %get-tuple-element.52.mine, f32[7,16,128]{2,1,0:T(8,128)S(1)} %collective-permute-done.17.theirs), custom_call_target="tpu_custom_call" | custom-call | tf_op jit(solution)/shard_map/pallas_call | solution.py:376
  (18 shorter events, 0.4 us)
Async XLA Ops:
  0.6 1.0 %copy-start = (f32[512,256]{1,0:T(8,128)S(1)}, f32[512,256]{1,0:T(8,128)}, u32[]{:S(2)}) copy-start(f32[512,256]{1,0:T(8,128)} %matrix.3) | copy-start | bytes 1572868
  1.8 7.7 %collective-permute-start = (f32[5,128,128]{2,1,0:T(8,128)S(1)}, f32[5,128,128]{2,1,0:T(8,128)S(1)}, u32[]{:S(2)}, u32[]{:S(2)}) collective-permute-start(f32[5,128,128]{2,1,0:T(8,128)S(1)} %get-tuple-element.30), channel_id=1, source_target_pairs={{0,1},{1,0},{2,3},{3,2},{4,5},{5,4},{6,7},{7,6},{8,16},{9,17},{10,... | collective-permute-start | bytes 983048 | tf_op jit(solution)/shard_map/ppermute | solution.py:131
  2.3 12.9 %collective-permute-start.2 = (f32[5,128,128]{2,1,0:T(8,128)S(1)}, f32[5,128,128]{2,1,0:T(8,128)S(1)}, u32[]{:S(2)}, u32[]{:S(2)}) collective-permute-start(f32[5,128,128]{2,1,0:T(8,128)S(1)} %get-tuple-element.30), channel_id=1, source_target_pairs={{0,8},{1,9},{2,10},{3,11},{4,12},{5,13},{6,14},{7,15},{8,0},{9,1},... | collective-permute-start | bytes 983048 | tf_op jit(solution)/shard_map/ppermute | solution.py:131
  6.5 8.7 %collective-permute-start.1 = (f32[4,128,128]{2,1,0:T(8,128)S(1)}, f32[4,128,128]{2,1,0:T(8,128)S(1)}, u32[]{:S(2)}, u32[]{:S(2)}) collective-permute-start(f32[4,128,128]{2,1,0:T(8,128)S(1)} %get-tuple-element.29.refs_0_), channel_id=1, source_target_pairs={{0,2},{1,5},{2,0},{3,7},{4,6},{5,1},{6,4},{7,3},{8,10},{9,13},{10,... | collective-permute-start | bytes 786440 | tf_op jit(solution)/shard_map/ppermute | solution.py:131
  7.9 7.3 %collective-permute-start.4 = (f32[4,128,128]{2,1,0:T(8,128)S(1)}, f32[4,128,128]{2,1,0:T(8,128)S(1)}, u32[]{:S(2)}, u32[]{:S(2)}) collective-permute-start(f32[4,128,128]{2,1,0:T(8,128)S(1)} %get-tuple-element.29.refs_0_), channel_id=1, source_target_pairs={{0,4},{1,3},{2,6},{3,1},{4,0},{5,7},{6,2},{7,5},{8,12},{9,11},{10,... | collective-permute-start | bytes 786440 | tf_op jit(solution)/shard_map/ppermute | solution.py:131
  15.3 19.2 %collective-permute-start.10 = (f32[22,128,128]{2,1,0:T(8,128)S(1)}, f32[22,128,128]{2,1,0:T(8,128)S(1)}, u32[]{:S(2)}, u32[]{:S(2)}) collective-permute-start(f32[22,128,128]{2,1,0:T(8,128)S(1)} %constant_dynamic-update-slice_fusion), channel_id=1, source_target_pairs={{0,1},{1,0},{2,3},{3,2},{4,5},{5,4},{6,7},{7,6},{8,9},{9,8},{10,11... | collective-permute-start | bytes 4325384 | tf_op jit(solution)/shard_map/ppermute | solution.py:131
  15.4 8.7 %collective-permute-start.3 = (f32[4,128,128]{2,1,0:T(8,128)S(1)}, f32[4,128,128]{2,1,0:T(8,128)S(1)}, u32[]{:S(2)}, u32[]{:S(2)}) collective-permute-start(f32[4,128,128]{2,1,0:T(8,128)S(1)} %collective-permute-done.1.refs_1_), channel_id=1, source_target_pairs={{0,8},{1,9},{2,10},{3,11},{4,12},{5,13},{6,14},{7,15},{8,0},{9,1},... | collective-permute-start | bytes 786440 | tf_op jit(solution)/shard_map/ppermute | solution.py:131
  15.9 8.2 %collective-permute-start.6 = (f32[5,128,128]{2,1,0:T(8,128)S(1)}, f32[5,128,128]{2,1,0:T(8,128)S(1)}, u32[]{:S(2)}, u32[]{:S(2)}) collective-permute-start(f32[5,128,128]{2,1,0:T(8,128)S(1)} %collective-permute-done.2.refs_4_), channel_id=1, source_target_pairs={{0,1},{1,0},{2,3},{3,2},{4,5},{5,4},{6,7},{7,6},{8,16},{9,17},{10,... | collective-permute-start | bytes 983048 | tf_op jit(solution)/shard_map/ppermute | solution.py:131
  16.2 15.6 %collective-permute-start.5 = (f32[12,128,128]{2,1,0:T(8,128)S(1)}, f32[12,128,128]{2,1,0:T(8,128)S(1)}, u32[]{:S(2)}, u32[]{:S(2)}) collective-permute-start(f32[12,128,128]{2,1,0:T(8,128)S(1)} %pad_maximum_fusion.2), channel_id=1, source_target_pairs={{0,4},{1,3},{2,6},{3,1},{4,0},{5,7},{6,2},{7,5},{8,12},{9,11},{10,... | collective-permute-start | bytes 2359304 | tf_op jit(solution)/shard_map/ppermute | solution.py:131
  17.8 9.2 %collective-permute-start.7 = (f32[4,128,128]{2,1,0:T(8,128)S(1)}, f32[4,128,128]{2,1,0:T(8,128)S(1)}, u32[]{:S(2)}, u32[]{:S(2)}) collective-permute-start(f32[4,128,128]{2,1,0:T(8,128)S(1)} %slice.62), channel_id=1, source_target_pairs={{0,2},{1,5},{2,0},{3,7},{4,6},{5,1},{6,4},{7,3},{8,10},{9,13},{10,... | collective-permute-start | bytes 786440 | tf_op jit(solution)/shard_map/ppermute | solution.py:131
  24.1 5.1 %collective-permute-start.8 = (f32[4,128,128]{2,1,0:T(8,128)S(1)}, f32[4,128,128]{2,1,0:T(8,128)S(1)}, u32[]{:S(2)}, u32[]{:S(2)}) collective-permute-start(f32[4,128,128]{2,1,0:T(8,128)S(1)} %collective-permute-done.3.refs_5_), channel_id=1, source_target_pairs={{0,1},{1,0},{2,3},{3,2},{4,5},{5,4},{6,7},{7,6},{8,16},{9,17},{10,... | collective-permute-start | bytes 786440 | tf_op jit(solution)/shard_map/ppermute | solution.py:131
  24.1 5.1 %collective-permute-start.9 = (f32[1,128,128]{2,1,0:T(8,128)S(1)}, f32[1,128,128]{2,1,0:T(8,128)S(1)}, u32[]{:S(2)}, u32[]{:S(2)}) collective-permute-start(f32[1,128,128]{2,1,0:T(8,128)S(1)} %fusion), channel_id=1, source_target_pairs={{0,2},{1,5},{2,0},{3,7},{4,6},{5,1},{6,4},{7,3},{8,10},{9,13},{10,... | collective-permute-start | bytes 196616 | tf_op jit(solution)/shard_map/ppermute | solution.py:131
  27.1 11.0 %collective-permute-start.12 = (f32[9,128,128]{2,1,0:T(8,128)S(1)}, f32[9,128,128]{2,1,0:T(8,128)S(1)}, u32[]{:S(2)}, u32[]{:S(2)}) collective-permute-start(f32[9,128,128]{2,1,0:T(8,128)S(1)} %pad_maximum_fusion.3), channel_id=1, source_target_pairs={{0,4},{1,3},{2,6},{3,1},{4,0},{5,7},{6,2},{7,5},{8,12},{9,11},{10,... | collective-permute-start | bytes 1769480 | tf_op jit(solution)/shard_map/ppermute | solution.py:131
  31.8 7.9 %collective-permute-start.13 = (f32[4,128,128]{2,1,0:T(8,128)S(1)}, f32[4,128,128]{2,1,0:T(8,128)S(1)}, u32[]{:S(2)}, u32[]{:S(2)}) collective-permute-start(f32[4,128,128]{2,1,0:T(8,128)S(1)} %get-tuple-element.45.refs_3_), channel_id=1, source_target_pairs={{0,8},{1,9},{2,10},{3,11},{4,12},{5,13},{6,14},{7,15},{8,0},{9,1},... | collective-permute-start | bytes 786440 | tf_op jit(solution)/shard_map/ppermute | solution.py:131
  34.4 9.3 %collective-permute-start.14 = (f32[25,128,128]{2,1,0:T(8,128)S(1)}, f32[25,128,128]{2,1,0:T(8,128)S(1)}, u32[]{:S(2)}, u32[]{:S(2)}) collective-permute-start(f32[25,128,128]{2,1,0:T(8,128)S(1)} %pad_maximum_fusion), channel_id=1, source_target_pairs={{0,1},{1,0},{2,3},{3,2},{4,5},{5,4},{6,7},{7,6},{8,9},{9,8},{10,11... | collective-permute-start | bytes 4915208 | tf_op jit(solution)/shard_map/ppermute | solution.py:131
  34.5 7.1 %collective-permute-start.11 = (f32[5,128,128]{2,1,0:T(8,128)S(1)}, f32[5,128,128]{2,1,0:T(8,128)S(1)}, u32[]{:S(2)}, u32[]{:S(2)}) collective-permute-start(f32[5,128,128]{2,1,0:T(8,128)S(1)} %pad_maximum_fusion.4), channel_id=1, source_target_pairs={{0,4},{1,3},{2,6},{3,1},{4,0},{5,7},{6,2},{7,5},{8,12},{9,11},{10,... | collective-permute-start | bytes 983048 | tf_op jit(solution)/shard_map/ppermute | solution.py:131
  39.9 2.7 %collective-permute-start.15 = (f32[16,128,128]{2,1,0:T(8,128)S(1)}, f32[16,128,128]{2,1,0:T(8,128)S(1)}, u32[]{:S(2)}, u32[]{:S(2)}) collective-permute-start(f32[16,128,128]{2,1,0:T(8,128)S(1)} %pad_maximum_fusion.1), channel_id=1, source_target_pairs={{0,1},{1,0},{2,3},{3,2},{4,5},{5,4},{6,7},{7,6},{8,9},{9,8},{10,11... | collective-permute-start | bytes 3145736 | tf_op jit(solution)/shard_map/ppermute | solution.py:131
  41.7 2.0 %collective-permute-start.16 = (f32[8,128,128]{2,1,0:T(8,128)S(1)}, f32[8,128,128]{2,1,0:T(8,128)S(1)}, u32[]{:S(2)}, u32[]{:S(2)}) collective-permute-start(f32[8,128,128]{2,1,0:T(8,128)S(1)} %get-tuple-element.51), channel_id=1, source_target_pairs={{0,1},{1,0},{2,3},{3,2},{4,5},{5,4},{6,7},{7,6},{8,9},{9,8},{10,11... | collective-permute-start | bytes 1572872 | tf_op jit(solution)/shard_map/ppermute | solution.py:131
  43.7 17.6 %copy-start.1 = (f32[512,256]{1,0:T(8,128)S(1)}, f32[512,256]{1,0:T(8,128)}, u32[]{:S(2)}) copy-start(f32[512,256]{1,0:T(8,128)} %matrix.3) | copy-start | bytes 1572868
  45.7 15.6 %collective-permute-start.17 = (f32[7,16,128]{2,1,0:T(8,128)S(1)}, f32[7,16,128]{2,1,0:T(8,128)S(1)}, u32[]{:S(2)}, u32[]{:S(2)}) collective-permute-start(f32[7,16,128]{2,1,0:T(8,128)S(1)} %get-tuple-element.53), channel_id=1, source_target_pairs={{0,8},{1,9},{2,10},{3,11},{4,12},{5,13},{6,14},{7,15},{8,0},{9,1},... | collective-permute-start | bytes 172040 | tf_op jit(solution)/shard_map/ppermute | solution.py:131

commit v6 on v5

--- a/solution.py
+++ b/solution.py
@@ -296,15 +296,16 @@
         product = tail_product * inverse + rows[:, pl.ds(j + 1, 1), :].reshape(BLOCKS, TILE)
         inner = scaling * (total(v * product) - v_correction)
         w = scaling * (product - correction) - (0.5 * scaling * inner) * v
+        ahead = p_all[:, pl.ds(jnp.minimum(j + 1, PANEL - 1), 1), :].reshape(BLOCKS, TILE)
+        column = ahead - total(jnp.where(first, w, 0.0)) * v - w
         w3 = w[:, None, :]
         v_heads = jnp.sum(jnp.where(on_diagonal, v[0:1], 0.0), axis=1, keepdims=True)
         w_heads = jnp.sum(jnp.where(on_diagonal, w[0:1], 0.0), axis=1, keepdims=True)
-        panel = p_all[...] - w_heads[None] * v3 - v_heads[None] * w3
-        p_all[...] = panel
+        p_all[...] = p_all[...] - w_heads[None] * v3 - v_heads[None] * w3
         v_all[...] = jnp.where(which == j, v3, refl)
         w_all[...] = jnp.where(which == j, w3, images)
         radii[...] = jnp.where(which_sub == j, -radius, radii[...])
-        return jnp.sum(jnp.where(which == j + 1, panel, 0.0), axis=1)
+        return column
 
     steps = jnp.where(jnp.logical_or(r == 1, r == 2), PANEL, 0)
     lax.fori_loop(0, steps, step, rows[:, 0, :])

time: 62.9 us -> 62.7 us (level)
  no operation moved by 1% of the time
where the time goes in v6:
time: 62.7 us; the launch traced here: 62.6 us
  starting transfers between devices  31.1 us (50%)
  waiting for transfers between devices  25.4 us (41%)
  Pallas kernels  3.49 us (6%)
  local copies, waits for them, and re-layouts  1.36 us (2%)
  between operations  0.86 us (1%)
    ppermute x18, starting transfers between devices, send(): return lax.ppermute(value, AXES, pairs)  31.1 us
    ppermute x18, waiting for transfers between devices, send(): return lax.ppermute(value, AXES, pairs)  25.4 us
    pallas_call x1, Pallas kernels, reduce_panel(): pl.pallas_call(panel_kernel, out_shape=(jax.ShapeDtypeStruct((7, 2 * PANE...  1.96 us
    pallas_call x1, Pallas kernels, finish(): pl.pallas_call(update_kernel, out_shape=(jax.ShapeDtypeStruct(matrix.shap...  1.42 us
  transfers between devices with their start and end apart: 18, of which 11 were waited for; matrix products, arithmetic and copies ran while one was open for 1% of the time, Pallas kernels for 0%

profile of v6, /device:TPU:0, one launch (start us, length us, event | category | flops | bytes accessed | tf_op | source)
XLA Modules:
  0.0 62.6 jit_solution(8581508015391802455)
XLA Ops:
  0.6 0.0 copy-start
  0.6 1.0 %copy-done = f32[512,256]{1,0:T(8,128)S(1)} copy-done((f32[512,256]{1,0:T(8,128)S(1)}, f32[512,256]{1,0:T(8,128)}, u32[]{:S(2)}) %copy-start) | copy-done | bytes 524312
  1.7 0.1 shard_map.46
  1.8 0.5 collective-permute-start
  2.3 4.1 %collective-permute-start.2 = (f32[5,128,128]{2,1,0:T(8,128)S(1)}, f32[5,128,128]{2,1,0:T(8,128)S(1)}, u32[]{:S(2)}, u32[]{:S(2)}) collective-permute-start(f32[5,128,128]{2,1,0:T(8,128)S(1)} %get-tuple-element.30), channel_id=1, source_target_pairs={{0,8},{1,9},{2,10},{3,11},{4,12},{5,13},{6,14},{7,15},{8,0},{9,1},... | collective-permute-start | bytes 983048 | tf_op jit(solution)/shard_map/ppermute | solution.py:131
  6.5 1.5 %collective-permute-start.1 = (f32[4,128,128]{2,1,0:T(8,128)S(1)}, f32[4,128,128]{2,1,0:T(8,128)S(1)}, u32[]{:S(2)}, u32[]{:S(2)}) collective-permute-start(f32[4,128,128]{2,1,0:T(8,128)S(1)} %get-tuple-element.29.refs_0_), channel_id=1, source_target_pairs={{0,2},{1,5},{2,0},{3,7},{4,6},{5,1},{6,4},{7,3},{8,10},{9,13},{10,... | collective-permute-start | bytes 786440 | tf_op jit(solution)/shard_map/ppermute | solution.py:131
  7.9 1.5 %collective-permute-start.4 = (f32[4,128,128]{2,1,0:T(8,128)S(1)}, f32[4,128,128]{2,1,0:T(8,128)S(1)}, u32[]{:S(2)}, u32[]{:S(2)}) collective-permute-start(f32[4,128,128]{2,1,0:T(8,128)S(1)} %get-tuple-element.29.refs_0_), channel_id=1, source_target_pairs={{0,4},{1,3},{2,6},{3,1},{4,0},{5,7},{6,2},{7,5},{8,12},{9,11},{10,... | collective-permute-start | bytes 786440 | tf_op jit(solution)/shard_map/ppermute | solution.py:131
  9.5 0.0 collective-permute-done.refs_8_
  9.5 5.7 %collective-permute-done.1.refs_1_ = f32[4,128,128]{2,1,0:T(8,128)S(1)} collective-permute-done((f32[4,128,128]{2,1,0:T(8,128)S(1)}, f32[4,128,128]{2,1,0:T(8,128)S(1)}, u32[]{:S(2)}, u32[]{:S(2)}) %collective-permute-start.1) | collective-permute-done | bytes 262176 | tf_op jit(solution)/shard_map/ppermute | solution.py:131
  15.2 0.0 collective-permute-done.2.refs_4_
  15.2 0.0 collective-permute-done.4.refs_2_
  15.3 0.1 collective-permute-start.10
  15.4 0.5 collective-permute-start.3
  15.9 0.2 collective-permute-start.6
  16.1 0.1 pad_maximum_fusion.2
  16.2 1.6 %collective-permute-start.5 = (f32[12,128,128]{2,1,0:T(8,128)S(1)}, f32[12,128,128]{2,1,0:T(8,128)S(1)}, u32[]{:S(2)}, u32[]{:S(2)}) collective-permute-start(f32[12,128,128]{2,1,0:T(8,128)S(1)} %pad_maximum_fusion.2), channel_id=1, source_target_pairs={{0,4},{1,3},{2,6},{3,1},{4,0},{5,7},{6,2},{7,5},{8,12},{9,11},{10,... | collective-permute-start | bytes 2359304 | tf_op jit(solution)/shard_map/ppermute | solution.py:131
  17.8 1.5 %collective-permute-start.7 = (f32[4,128,128]{2,1,0:T(8,128)S(1)}, f32[4,128,128]{2,1,0:T(8,128)S(1)}, u32[]{:S(2)}, u32[]{:S(2)}) collective-permute-start(f32[4,128,128]{2,1,0:T(8,128)S(1)} %slice.62), channel_id=1, source_target_pairs={{0,2},{1,5},{2,0},{3,7},{4,6},{5,1},{6,4},{7,3},{8,10},{9,13},{10,... | collective-permute-start | bytes 786440 | tf_op jit(solution)/shard_map/ppermute | solution.py:131
  19.3 4.8 %collective-permute-done.3.refs_5_ = f32[4,128,128]{2,1,0:T(8,128)S(1)} collective-permute-done((f32[4,128,128]{2,1,0:T(8,128)S(1)}, f32[4,128,128]{2,1,0:T(8,128)S(1)}, u32[]{:S(2)}, u32[]{:S(2)}) %collective-permute-start.3) | collective-permute-done | bytes 262176 | tf_op jit(solution)/shard_map/ppermute | solution.py:131
  24.1 0.0 collective-permute-start.8
  24.1 0.0 collective-permute-done.6.refs_12_
  24.1 1.6 %collective-permute-start.9 = (f32[1,128,128]{2,1,0:T(8,128)S(1)}, f32[1,128,128]{2,1,0:T(8,128)S(1)}, u32[]{:S(2)}, u32[]{:S(2)}) collective-permute-start(f32[1,128,128]{2,1,0:T(8,128)S(1)} %fusion), channel_id=1, source_target_pairs={{0,2},{1,5},{2,0},{3,7},{4,6},{5,1},{6,4},{7,3},{8,10},{9,13},{10,... | collective-permute-start | bytes 196616 | tf_op jit(solution)/shard_map/ppermute | solution.py:131
  25.7 1.3 %collective-permute-done.7.refs_9_ = f32[4,128,128]{2,1,0:T(8,128)S(1)} collective-permute-done((f32[4,128,128]{2,1,0:T(8,128)S(1)}, f32[4,128,128]{2,1,0:T(8,128)S(1)}, u32[]{:S(2)}, u32[]{:S(2)}) %collective-permute-start.7) | collective-permute-done | bytes 262176 | tf_op jit(solution)/shard_map/ppermute | solution.py:131
  27.1 0.5 collective-permute-start.12
  27.6 1.6 %collective-permute-done.9 = f32[1,128,128]{2,1,0:T(8,128)S(1)} collective-permute-done((f32[1,128,128]{2,1,0:T(8,128)S(1)}, f32[1,128,128]{2,1,0:T(8,128)S(1)}, u32[]{:S(2)}, u32[]{:S(2)}) %collective-permute-start.9) | collective-permute-done | bytes 65568 | tf_op jit(solution)/shard_map/ppermute | solution.py:131
  29.2 0.0 collective-permute-done.8.refs_13_
  29.3 2.5 %collective-permute-done.5 = f32[12,128,128]{2,1,0:T(8,128)S(1)} collective-permute-done((f32[12,128,128]{2,1,0:T(8,128)S(1)}, f32[12,128,128]{2,1,0:T(8,128)S(1)}, u32[]{:S(2)}, u32[]{:S(2)}) %collective-permute-start.5) | collective-permute-done | bytes 786464 | tf_op jit(solution)/shard_map/ppermute | solution.py:131
  31.8 0.1 fusion.1
  31.8 2.4 %collective-permute-start.13 = (f32[4,128,128]{2,1,0:T(8,128)S(1)}, f32[4,128,128]{2,1,0:T(8,128)S(1)}, u32[]{:S(2)}, u32[]{:S(2)}) collective-permute-start(f32[4,128,128]{2,1,0:T(8,128)S(1)} %get-tuple-element.45.refs_3_), channel_id=1, source_target_pairs={{0,8},{1,9},{2,10},{3,11},{4,12},{5,13},{6,14},{7,15},{8,0},{9,1},... | collective-permute-start | bytes 786440 | tf_op jit(solution)/shard_map/ppermute | solution.py:131
  34.3 0.1 pad_maximum_fusion
  34.4 0.1 collective-permute-start.14
  34.5 0.0 collective-permute-done.10.refs_17_
  34.5 1.6 %collective-permute-start.11 = (f32[5,128,128]{2,1,0:T(8,128)S(1)}, f32[5,128,128]{2,1,0:T(8,128)S(1)}, u32[]{:S(2)}, u32[]{:S(2)}) collective-permute-start(f32[5,128,128]{2,1,0:T(8,128)S(1)} %pad_maximum_fusion.4), channel_id=1, source_target_pairs={{0,4},{1,3},{2,6},{3,1},{4,0},{5,7},{6,2},{7,5},{8,12},{9,11},{10,... | collective-permute-start | bytes 983048 | tf_op jit(solution)/shard_map/ppermute | solution.py:131
  36.1 2.0 %collective-permute-done.12 = f32[9,128,128]{2,1,0:T(8,128)S(1)} collective-permute-done((f32[9,128,128]{2,1,0:T(8,128)S(1)}, f32[9,128,128]{2,1,0:T(8,128)S(1)}, u32[]{:S(2)}, u32[]{:S(2)}) %collective-permute-start.12) | collective-permute-done | bytes 589856 | tf_op jit(solution)/shard_map/ppermute | solution.py:131
  38.1 1.6 %collective-permute-done.13.refs_7_ = f32[4,128,128]{2,1,0:T(8,128)S(1)} collective-permute-done((f32[4,128,128]{2,1,0:T(8,128)S(1)}, f32[4,128,128]{2,1,0:T(8,128)S(1)}, u32[]{:S(2)}, u32[]{:S(2)}) %collective-permute-start.13) | collective-permute-done | bytes 262176 | tf_op jit(solution)/shard_map/ppermute | solution.py:131
  39.8 0.1 pad_maximum_fusion.1
  39.9 0.1 collective-permute-start.15
  40.0 1.7 %collective-permute-done.11 = f32[5,128,128]{2,1,0:T(8,128)S(1)} collective-permute-done((f32[5,128,128]{2,1,0:T(8,128)S(1)}, f32[5,128,128]{2,1,0:T(8,128)S(1)}, u32[]{:S(2)}, u32[]{:S(2)}) %collective-permute-start.11) | collective-permute-done | bytes 327712 | tf_op jit(solution)/shard_map/ppermute | solution.py:131
  41.7 0.1 collective-permute-start.16
  41.8 0.8 %collective-permute-done.15.refs_19_ = f32[16,128,128]{2,1,0:T(8,128)S(1)} collective-permute-done((f32[16,128,128]{2,1,0:T(8,128)S(1)}, f32[16,128,128]{2,1,0:T(8,128)S(1)}, u32[]{:S(2)}, u32[]{:S(2)}) %collective-permute-start.15) | collective-permute-done | bytes 1048608 | tf_op jit(solution)/shard_map/ppermute | solution.py:131
  42.6 1.1 %collective-permute-done.16.refs_20_ = f32[8,128,128]{2,1,0:T(8,128)S(1)} collective-permute-done((f32[8,128,128]{2,1,0:T(8,128)S(1)}, f32[8,128,128]{2,1,0:T(8,128)S(1)}, u32[]{:S(2)}, u32[]{:S(2)}) %collective-permute-start.16) | collective-permute-done | bytes 524320 | tf_op jit(solution)/shard_map/ppermute | solution.py:131
  43.7 0.0 collective-permute-done.14.refs_18_
  43.7 0.0 copy-start.1
  43.7 2.0 %shard_map.47 = (f32[7,16,128]{2,1,0:T(8,128)S(1)}, f32[7,16,128]{2,1,0:T(8,128)S(1)}) custom-call(f32[4,128,128]{2,1,0:T(8,128)S(1)} %get-tuple-element.29.refs_0_, f32[4,128,128]{2,1,0:T(8,128)S(1)} %collective-permute-done.1.refs_1_, f32[4,128,128]{2,1,0:T(8,128)S(1)} %collective-permute-done.4.refs_2_, f32[4,128,128]{2,1,0:T(8,128)S(1)} %get-tuple-element.45.refs_3_, ...), custom_call_target="tpu_custom_call" | custom-call | tf_op jit(solution)/shard_map/pallas_call | solution.py:323
  45.7 13.3 %collective-permute-start.17 = (f32[7,16,128]{2,1,0:T(8,128)S(1)}, f32[7,16,128]{2,1,0:T(8,128)S(1)}, u32[]{:S(2)}, u32[]{:S(2)}) collective-permute-start(f32[7,16,128]{2,1,0:T(8,128)S(1)} %get-tuple-element.53), channel_id=1, source_target_pairs={{0,8},{1,9},{2,10},{3,11},{4,12},{5,13},{6,14},{7,15},{8,0},{9,1},... | collective-permute-start | bytes 172040 | tf_op jit(solution)/shard_map/ppermute | solution.py:131
  58.9 2.2 %collective-permute-done.17.theirs = f32[7,16,128]{2,1,0:T(8,128)S(1)} collective-permute-done((f32[7,16,128]{2,1,0:T(8,128)S(1)}, f32[7,16,128]{2,1,0:T(8,128)S(1)}, u32[]{:S(2)}, u32[]{:S(2)}) %collective-permute-start.17) | collective-permute-done | bytes 57376 | tf_op jit(solution)/shard_map/ppermute | solution.py:131
  61.2 0.0 copy-done.1
  61.2 1.4 %shard_map.48 = (f32[512,256]{1,0:T(8,128)}, f32[8,512]{1,0:T(8,128)}, f32[8,512]{1,0:T(8,128)}, f32[8]{0:T(128)}) custom-call(f32[512,256]{1,0:T(8,128)S(1)} %copy-done.1, f32[7,16,128]{2,1,0:T(8,128)S(1)} %get-tuple-element.52.mine, f32[7,16,128]{2,1,0:T(8,128)S(1)} %collective-permute-done.17.theirs), custom_call_target="tpu_custom_call" | custom-call | tf_op jit(solution)/shard_map/pallas_call | solution.py:377
  (18 shorter events, 0.4 us)
Async XLA Ops:
  0.6 1.0 %copy-start = (f32[512,256]{1,0:T(8,128)S(1)}, f32[512,256]{1,0:T(8,128)}, u32[]{:S(2)}) copy-start(f32[512,256]{1,0:T(8,128)} %matrix.3) | copy-start | bytes 1572868
  1.8 7.7 %collective-permute-start = (f32[5,128,128]{2,1,0:T(8,128)S(1)}, f32[5,128,128]{2,1,0:T(8,128)S(1)}, u32[]{:S(2)}, u32[]{:S(2)}) collective-permute-start(f32[5,128,128]{2,1,0:T(8,128)S(1)} %get-tuple-element.30), channel_id=1, source_target_pairs={{0,1},{1,0},{2,3},{3,2},{4,5},{5,4},{6,7},{7,6},{8,16},{9,17},{10,... | collective-permute-start | bytes 983048 | tf_op jit(solution)/shard_map/ppermute | solution.py:131
  2.3 12.9 %collective-permute-start.2 = (f32[5,128,128]{2,1,0:T(8,128)S(1)}, f32[5,128,128]{2,1,0:T(8,128)S(1)}, u32[]{:S(2)}, u32[]{:S(2)}) collective-permute-start(f32[5,128,128]{2,1,0:T(8,128)S(1)} %get-tuple-element.30), channel_id=1, source_target_pairs={{0,8},{1,9},{2,10},{3,11},{4,12},{5,13},{6,14},{7,15},{8,0},{9,1},... | collective-permute-start | bytes 983048 | tf_op jit(solution)/shard_map/ppermute | solution.py:131
  6.5 8.7 %collective-permute-start.1 = (f32[4,128,128]{2,1,0:T(8,128)S(1)}, f32[4,128,128]{2,1,0:T(8,128)S(1)}, u32[]{:S(2)}, u32[]{:S(2)}) collective-permute-start(f32[4,128,128]{2,1,0:T(8,128)S(1)} %get-tuple-element.29.refs_0_), channel_id=1, source_target_pairs={{0,2},{1,5},{2,0},{3,7},{4,6},{5,1},{6,4},{7,3},{8,10},{9,13},{10,... | collective-permute-start | bytes 786440 | tf_op jit(solution)/shard_map/ppermute | solution.py:131
  7.9 7.3 %collective-permute-start.4 = (f32[4,128,128]{2,1,0:T(8,128)S(1)}, f32[4,128,128]{2,1,0:T(8,128)S(1)}, u32[]{:S(2)}, u32[]{:S(2)}) collective-permute-start(f32[4,128,128]{2,1,0:T(8,128)S(1)} %get-tuple-element.29.refs_0_), channel_id=1, source_target_pairs={{0,4},{1,3},{2,6},{3,1},{4,0},{5,7},{6,2},{7,5},{8,12},{9,11},{10,... | collective-permute-start | bytes 786440 | tf_op jit(solution)/shard_map/ppermute | solution.py:131
  15.3 19.2 %collective-permute-start.10 = (f32[22,128,128]{2,1,0:T(8,128)S(1)}, f32[22,128,128]{2,1,0:T(8,128)S(1)}, u32[]{:S(2)}, u32[]{:S(2)}) collective-permute-start(f32[22,128,128]{2,1,0:T(8,128)S(1)} %constant_dynamic-update-slice_fusion), channel_id=1, source_target_pairs={{0,1},{1,0},{2,3},{3,2},{4,5},{5,4},{6,7},{7,6},{8,9},{9,8},{10,11... | collective-permute-start | bytes 4325384 | tf_op jit(solution)/shard_map/ppermute | solution.py:131
  15.4 8.7 %collective-permute-start.3 = (f32[4,128,128]{2,1,0:T(8,128)S(1)}, f32[4,128,128]{2,1,0:T(8,128)S(1)}, u32[]{:S(2)}, u32[]{:S(2)}) collective-permute-start(f32[4,128,128]{2,1,0:T(8,128)S(1)} %collective-permute-done.1.refs_1_), channel_id=1, source_target_pairs={{0,8},{1,9},{2,10},{3,11},{4,12},{5,13},{6,14},{7,15},{8,0},{9,1},... | collective-permute-start | bytes 786440 | tf_op jit(solution)/shard_map/ppermute | solution.py:131
  15.9 8.2 %collective-permute-start.6 = (f32[5,128,128]{2,1,0:T(8,128)S(1)}, f32[5,128,128]{2,1,0:T(8,128)S(1)}, u32[]{:S(2)}, u32[]{:S(2)}) collective-permute-start(f32[5,128,128]{2,1,0:T(8,128)S(1)} %collective-permute-done.2.refs_4_), channel_id=1, source_target_pairs={{0,1},{1,0},{2,3},{3,2},{4,5},{5,4},{6,7},{7,6},{8,16},{9,17},{10,... | collective-permute-start | bytes 983048 | tf_op jit(solution)/shard_map/ppermute | solution.py:131
  16.2 15.6 %collective-permute-start.5 = (f32[12,128,128]{2,1,0:T(8,128)S(1)}, f32[12,128,128]{2,1,0:T(8,128)S(1)}, u32[]{:S(2)}, u32[]{:S(2)}) collective-permute-start(f32[12,128,128]{2,1,0:T(8,128)S(1)} %pad_maximum_fusion.2), channel_id=1, source_target_pairs={{0,4},{1,3},{2,6},{3,1},{4,0},{5,7},{6,2},{7,5},{8,12},{9,11},{10,... | collective-permute-start | bytes 2359304 | tf_op jit(solution)/shard_map/ppermute | solution.py:131
  17.8 9.2 %collective-permute-start.7 = (f32[4,128,128]{2,1,0:T(8,128)S(1)}, f32[4,128,128]{2,1,0:T(8,128)S(1)}, u32[]{:S(2)}, u32[]{:S(2)}) collective-permute-start(f32[4,128,128]{2,1,0:T(8,128)S(1)} %slice.62), channel_id=1, source_target_pairs={{0,2},{1,5},{2,0},{3,7},{4,6},{5,1},{6,4},{7,3},{8,10},{9,13},{10,... | collective-permute-start | bytes 786440 | tf_op jit(solution)/shard_map/ppermute | solution.py:131
  24.1 5.1 %collective-permute-start.8 = (f32[4,128,128]{2,1,0:T(8,128)S(1)}, f32[4,128,128]{2,1,0:T(8,128)S(1)}, u32[]{:S(2)}, u32[]{:S(2)}) collective-permute-start(f32[4,128,128]{2,1,0:T(8,128)S(1)} %collective-permute-done.3.refs_5_), channel_id=1, source_target_pairs={{0,1},{1,0},{2,3},{3,2},{4,5},{5,4},{6,7},{7,6},{8,16},{9,17},{10,... | collective-permute-start | bytes 786440 | tf_op jit(solution)/shard_map/ppermute | solution.py:131
  24.1 5.1 %collective-permute-start.9 = (f32[1,128,128]{2,1,0:T(8,128)S(1)}, f32[1,128,128]{2,1,0:T(8,128)S(1)}, u32[]{:S(2)}, u32[]{:S(2)}) collective-permute-start(f32[1,128,128]{2,1,0:T(8,128)S(1)} %fusion), channel_id=1, source_target_pairs={{0,2},{1,5},{2,0},{3,7},{4,6},{5,1},{6,4},{7,3},{8,10},{9,13},{10,... | collective-permute-start | bytes 196616 | tf_op jit(solution)/shard_map/ppermute | solution.py:131
  27.1 11.0 %collective-permute-start.12 = (f32[9,128,128]{2,1,0:T(8,128)S(1)}, f32[9,128,128]{2,1,0:T(8,128)S(1)}, u32[]{:S(2)}, u32[]{:S(2)}) collective-permute-start(f32[9,128,128]{2,1,0:T(8,128)S(1)} %pad_maximum_fusion.3), channel_id=1, source_target_pairs={{0,4},{1,3},{2,6},{3,1},{4,0},{5,7},{6,2},{7,5},{8,12},{9,11},{10,... | collective-permute-start | bytes 1769480 | tf_op jit(solution)/shard_map/ppermute | solution.py:131
  31.8 7.9 %collective-permute-start.13 = (f32[4,128,128]{2,1,0:T(8,128)S(1)}, f32[4,128,128]{2,1,0:T(8,128)S(1)}, u32[]{:S(2)}, u32[]{:S(2)}) collective-permute-start(f32[4,128,128]{2,1,0:T(8,128)S(1)} %get-tuple-element.45.refs_3_), channel_id=1, source_target_pairs={{0,8},{1,9},{2,10},{3,11},{4,12},{5,13},{6,14},{7,15},{8,0},{9,1},... | collective-permute-start | bytes 786440 | tf_op jit(solution)/shard_map/ppermute | solution.py:131
  34.4 9.3 %collective-permute-start.14 = (f32[25,128,128]{2,1,0:T(8,128)S(1)}, f32[25,128,128]{2,1,0:T(8,128)S(1)}, u32[]{:S(2)}, u32[]{:S(2)}) collective-permute-start(f32[25,128,128]{2,1,0:T(8,128)S(1)} %pad_maximum_fusion), channel_id=1, source_target_pairs={{0,1},{1,0},{2,3},{3,2},{4,5},{5,4},{6,7},{7,6},{8,9},{9,8},{10,11... | collective-permute-start | bytes 4915208 | tf_op jit(solution)/shard_map/ppermute | solution.py:131
  34.5 7.1 %collective-permute-start.11 = (f32[5,128,128]{2,1,0:T(8,128)S(1)}, f32[5,128,128]{2,1,0:T(8,128)S(1)}, u32[]{:S(2)}, u32[]{:S(2)}) collective-permute-start(f32[5,128,128]{2,1,0:T(8,128)S(1)} %pad_maximum_fusion.4), channel_id=1, source_target_pairs={{0,4},{1,3},{2,6},{3,1},{4,0},{5,7},{6,2},{7,5},{8,12},{9,11},{10,... | collective-permute-start | bytes 983048 | tf_op jit(solution)/shard_map/ppermute | solution.py:131
  39.9 2.7 %collective-permute-start.15 = (f32[16,128,128]{2,1,0:T(8,128)S(1)}, f32[16,128,128]{2,1,0:T(8,128)S(1)}, u32[]{:S(2)}, u32[]{:S(2)}) collective-permute-start(f32[16,128,128]{2,1,0:T(8,128)S(1)} %pad_maximum_fusion.1), channel_id=1, source_target_pairs={{0,1},{1,0},{2,3},{3,2},{4,5},{5,4},{6,7},{7,6},{8,9},{9,8},{10,11... | collective-permute-start | bytes 3145736 | tf_op jit(solution)/shard_map/ppermute | solution.py:131
  41.7 2.0 %collective-permute-start.16 = (f32[8,128,128]{2,1,0:T(8,128)S(1)}, f32[8,128,128]{2,1,0:T(8,128)S(1)}, u32[]{:S(2)}, u32[]{:S(2)}) collective-permute-start(f32[8,128,128]{2,1,0:T(8,128)S(1)} %get-tuple-element.51), channel_id=1, source_target_pairs={{0,1},{1,0},{2,3},{3,2},{4,5},{5,4},{6,7},{7,6},{8,9},{9,8},{10,11... | collective-permute-start | bytes 1572872 | tf_op jit(solution)/shard_map/ppermute | solution.py:131
  43.7 17.5 %copy-start.1 = (f32[512,256]{1,0:T(8,128)S(1)}, f32[512,256]{1,0:T(8,128)}, u32[]{:S(2)}) copy-start(f32[512,256]{1,0:T(8,128)} %matrix.3) | copy-start | bytes 1572868
  45.7 15.5 %collective-permute-start.17 = (f32[7,16,128]{2,1,0:T(8,128)S(1)}, f32[7,16,128]{2,1,0:T(8,128)S(1)}, u32[]{:S(2)}, u32[]{:S(2)}) collective-permute-start(f32[7,16,128]{2,1,0:T(8,128)S(1)} %get-tuple-element.53), channel_id=1, source_target_pairs={{0,8},{1,9},{2,10},{3,11},{4,12},{5,13},{6,14},{7,15},{8,0},{9,1},... | collective-permute-start | bytes 172040 | tf_op jit(solution)/shard_map/ppermute | solution.py:131

commit v7 on v6

--- a/solution.py
+++ b/solution.py
@@ -140,10 +140,11 @@
     ma = send(a5, MIDDLE)
     c = send(a, SIDE_B)
     first_b = send(jnp.concatenate([b, ua[:4], ma[:4]]), SIDE_B)
-    na = send(ua, MIDDLE)
+    held, c = lax.optimization_barrier((ua, c))
+    na = send(held, MIDDLE)
     held, b = lax.optimization_barrier((ma[:4], b))
     mb = send(held, SIDE_A)
-    held, ua = lax.optimization_barrier((b, ua))
+    held, ma = lax.optimization_barrier((b, ma))
     ub = send(held, OUTER)
     held, ma = lax.optimization_barrier((jnp.concatenate([a, b, c, ua, ma]), ma))
     g0 = send(held, TO_CORE)

time: 62.7 us -> 61.7 us (0.984)
  starting transfers between devices: 31.1 us -> 28.2 us
  waiting for transfers between devices: 25.4 us -> 27.4 us
    ppermute x18, starting transfers between devices: 31.1 us -> 28.2 us  [send(): return lax.ppermute(value, AXES, pairs)]
    ppermute x18, waiting for transfers between devices: 25.4 us -> 27.4 us  [send(): return lax.ppermute(value, AXES, pairs)]
  transfers between devices with their start and end apart: 18 -> 18, of which waited for: 11 -> 12; matrix products, arithmetic and copies ran while one was open for 1% -> 1% of each run, Pallas kernels for 0% -> 0%
where the time goes in v7:
time: 61.7 us; the launch traced here: 61.6 us
  starting transfers between devices  28.2 us (46%)
  waiting for transfers between devices  27.4 us (44%)
  Pallas kernels  3.49 us (6%)
  local copies, waits for them, and re-layouts  1.36 us (2%)
  between operations  0.84 us (1%)
    ppermute x18, starting transfers between devices, send(): return lax.ppermute(value, AXES, pairs)  28.2 us
    ppermute x18, waiting for transfers between devices, send(): return lax.ppermute(value, AXES, pairs)  27.4 us
    pallas_call x1, Pallas kernels, reduce_panel(): pl.pallas_call(panel_kernel, out_shape=(jax.ShapeDtypeStruct((7, 2 * PANE...  1.96 us
    pallas_call x1, Pallas kernels, finish(): pl.pallas_call(update_kernel, out_shape=(jax.ShapeDtypeStruct(matrix.shap...  1.42 us
  transfers between devices with their start and end apart: 18, of which 12 were waited for; matrix products, arithmetic and copies ran while one was open for 1% of the time, Pallas kernels for 0%

profile of v7, /device:TPU:0, one launch (start us, length us, event | category | flops | bytes accessed | tf_op | source)
XLA Modules:
  0.0 61.6 jit_solution(17978962609416057763)
XLA Ops:
  0.6 0.0 copy-start
  0.6 1.0 %copy-done = f32[512,256]{1,0:T(8,128)S(1)} copy-done((f32[512,256]{1,0:T(8,128)S(1)}, f32[512,256]{1,0:T(8,128)}, u32[]{:S(2)}) %copy-start) | copy-done | bytes 524312
  1.7 0.1 shard_map.46
  1.8 3.1 %collective-permute-start.3 = (f32[5,128,128]{2,1,0:T(8,128)S(1)}, f32[5,128,128]{2,1,0:T(8,128)S(1)}, u32[]{:S(2)}, u32[]{:S(2)}) collective-permute-start(f32[5,128,128]{2,1,0:T(8,128)S(1)} %get-tuple-element.32), channel_id=1, source_target_pairs={{0,8},{1,9},{2,10},{3,11},{4,12},{5,13},{6,14},{7,15},{8,0},{9,1},... | collective-permute-start | bytes 983048 | tf_op jit(solution)/shard_map/ppermute | solution.py:131
  4.9 0.0 collective-permute-start
  4.9 1.5 %collective-permute-start.4 = (f32[4,128,128]{2,1,0:T(8,128)S(1)}, f32[4,128,128]{2,1,0:T(8,128)S(1)}, u32[]{:S(2)}, u32[]{:S(2)}) collective-permute-start(f32[4,128,128]{2,1,0:T(8,128)S(1)} %get-tuple-element.31.refs_0_), channel_id=1, source_target_pairs={{0,4},{1,3},{2,6},{3,1},{4,0},{5,7},{6,2},{7,5},{8,12},{9,11},{10,... | collective-permute-start | bytes 786440 | tf_op jit(solution)/shard_map/ppermute | solution.py:131
  6.4 1.5 %collective-permute-start.1 = (f32[4,128,128]{2,1,0:T(8,128)S(1)}, f32[4,128,128]{2,1,0:T(8,128)S(1)}, u32[]{:S(2)}, u32[]{:S(2)}) collective-permute-start(f32[4,128,128]{2,1,0:T(8,128)S(1)} %get-tuple-element.31.refs_0_), channel_id=1, source_target_pairs={{0,2},{1,5},{2,0},{3,7},{4,6},{5,1},{6,4},{7,3},{8,10},{9,13},{10,... | collective-permute-start | bytes 786440 | tf_op jit(solution)/shard_map/ppermute | solution.py:131
  7.9 5.4 %collective-permute-done.4.refs_2_ = f32[4,128,128]{2,1,0:T(8,128)S(1)} collective-permute-done((f32[4,128,128]{2,1,0:T(8,128)S(1)}, f32[4,128,128]{2,1,0:T(8,128)S(1)}, u32[]{:S(2)}, u32[]{:S(2)}) %collective-permute-start.4) | collective-permute-done | bytes 262176 | tf_op jit(solution)/shard_map/ppermute | solution.py:131
  13.3 0.0 collective-permute-done.3.refs_4_
  13.4 0.0 collective-permute-done.refs_8_
  13.4 0.2 collective-permute-done.1.refs_1_
  13.7 0.3 collective-permute-start.10
  14.1 0.2 collective-permute-start.6
  14.3 3.2 %collective-permute-start.2 = (f32[4,128,128]{2,1,0:T(8,128)S(1)}, f32[4,128,128]{2,1,0:T(8,128)S(1)}, u32[]{:S(2)}, u32[]{:S(2)}) collective-permute-start(f32[4,128,128]{2,1,0:T(8,128)S(1)} %collective-permute-done.1.refs_1_), channel_id=1, source_target_pairs={{0,8},{1,9},{2,10},{3,11},{4,12},{5,13},{6,14},{7,15},{8,0},{9,1},... | collective-permute-start | bytes 786440 | tf_op jit(solution)/shard_map/ppermute | solution.py:131
  17.5 0.1 pad_maximum_fusion.2
  17.6 1.6 %collective-permute-start.5 = (f32[12,128,128]{2,1,0:T(8,128)S(1)}, f32[12,128,128]{2,1,0:T(8,128)S(1)}, u32[]{:S(2)}, u32[]{:S(2)}) collective-permute-start(f32[12,128,128]{2,1,0:T(8,128)S(1)} %pad_maximum_fusion.2), channel_id=1, source_target_pairs={{0,4},{1,3},{2,6},{3,1},{4,0},{5,7},{6,2},{7,5},{8,12},{9,11},{10,... | collective-permute-start | bytes 2359304 | tf_op jit(solution)/shard_map/ppermute | solution.py:131
  19.2 1.5 %collective-permute-start.7 = (f32[4,128,128]{2,1,0:T(8,128)S(1)}, f32[4,128,128]{2,1,0:T(8,128)S(1)}, u32[]{:S(2)}, u32[]{:S(2)}) collective-permute-start(f32[4,128,128]{2,1,0:T(8,128)S(1)} %slice.62), channel_id=1, source_target_pairs={{0,2},{1,5},{2,0},{3,7},{4,6},{5,1},{6,4},{7,3},{8,10},{9,13},{10,... | collective-permute-start | bytes 786440 | tf_op jit(solution)/shard_map/ppermute | solution.py:131
  20.7 3.5 %collective-permute-done.2.refs_5_ = f32[4,128,128]{2,1,0:T(8,128)S(1)} collective-permute-done((f32[4,128,128]{2,1,0:T(8,128)S(1)}, f32[4,128,128]{2,1,0:T(8,128)S(1)}, u32[]{:S(2)}, u32[]{:S(2)}) %collective-permute-start.2) | collective-permute-done | bytes 262176 | tf_op jit(solution)/shard_map/ppermute | solution.py:131
  24.1 0.0 collective-permute-start.8
  24.1 0.0 collective-permute-done.6.refs_12_
  24.2 1.6 %collective-permute-start.9 = (f32[1,128,128]{2,1,0:T(8,128)S(1)}, f32[1,128,128]{2,1,0:T(8,128)S(1)}, u32[]{:S(2)}, u32[]{:S(2)}) collective-permute-start(f32[1,128,128]{2,1,0:T(8,128)S(1)} %fusion), channel_id=1, source_target_pairs={{0,2},{1,5},{2,0},{3,7},{4,6},{5,1},{6,4},{7,3},{8,10},{9,13},{10,... | collective-permute-start | bytes 196616 | tf_op jit(solution)/shard_map/ppermute | solution.py:131
  25.7 2.7 %collective-permute-done.7.refs_9_ = f32[4,128,128]{2,1,0:T(8,128)S(1)} collective-permute-done((f32[4,128,128]{2,1,0:T(8,128)S(1)}, f32[4,128,128]{2,1,0:T(8,128)S(1)}, u32[]{:S(2)}, u32[]{:S(2)}) %collective-permute-start.7) | collective-permute-done | bytes 262176 | tf_op jit(solution)/shard_map/ppermute | solution.py:131
  28.5 0.6 collective-permute-start.12
  29.0 0.8 %collective-permute-done.9 = f32[1,128,128]{2,1,0:T(8,128)S(1)} collective-permute-done((f32[1,128,128]{2,1,0:T(8,128)S(1)}, f32[1,128,128]{2,1,0:T(8,128)S(1)}, u32[]{:S(2)}, u32[]{:S(2)}) %collective-permute-start.9) | collective-permute-done | bytes 65568 | tf_op jit(solution)/shard_map/ppermute | solution.py:131
  29.8 0.0 collective-permute-done.8.refs_13_
  29.8 3.3 %collective-permute-done.5 = f32[12,128,128]{2,1,0:T(8,128)S(1)} collective-permute-done((f32[12,128,128]{2,1,0:T(8,128)S(1)}, f32[12,128,128]{2,1,0:T(8,128)S(1)}, u32[]{:S(2)}, u32[]{:S(2)}) %collective-permute-start.5) | collective-permute-done | bytes 786464 | tf_op jit(solution)/shard_map/ppermute | solution.py:131
  33.1 0.1 fusion.1
  33.2 0.4 collective-permute-start.13
  33.6 0.1 pad_maximum_fusion
  33.7 0.1 collective-permute-start.14
  33.8 0.0 collective-permute-done.10.refs_17_
  33.8 1.6 %collective-permute-start.11 = (f32[5,128,128]{2,1,0:T(8,128)S(1)}, f32[5,128,128]{2,1,0:T(8,128)S(1)}, u32[]{:S(2)}, u32[]{:S(2)}) collective-permute-start(f32[5,128,128]{2,1,0:T(8,128)S(1)} %pad_maximum_fusion.4), channel_id=1, source_target_pairs={{0,4},{1,3},{2,6},{3,1},{4,0},{5,7},{6,2},{7,5},{8,12},{9,11},{10,... | collective-permute-start | bytes 983048 | tf_op jit(solution)/shard_map/ppermute | solution.py:131
  35.4 4.1 %collective-permute-done.12 = f32[9,128,128]{2,1,0:T(8,128)S(1)} collective-permute-done((f32[9,128,128]{2,1,0:T(8,128)S(1)}, f32[9,128,128]{2,1,0:T(8,128)S(1)}, u32[]{:S(2)}, u32[]{:S(2)}) %collective-permute-start.12) | collective-permute-done | bytes 589856 | tf_op jit(solution)/shard_map/ppermute | solution.py:131
  39.5 1.0 %collective-permute-done.13.refs_7_ = f32[4,128,128]{2,1,0:T(8,128)S(1)} collective-permute-done((f32[4,128,128]{2,1,0:T(8,128)S(1)}, f32[4,128,128]{2,1,0:T(8,128)S(1)}, u32[]{:S(2)}, u32[]{:S(2)}) %collective-permute-start.13) | collective-permute-done | bytes 262176 | tf_op jit(solution)/shard_map/ppermute | solution.py:131
  40.5 0.1 pad_maximum_fusion.1
  40.6 0.1 collective-permute-start.15
  40.7 2.3 %collective-permute-done.11 = f32[5,128,128]{2,1,0:T(8,128)S(1)} collective-permute-done((f32[5,128,128]{2,1,0:T(8,128)S(1)}, f32[5,128,128]{2,1,0:T(8,128)S(1)}, u32[]{:S(2)}, u32[]{:S(2)}) %collective-permute-start.11) | collective-permute-done | bytes 327712 | tf_op jit(solution)/shard_map/ppermute | solution.py:131
  43.1 0.1 collective-permute-start.16
  43.2 0.1 collective-permute-done.15.refs_19_
  43.3 1.7 %collective-permute-done.16.refs_20_ = f32[8,128,128]{2,1,0:T(8,128)S(1)} collective-permute-done((f32[8,128,128]{2,1,0:T(8,128)S(1)}, f32[8,128,128]{2,1,0:T(8,128)S(1)}, u32[]{:S(2)}, u32[]{:S(2)}) %collective-permute-start.16) | collective-permute-done | bytes 524320 | tf_op jit(solution)/shard_map/ppermute | solution.py:131
  45.1 0.0 collective-permute-done.14.refs_18_
  45.1 0.0 copy-start.1
  45.1 2.0 %shard_map.47 = (f32[7,16,128]{2,1,0:T(8,128)S(1)}, f32[7,16,128]{2,1,0:T(8,128)S(1)}) custom-call(f32[4,128,128]{2,1,0:T(8,128)S(1)} %get-tuple-element.31.refs_0_, f32[4,128,128]{2,1,0:T(8,128)S(1)} %collective-permute-done.1.refs_1_, f32[4,128,128]{2,1,0:T(8,128)S(1)} %collective-permute-done.4.refs_2_, f32[4,128,128]{2,1,0:T(8,128)S(1)} %get-tuple-element.49.refs_3_, ...), custom_call_target="tpu_custom_call" | custom-call | tf_op jit(solution)/shard_map/pallas_call | solution.py:324
  47.0 10.9 %collective-permute-start.17 = (f32[7,16,128]{2,1,0:T(8,128)S(1)}, f32[7,16,128]{2,1,0:T(8,128)S(1)}, u32[]{:S(2)}, u32[]{:S(2)}) collective-permute-start(f32[7,16,128]{2,1,0:T(8,128)S(1)} %get-tuple-element.57), channel_id=1, source_target_pairs={{0,8},{1,9},{2,10},{3,11},{4,12},{5,13},{6,14},{7,15},{8,0},{9,1},... | collective-permute-start | bytes 172040 | tf_op jit(solution)/shard_map/ppermute | solution.py:131
  57.9 2.2 %collective-permute-done.17.theirs = f32[7,16,128]{2,1,0:T(8,128)S(1)} collective-permute-done((f32[7,16,128]{2,1,0:T(8,128)S(1)}, f32[7,16,128]{2,1,0:T(8,128)S(1)}, u32[]{:S(2)}, u32[]{:S(2)}) %collective-permute-start.17) | collective-permute-done | bytes 57376 | tf_op jit(solution)/shard_map/ppermute | solution.py:131
  60.2 0.0 copy-done.1
  60.2 1.4 %shard_map.48 = (f32[512,256]{1,0:T(8,128)}, f32[8,512]{1,0:T(8,128)}, f32[8,512]{1,0:T(8,128)}, f32[8]{0:T(128)}) custom-call(f32[512,256]{1,0:T(8,128)S(1)} %copy-done.1, f32[7,16,128]{2,1,0:T(8,128)S(1)} %get-tuple-element.56.mine, f32[7,16,128]{2,1,0:T(8,128)S(1)} %collective-permute-done.17.theirs), custom_call_target="tpu_custom_call" | custom-call | tf_op jit(solution)/shard_map/pallas_call | solution.py:378
  (18 shorter events, 0.4 us)
Async XLA Ops:
  0.6 1.0 %copy-start = (f32[512,256]{1,0:T(8,128)S(1)}, f32[512,256]{1,0:T(8,128)}, u32[]{:S(2)}) copy-start(f32[512,256]{1,0:T(8,128)} %matrix.3) | copy-start | bytes 1572868
  1.8 11.6 %collective-permute-start.3 = (f32[5,128,128]{2,1,0:T(8,128)S(1)}, f32[5,128,128]{2,1,0:T(8,128)S(1)}, u32[]{:S(2)}, u32[]{:S(2)}) collective-permute-start(f32[5,128,128]{2,1,0:T(8,128)S(1)} %get-tuple-element.32), channel_id=1, source_target_pairs={{0,8},{1,9},{2,10},{3,11},{4,12},{5,13},{6,14},{7,15},{8,0},{9,1},... | collective-permute-start | bytes 983048 | tf_op jit(solution)/shard_map/ppermute | solution.py:131
  4.9 8.5 %collective-permute-start = (f32[5,128,128]{2,1,0:T(8,128)S(1)}, f32[5,128,128]{2,1,0:T(8,128)S(1)}, u32[]{:S(2)}, u32[]{:S(2)}) collective-permute-start(f32[5,128,128]{2,1,0:T(8,128)S(1)} %get-tuple-element.32), channel_id=1, source_target_pairs={{0,1},{1,0},{2,3},{3,2},{4,5},{5,4},{6,7},{7,6},{8,16},{9,17},{10,... | collective-permute-start | bytes 983048 | tf_op jit(solution)/shard_map/ppermute | solution.py:131
  4.9 8.5 %collective-permute-start.4 = (f32[4,128,128]{2,1,0:T(8,128)S(1)}, f32[4,128,128]{2,1,0:T(8,128)S(1)}, u32[]{:S(2)}, u32[]{:S(2)}) collective-permute-start(f32[4,128,128]{2,1,0:T(8,128)S(1)} %get-tuple-element.31.refs_0_), channel_id=1, source_target_pairs={{0,4},{1,3},{2,6},{3,1},{4,0},{5,7},{6,2},{7,5},{8,12},{9,11},{10,... | collective-permute-start | bytes 786440 | tf_op jit(solution)/shard_map/ppermute | solution.py:131
  6.4 7.2 %collective-permute-start.1 = (f32[4,128,128]{2,1,0:T(8,128)S(1)}, f32[4,128,128]{2,1,0:T(8,128)S(1)}, u32[]{:S(2)}, u32[]{:S(2)}) collective-permute-start(f32[4,128,128]{2,1,0:T(8,128)S(1)} %get-tuple-element.31.refs_0_), channel_id=1, source_target_pairs={{0,2},{1,5},{2,0},{3,7},{4,6},{5,1},{6,4},{7,3},{8,10},{9,13},{10,... | collective-permute-start | bytes 786440 | tf_op jit(solution)/shard_map/ppermute | solution.py:131
  13.7 20.1 %collective-permute-start.10 = (f32[22,128,128]{2,1,0:T(8,128)S(1)}, f32[22,128,128]{2,1,0:T(8,128)S(1)}, u32[]{:S(2)}, u32[]{:S(2)}) collective-permute-start(f32[22,128,128]{2,1,0:T(8,128)S(1)} %constant_dynamic-update-slice_fusion), channel_id=1, source_target_pairs={{0,1},{1,0},{2,3},{3,2},{4,5},{5,4},{6,7},{7,6},{8,9},{9,8},{10,11... | collective-permute-start | bytes 4325384 | tf_op jit(solution)/shard_map/ppermute | solution.py:131
  14.1 10.1 %collective-permute-start.6 = (f32[5,128,128]{2,1,0:T(8,128)S(1)}, f32[5,128,128]{2,1,0:T(8,128)S(1)}, u32[]{:S(2)}, u32[]{:S(2)}) collective-permute-start(f32[5,128,128]{2,1,0:T(8,128)S(1)} %collective-permute-done.3.refs_4_), channel_id=1, source_target_pairs={{0,1},{1,0},{2,3},{3,2},{4,5},{5,4},{6,7},{7,6},{8,16},{9,17},{10,... | collective-permute-start | bytes 983048 | tf_op jit(solution)/shard_map/ppermute | solution.py:131
  14.3 9.8 %collective-permute-start.2 = (f32[4,128,128]{2,1,0:T(8,128)S(1)}, f32[4,128,128]{2,1,0:T(8,128)S(1)}, u32[]{:S(2)}, u32[]{:S(2)}) collective-permute-start(f32[4,128,128]{2,1,0:T(8,128)S(1)} %collective-permute-done.1.refs_1_), channel_id=1, source_target_pairs={{0,8},{1,9},{2,10},{3,11},{4,12},{5,13},{6,14},{7,15},{8,0},{9,1},... | collective-permute-start | bytes 786440 | tf_op jit(solution)/shard_map/ppermute | solution.py:131
  17.6 15.6 %collective-permute-start.5 = (f32[12,128,128]{2,1,0:T(8,128)S(1)}, f32[12,128,128]{2,1,0:T(8,128)S(1)}, u32[]{:S(2)}, u32[]{:S(2)}) collective-permute-start(f32[12,128,128]{2,1,0:T(8,128)S(1)} %pad_maximum_fusion.2), channel_id=1, source_target_pairs={{0,4},{1,3},{2,6},{3,1},{4,0},{5,7},{6,2},{7,5},{8,12},{9,11},{10,... | collective-permute-start | bytes 2359304 | tf_op jit(solution)/shard_map/ppermute | solution.py:131
  19.2 9.2 %collective-permute-start.7 = (f32[4,128,128]{2,1,0:T(8,128)S(1)}, f32[4,128,128]{2,1,0:T(8,128)S(1)}, u32[]{:S(2)}, u32[]{:S(2)}) collective-permute-start(f32[4,128,128]{2,1,0:T(8,128)S(1)} %slice.62), channel_id=1, source_target_pairs={{0,2},{1,5},{2,0},{3,7},{4,6},{5,1},{6,4},{7,3},{8,10},{9,13},{10,... | collective-permute-start | bytes 786440 | tf_op jit(solution)/shard_map/ppermute | solution.py:131
  24.1 5.7 %collective-permute-start.8 = (f32[4,128,128]{2,1,0:T(8,128)S(1)}, f32[4,128,128]{2,1,0:T(8,128)S(1)}, u32[]{:S(2)}, u32[]{:S(2)}) collective-permute-start(f32[4,128,128]{2,1,0:T(8,128)S(1)} %collective-permute-done.2.refs_5_), channel_id=1, source_target_pairs={{0,1},{1,0},{2,3},{3,2},{4,5},{5,4},{6,7},{7,6},{8,16},{9,17},{10,... | collective-permute-start | bytes 786440 | tf_op jit(solution)/shard_map/ppermute | solution.py:131
  24.2 5.7 %collective-permute-start.9 = (f32[1,128,128]{2,1,0:T(8,128)S(1)}, f32[1,128,128]{2,1,0:T(8,128)S(1)}, u32[]{:S(2)}, u32[]{:S(2)}) collective-permute-start(f32[1,128,128]{2,1,0:T(8,128)S(1)} %fusion), channel_id=1, source_target_pairs={{0,2},{1,5},{2,0},{3,7},{4,6},{5,1},{6,4},{7,3},{8,10},{9,13},{10,... | collective-permute-start | bytes 196616 | tf_op jit(solution)/shard_map/ppermute | solution.py:131
  28.5 11.0 %collective-permute-start.12 = (f32[9,128,128]{2,1,0:T(8,128)S(1)}, f32[9,128,128]{2,1,0:T(8,128)S(1)}, u32[]{:S(2)}, u32[]{:S(2)}) collective-permute-start(f32[9,128,128]{2,1,0:T(8,128)S(1)} %pad_maximum_fusion.3), channel_id=1, source_target_pairs={{0,4},{1,3},{2,6},{3,1},{4,0},{5,7},{6,2},{7,5},{8,12},{9,11},{10,... | collective-permute-start | bytes 1769480 | tf_op jit(solution)/shard_map/ppermute | solution.py:131
  33.2 7.3 %collective-permute-start.13 = (f32[4,128,128]{2,1,0:T(8,128)S(1)}, f32[4,128,128]{2,1,0:T(8,128)S(1)}, u32[]{:S(2)}, u32[]{:S(2)}) collective-permute-start(f32[4,128,128]{2,1,0:T(8,128)S(1)} %get-tuple-element.49.refs_3_), channel_id=1, source_target_pairs={{0,8},{1,9},{2,10},{3,11},{4,12},{5,13},{6,14},{7,15},{8,0},{9,1},... | collective-permute-start | bytes 786440 | tf_op jit(solution)/shard_map/ppermute | solution.py:131
  33.7 11.4 %collective-permute-start.14 = (f32[25,128,128]{2,1,0:T(8,128)S(1)}, f32[25,128,128]{2,1,0:T(8,128)S(1)}, u32[]{:S(2)}, u32[]{:S(2)}) collective-permute-start(f32[25,128,128]{2,1,0:T(8,128)S(1)} %pad_maximum_fusion), channel_id=1, source_target_pairs={{0,1},{1,0},{2,3},{3,2},{4,5},{5,4},{6,7},{7,6},{8,9},{9,8},{10,11... | collective-permute-start | bytes 4915208 | tf_op jit(solution)/shard_map/ppermute | solution.py:131
  33.8 9.2 %collective-permute-start.11 = (f32[5,128,128]{2,1,0:T(8,128)S(1)}, f32[5,128,128]{2,1,0:T(8,128)S(1)}, u32[]{:S(2)}, u32[]{:S(2)}) collective-permute-start(f32[5,128,128]{2,1,0:T(8,128)S(1)} %pad_maximum_fusion.4), channel_id=1, source_target_pairs={{0,4},{1,3},{2,6},{3,1},{4,0},{5,7},{6,2},{7,5},{8,12},{9,11},{10,... | collective-permute-start | bytes 983048 | tf_op jit(solution)/shard_map/ppermute | solution.py:131
  40.6 2.7 %collective-permute-start.15 = (f32[16,128,128]{2,1,0:T(8,128)S(1)}, f32[16,128,128]{2,1,0:T(8,128)S(1)}, u32[]{:S(2)}, u32[]{:S(2)}) collective-permute-start(f32[16,128,128]{2,1,0:T(8,128)S(1)} %pad_maximum_fusion.1), channel_id=1, source_target_pairs={{0,1},{1,0},{2,3},{3,2},{4,5},{5,4},{6,7},{7,6},{8,9},{9,8},{10,11... | collective-permute-start | bytes 3145736 | tf_op jit(solution)/shard_map/ppermute | solution.py:131
  43.1 2.0 %collective-permute-start.16 = (f32[8,128,128]{2,1,0:T(8,128)S(1)}, f32[8,128,128]{2,1,0:T(8,128)S(1)}, u32[]{:S(2)}, u32[]{:S(2)}) collective-permute-start(f32[8,128,128]{2,1,0:T(8,128)S(1)} %get-tuple-element.55), channel_id=1, source_target_pairs={{0,1},{1,0},{2,3},{3,2},{4,5},{5,4},{6,7},{7,6},{8,9},{9,8},{10,11... | collective-permute-start | bytes 1572872 | tf_op jit(solution)/shard_map/ppermute | solution.py:131
  45.1 15.1 %copy-start.1 = (f32[512,256]{1,0:T(8,128)S(1)}, f32[512,256]{1,0:T(8,128)}, u32[]{:S(2)}) copy-start(f32[512,256]{1,0:T(8,128)} %matrix.3) | copy-start | bytes 1572868
  47.0 13.1 %collective-permute-start.17 = (f32[7,16,128]{2,1,0:T(8,128)S(1)}, f32[7,16,128]{2,1,0:T(8,128)S(1)}, u32[]{:S(2)}, u32[]{:S(2)}) collective-permute-start(f32[7,16,128]{2,1,0:T(8,128)S(1)} %get-tuple-element.57), channel_id=1, source_target_pairs={{0,8},{1,9},{2,10},{3,11},{4,12},{5,13},{6,14},{7,15},{8,0},{9,1},... | collective-permute-start | bytes 172040 | tf_op jit(solution)/shard_map/ppermute | solution.py:131
